TPU v7x, 32 devices: a whole 2x2x4 slice. The times are simulated.
32 devices in a mesh: wide: 8 (over y, x, core), grp: 4 (over z).
Axes of the slice: x: 2, y: 2, z: 4, core: 2. Of those that a mesh axis runs over, the one named last changes fastest.
Arguments:
- solution: float32 [64, 32768], P(None, ('wide', 'grp')), may hold values from -6 to 6
- incident: float32 [64, 32768], P(None, ('wide', 'grp')), may hold values from -12 to 12
- leaf_blocks: float32 [512, 32768], P(None, ('wide', 'grp')), may hold values from -0.25 to 0.25
- leaf_inverse: float32 [512, 32768], P(None, ('wide', 'grp')), may hold values from -0.25 to 0.25
- col_basis: float32 [6, 96, 32768], P(None, None, ('wide', 'grp')), may hold values from -0.625 to 0.625
- row_basis: float32 [6, 96, 32768], P(None, None, ('wide', 'grp')), may hold values from -6 to 6
Outputs:
- refined: float32 [64, 32768], P(None, ('wide', 'grp'))
- residual: float32 [64, 32768], P(None, ('wide', 'grp'))
All inputs are finite; a program needn't handle non-finite values.
Results may differ from a plain program's by a relative error of at most 0.0001.
Values sent between devices are 32-bit elements; how exact they have to be, the bound alone decides.
No kernel may reach another device: no remote copies, remote signals or barrier semaphores. Data moves between devices by JAX's collectives and lax.ppermute only.
A program may use at most 64 MiB of HBM per device.

v0:
```python
import jax
import jax.numpy as jnp
from jax import lax
from jax.sharding import PartitionSpec as P


def from_partner(block, axis, stride):
    count = lax.axis_size(axis)
    route = []
    for low in range(count):
        high = low | 1 << stride
        if high != low and high < count:
            route += [(low, high), (high, low)]
    return lax.ppermute(block, axis, route)


def leaf_apply(field, blocks):
    cols, rows = field.shape
    leaf = blocks.shape[0]
    count = rows // leaf
    pieces = field.reshape(cols, count, leaf)
    tables = blocks.reshape(leaf, count, leaf)
    image = jnp.einsum("pkj,jki->pki", pieces, tables, precision=lax.Precision.HIGHEST)
    return image.reshape(cols, rows)


def climb_tree(partials):
    grp_bits = lax.axis_size("grp").bit_length() - 1
    wide_bits = lax.axis_size("wide").bit_length() - 1
    gathered_coefs = []
    pending = partials
    for bit_pos in range(grp_bits):
        received = from_partner(pending, "grp", bit_pos)
        gathered_coefs.append(received[0])
        pending = (pending + received)[1:]
    for bit_pos in range(wide_bits):
        received = from_partner(pending, "wide", bit_pos)
        gathered_coefs.append(received[0])
        pending = (pending + received)[1:]
    return jnp.stack(gathered_coefs)


def operator(field, leaf_blocks, col_basis, row_basis):
    cols, rows = field.shape
    leaf = leaf_blocks.shape[0]
    image = leaf_apply(field, leaf_blocks)
    pieces = field.reshape(cols, 2, leaf)
    rights = row_basis[0].reshape(row_basis.shape[1], 2, leaf)
    lefts = col_basis[0].reshape(col_basis.shape[1], 2, leaf)
    leaf_coefs = jnp.einsum("pks,rks->kpr", pieces, rights, precision=lax.Precision.HIGHEST)[::-1]
    image = image + jnp.einsum(
        "kpr,rks->pks", leaf_coefs, lefts, precision=lax.Precision.HIGHEST
    ).reshape(cols, rows)
    partials = jnp.einsum("pn,lrn->lpr", field, row_basis[1:], precision=lax.Precision.HIGHEST)
    sibling_coefs = climb_tree(partials)
    image = image + jnp.einsum(
        "lpr,lrn->pn", sibling_coefs, col_basis[1:], precision=lax.Precision.HIGHEST
    )
    return image


def per_device(solution, incident, leaf_blocks, leaf_inverse, col_basis, row_basis):
    first_residual = incident - operator(solution, leaf_blocks, col_basis, row_basis)
    refined = solution + leaf_apply(first_residual, leaf_inverse)
    residual = incident - operator(refined, leaf_blocks, col_basis, row_basis)
    return (refined, residual)


def solution(mesh):
    in_specs = (
        P(None, ("wide", "grp")),
        P(None, ("wide", "grp")),
        P(None, ("wide", "grp")),
        P(None, ("wide", "grp")),
        P(None, None, ("wide", "grp")),
        P(None, None, ("wide", "grp")),
    )
    out_specs = (P(None, ("wide", "grp")), P(None, ("wide", "grp")))
    return jax.shard_map(
        per_device, mesh=mesh, in_specs=in_specs, out_specs=out_specs, check_vma=False
    )
```

profile of v0, /device:TPU:0, one launch (start us, length us, event | category | flops | bytes accessed | tf_op | source)
XLA Modules:
  0.0 62.3 jit_solution(6531442453639561755)
XLA Ops:
  0.7 4.3 %convolution_bitcast_fusion.1 = f32[5,64,96]{2,1,0:T(8,128)} fusion(f32[6,96,1024]{2,1,0:T(8,128)} %param.11, f32[64,1024]{1,0:T(8,128)} %param.6), kind=kOutput, calls=%fused_computation.28 | convolution fusion | flops 377487360 | bytes 2744320 | tf_op jit(solution)/shard_map/pn,lrn->lpr/dot_general | solution.py:54
  5.0 3.0 %collective-permute-start = (f32[5,64,96]{2,1,0:T(8,128)}, f32[5,64,96]{2,1,0:T(8,128)}, u32[]{:S(2)}, u32[]{:S(2)}) collective-permute-start(f32[5,64,96]{2,1,0:T(8,128)} %convolution_bitcast_fusion.1), channel_id=1, source_target_pairs={{0,1},{1,0},{2,3},{3,2},{4,5},{5,4},{6,7},{7,6},{8,9},{9,8},{10,11... | collective-permute-start | bytes 368648 | tf_op jit(solution)/shard_map/ppermute | solution.py:14
  8.4 0.3 reshape_squeeze.8
  8.7 0.6 fusion.56
  9.3 0.5 convolution_bitcast_fusion
  9.8 2.8 %collective-permute-done = f32[5,64,96]{2,1,0:T(8,128)} collective-permute-done((f32[5,64,96]{2,1,0:T(8,128)}, f32[5,64,96]{2,1,0:T(8,128)}, u32[]{:S(2)}, u32[]{:S(2)}) %collective-permute-start) | collective-permute-done | bytes 122912 | tf_op jit(solution)/shard_map/ppermute | solution.py:14
  12.5 1.0 %slice_add_fusion.1 = f32[4,64,96]{2,1,0:T(8,128)S(1)} fusion(f32[5,64,96]{2,1,0:T(8,128)} %collective-permute-done, f32[5,64,96]{2,1,0:T(8,128)} %convolution_bitcast_fusion.1), kind=kLoop, calls=%fused_computation.50 | loop fusion | flops 24576 | bytes 294912 | tf_op jit(solution)/shard_map/add | solution.py:35
  13.5 2.8 %collective-permute-start.1 = (f32[4,64,96]{2,1,0:T(8,128)S(1)}, f32[4,64,96]{2,1,0:T(8,128)S(1)}, u32[]{:S(2)}, u32[]{:S(2)}) collective-permute-start(f32[4,64,96]{2,1,0:T(8,128)S(1)} %slice_add_fusion.1), channel_id=1, source_target_pairs={{0,2},{2,0},{1,3},{3,1},{4,6},{6,4},{5,7},{7,5},{8,10},{10,8},{9,1... | collective-permute-start | bytes 294920 | tf_op jit(solution)/shard_map/ppermute | solution.py:14
  16.4 0.8 %slice_dynamic-update-slice_fusion.7 = f32[5,64,96]{2,1,0:T(8,128)S(1)} fusion(f32[5,64,96]{2,1,0:T(8,128)} %collective-permute-done), kind=kLoop, calls=%fused_computation.64 | loop fusion | bytes 57344
  17.1 4.9 %collective-permute-done.1 = f32[4,64,96]{2,1,0:T(8,128)S(1)} collective-permute-done((f32[4,64,96]{2,1,0:T(8,128)S(1)}, f32[4,64,96]{2,1,0:T(8,128)S(1)}, u32[]{:S(2)}, u32[]{:S(2)}) %collective-permute-start.1) | collective-permute-done | bytes 98336 | tf_op jit(solution)/shard_map/ppermute | solution.py:14
  22.1 1.3 %collective-permute-done.2 = f32[3,64,96]{2,1,0:T(8,128)S(1)} collective-permute-done((f32[3,64,96]{2,1,0:T(8,128)S(1)}, f32[3,64,96]{2,1,0:T(8,128)S(1)}, u32[]{:S(2)}, u32[]{:S(2)}) %collective-permute-start.2) | collective-permute-done | bytes 73760 | tf_op jit(solution)/shard_map/ppermute | solution.py:14
  23.4 1.4 %collective-permute-start.3 = (f32[2,64,96]{2,1,0:T(8,128)S(1)}, f32[2,64,96]{2,1,0:T(8,128)S(1)}, u32[]{:S(2)}, u32[]{:S(2)}) collective-permute-start(f32[2,64,96]{2,1,0:T(8,128)S(1)} %slice_add_fusion.5), channel_id=1, source_target_pairs={{0,8},{8,0},{4,12},{12,4},{16,24},{24,16},{20,28},{28,20},{1,9},{9... | collective-permute-start | bytes 147464 | tf_op jit(solution)/shard_map/ppermute | solution.py:14
  24.8 2.9 %collective-permute-done.3 = f32[2,64,96]{2,1,0:T(8,128)S(1)} collective-permute-done((f32[2,64,96]{2,1,0:T(8,128)S(1)}, f32[2,64,96]{2,1,0:T(8,128)S(1)}, u32[]{:S(2)}, u32[]{:S(2)}) %collective-permute-start.3) | collective-permute-done | bytes 49184 | tf_op jit(solution)/shard_map/ppermute | solution.py:14
  27.7 1.4 %collective-permute-start.4 = (f32[1,64,96]{2,1,0:T(8,128)S(1)}, f32[1,64,96]{2,1,0:T(8,128)S(1)}, u32[]{:S(2)}, u32[]{:S(2)}) collective-permute-start(f32[1,64,96]{2,1,0:T(8,128)S(1)} %get-tuple-element.4), channel_id=1, source_target_pairs={{0,16},{16,0},{4,20},{20,4},{8,24},{24,8},{12,28},{28,12},{1,17},{... | collective-permute-start | bytes 73736 | tf_op jit(solution)/shard_map/ppermute | solution.py:14
  29.2 1.5 %fusion.21 = f32[2,8,8,512]{3,2,1,0:T(8,128)S(1)} fusion(f32[64,2,512]{2,0,1:T(8,128)S(1)} %convolution_bitcast_fusion, f32[64,2,8,512]{3,2,1,0:T(8,128)S(1)} %bitcast.84, f32[8,2,8,512]{3,2,1,0:T(8,128)S(1)} %bitcast.89), kind=kOutput, calls=%fused_computation.17 | convolution fusion | flops 402718720 | bytes 2883584 | tf_op jit(solution)/shard_map/pkj,jki->pki/dot_general | solution.py:23
  30.7 1.0 %collective-permute-done.4 = f32[1,64,96]{2,1,0:T(8,128)S(1)} collective-permute-done((f32[1,64,96]{2,1,0:T(8,128)S(1)}, f32[1,64,96]{2,1,0:T(8,128)S(1)}, u32[]{:S(2)}, u32[]{:S(2)}) %collective-permute-start.4) | collective-permute-done | bytes 24608 | tf_op jit(solution)/shard_map/ppermute | solution.py:14
  31.7 1.5 %fusion.48 = f32[64,1024]{1,0:T(8,128)S(1)} fusion(f32[64,1024]{1,0:T(8,128)S(1)} %copy-done.7, f32[64,1024]{1,0:T(8,128)S(1)} %bitcast.92, f32[5,64,96]{2,1,0:T(8,128)S(1)} %constant_dynamic-update-slice_fusion, f32[6,96,1024]{2,1,0:T(8,128)S(1)} %copy-done.2), kind=kOutput, calls=%fused_computation.27 | convolution fusion | flops 377618432 | bytes 2916352 | tf_op jit(solution)/shard_map/lpr,lrn->pn/dot_general | solution.py:56
  33.3 1.4 %fusion.30 = f32[2,8,8,512]{3,2,1,0:T(8,128)S(1)} fusion(f32[64,2,8,512]{3,2,1,0:T(8,128)S(1)} %bitcast.90, f32[8,2,8,512]{3,2,1,0:T(8,128)S(1)} %bitcast.91), kind=kOutput, calls=%fused_computation.20 | convolution fusion | flops 402653184 | bytes 2621440 | tf_op jit(solution)/shard_map/pkj,jki->pki/dot_general | solution.py:23
  34.9 2.1 %fusion.51 = f32[5,64,96]{2,1,0:T(8,128)S(1)} fusion(f32[6,96,1024]{2,1,0:T(8,128)S(1)} %copy-done, f32[64,1024]{1,0:T(8,128)S(1)} %add.55), kind=kOutput, calls=%fused_computation.29 | convolution fusion | flops 377487360 | bytes 2351104 | tf_op jit(solution)/shard_map/pn,lrn->lpr/dot_general | solution.py:54
  37.0 0.6 fusion.54
  37.6 0.6 collective-permute-start.5
  38.2 0.5 fusion.58
  38.7 4.3 %collective-permute-done.5 = f32[5,64,96]{2,1,0:T(8,128)S(1)} collective-permute-done((f32[5,64,96]{2,1,0:T(8,128)S(1)}, f32[5,64,96]{2,1,0:T(8,128)S(1)}, u32[]{:S(2)}, u32[]{:S(2)}) %collective-permute-start.5) | collective-permute-done | bytes 122912 | tf_op jit(solution)/shard_map/ppermute | solution.py:14
  43.0 2.2 %collective-permute-start.6 = (f32[4,64,96]{2,1,0:T(8,128)S(1)}, f32[4,64,96]{2,1,0:T(8,128)S(1)}, u32[]{:S(2)}, u32[]{:S(2)}) collective-permute-start(f32[4,64,96]{2,1,0:T(8,128)S(1)} %slice_add_fusion), channel_id=1, source_target_pairs={{0,2},{2,0},{1,3},{3,1},{4,6},{6,4},{5,7},{7,5},{8,10},{10,8},{9,1... | collective-permute-start | bytes 294920 | tf_op jit(solution)/shard_map/ppermute | solution.py:14
  45.2 5.1 %collective-permute-done.6 = f32[4,64,96]{2,1,0:T(8,128)S(1)} collective-permute-done((f32[4,64,96]{2,1,0:T(8,128)S(1)}, f32[4,64,96]{2,1,0:T(8,128)S(1)}, u32[]{:S(2)}, u32[]{:S(2)}) %collective-permute-start.6) | collective-permute-done | bytes 98336 | tf_op jit(solution)/shard_map/ppermute | solution.py:14
  50.4 1.3 %collective-permute-done.7 = f32[3,64,96]{2,1,0:T(8,128)S(1)} collective-permute-done((f32[3,64,96]{2,1,0:T(8,128)S(1)}, f32[3,64,96]{2,1,0:T(8,128)S(1)}, u32[]{:S(2)}, u32[]{:S(2)}) %collective-permute-start.7) | collective-permute-done | bytes 73760 | tf_op jit(solution)/shard_map/ppermute | solution.py:14
  51.7 1.4 %collective-permute-start.8 = (f32[2,64,96]{2,1,0:T(8,128)S(1)}, f32[2,64,96]{2,1,0:T(8,128)S(1)}, u32[]{:S(2)}, u32[]{:S(2)}) collective-permute-start(f32[2,64,96]{2,1,0:T(8,128)S(1)} %slice_add_fusion.4), channel_id=1, source_target_pairs={{0,8},{8,0},{4,12},{12,4},{16,24},{24,16},{20,28},{28,20},{1,9},{9... | collective-permute-start | bytes 147464 | tf_op jit(solution)/shard_map/ppermute | solution.py:14
  53.1 2.9 %collective-permute-done.8 = f32[2,64,96]{2,1,0:T(8,128)S(1)} collective-permute-done((f32[2,64,96]{2,1,0:T(8,128)S(1)}, f32[2,64,96]{2,1,0:T(8,128)S(1)}, u32[]{:S(2)}, u32[]{:S(2)}) %collective-permute-start.8) | collective-permute-done | bytes 49184 | tf_op jit(solution)/shard_map/ppermute | solution.py:14
  56.1 1.4 %collective-permute-start.9 = (f32[1,64,96]{2,1,0:T(8,128)S(1)}, f32[1,64,96]{2,1,0:T(8,128)S(1)}, u32[]{:S(2)}, u32[]{:S(2)}) collective-permute-start(f32[1,64,96]{2,1,0:T(8,128)S(1)} %get-tuple-element.2), channel_id=1, source_target_pairs={{0,16},{16,0},{4,20},{20,4},{8,24},{24,8},{12,28},{28,12},{1,17},{... | collective-permute-start | bytes 73736 | tf_op jit(solution)/shard_map/ppermute | solution.py:14
  57.5 1.4 %fusion.27 = f32[2,8,8,512]{3,2,1,0:T(8,128)S(1)} fusion(f32[2,64,512]{2,1,0:T(8,128)S(1)} %fusion.58, f32[64,2,8,512]{3,2,1,0:T(8,128)S(1)} %bitcast.85, f32[8,2,8,512]{3,2,1,0:T(8,128)S(1)} %bitcast.87), kind=kOutput, calls=%fused_computation.19 | convolution fusion | flops 402718720 | bytes 2883584 | tf_op jit(solution)/shard_map/pkj,jki->pki/dot_general | solution.py:23
  58.9 1.1 %collective-permute-done.9 = f32[1,64,96]{2,1,0:T(8,128)S(1)} collective-permute-done((f32[1,64,96]{2,1,0:T(8,128)S(1)}, f32[1,64,96]{2,1,0:T(8,128)S(1)}, u32[]{:S(2)}, u32[]{:S(2)}) %collective-permute-start.9) | collective-permute-done | bytes 24608 | tf_op jit(solution)/shard_map/ppermute | solution.py:14
  60.1 2.2 %fusion.42 = f32[64,1024]{1,0:T(8,128)} fusion(f32[64,1024]{1,0:T(8,128)S(1)} %copy-done.8, f32[64,1024]{1,0:T(8,128)S(1)} %bitcast.93, f32[5,64,96]{2,1,0:T(8,128)S(1)} %constant_dynamic-update-slice_fusion.1, f32[6,96,1024]{2,1,0:T(8,128)S(1)} %copy-done.3), kind=kOutput, calls=%fused_computation.25 | convolution fusion | flops 377618432 | bytes 2916352 | tf_op jit(solution)/shard_map/lpr,lrn->pn/dot_general | solution.py:56
  (45 shorter events, 0.9 us)
Async XLA Ops:
  0.6 7.7 %slice-start = ((f32[6,96,1024]{2,1,0:T(8,128)}), f32[1,96,1024]{2,1,0:T(8,128)S(1)}, s32[]{:S(2)}) async-start(f32[6,96,1024]{2,1,0:T(8,128)} %param.11), calls=%async_computation | async-start | bytes 786432 | tf_op jit(solution)/shard_map/slice | solution.py:48
  0.6 7.4 %slice-start.1 = ((f32[6,96,1024]{2,1,0:T(8,128)}), f32[1,96,1024]{2,1,0:T(8,128)S(1)}, s32[]{:S(2)}) async-start(f32[6,96,1024]{2,1,0:T(8,128)} %param.10), calls=%async_computation.1 | async-start | bytes 786432 | tf_op jit(solution)/shard_map/slice | solution.py:49
  5.0 3.7 %copy-start.5 = (f32[64,1024]{1,0:T(8,128)S(1)}, f32[64,1024]{1,0:T(8,128)}, u32[]{:S(2)}) copy-start(f32[64,1024]{1,0:T(8,128)} %param.6) | copy-start | bytes 786436
  5.0 7.5 %collective-permute-start = (f32[5,64,96]{2,1,0:T(8,128)}, f32[5,64,96]{2,1,0:T(8,128)}, u32[]{:S(2)}, u32[]{:S(2)}) collective-permute-start(f32[5,64,96]{2,1,0:T(8,128)} %convolution_bitcast_fusion.1), channel_id=1, source_target_pairs={{0,1},{1,0},{2,3},{3,2},{4,5},{5,4},{6,7},{7,6},{8,9},{9,8},{10,11... | collective-permute-start | bytes 368648 | tf_op jit(solution)/shard_map/ppermute | solution.py:14
  8.0 21.1 %copy-start.1 = (f32[512,1024]{1,0:T(8,128)S(1)}, f32[512,1024]{1,0:T(8,128)}, u32[]{:S(2)}) copy-start(f32[512,1024]{1,0:T(8,128)} %param.8) | copy-start | bytes 6291460
  13.5 8.5 %collective-permute-start.1 = (f32[4,64,96]{2,1,0:T(8,128)S(1)}, f32[4,64,96]{2,1,0:T(8,128)S(1)}, u32[]{:S(2)}, u32[]{:S(2)}) collective-permute-start(f32[4,64,96]{2,1,0:T(8,128)S(1)} %slice_add_fusion.1), channel_id=1, source_target_pairs={{0,2},{2,0},{1,3},{3,1},{4,6},{6,4},{5,7},{7,5},{8,10},{10,8},{9,1... | collective-permute-start | bytes 294920 | tf_op jit(solution)/shard_map/ppermute | solution.py:14
  17.1 14.6 %copy-start.2 = (f32[6,96,1024]{2,1,0:T(8,128)S(1)}, f32[6,96,1024]{2,1,0:T(8,128)}, u32[]{:S(2)}) copy-start(f32[6,96,1024]{2,1,0:T(8,128)} %param.10) | copy-start | bytes 7077892
  17.1 14.6 %copy-start.7 = (f32[64,1024]{1,0:T(8,128)S(1)}, f32[64,1024]{1,0:T(8,128)}, u32[]{:S(2)}) copy-start(f32[64,1024]{1,0:T(8,128)} %param.7) | copy-start | bytes 786436
  22.0 1.4 %collective-permute-start.2 = (f32[3,64,96]{2,1,0:T(8,128)S(1)}, f32[3,64,96]{2,1,0:T(8,128)S(1)}, u32[]{:S(2)}, u32[]{:S(2)}) collective-permute-start(f32[3,64,96]{2,1,0:T(8,128)S(1)} %slice_add_fusion.3), channel_id=1, source_target_pairs={{0,4},{4,0},{8,12},{12,8},{16,20},{20,16},{24,28},{28,24},{1,5},{5... | collective-permute-start | bytes 221192 | tf_op jit(solution)/shard_map/ppermute | solution.py:14
  23.4 4.3 %collective-permute-start.3 = (f32[2,64,96]{2,1,0:T(8,128)S(1)}, f32[2,64,96]{2,1,0:T(8,128)S(1)}, u32[]{:S(2)}, u32[]{:S(2)}) collective-permute-start(f32[2,64,96]{2,1,0:T(8,128)S(1)} %slice_add_fusion.5), channel_id=1, source_target_pairs={{0,8},{8,0},{4,12},{12,4},{16,24},{24,16},{20,28},{28,20},{1,9},{9... | collective-permute-start | bytes 147464 | tf_op jit(solution)/shard_map/ppermute | solution.py:14
  27.7 4.0 %collective-permute-start.4 = (f32[1,64,96]{2,1,0:T(8,128)S(1)}, f32[1,64,96]{2,1,0:T(8,128)S(1)}, u32[]{:S(2)}, u32[]{:S(2)}) collective-permute-start(f32[1,64,96]{2,1,0:T(8,128)S(1)} %get-tuple-element.4), channel_id=1, source_target_pairs={{0,16},{16,0},{4,20},{20,4},{8,24},{24,8},{12,28},{28,12},{1,17},{... | collective-permute-start | bytes 73736 | tf_op jit(solution)/shard_map/ppermute | solution.py:14
  30.6 2.6 %copy-start.6 = (f32[512,1024]{1,0:T(8,128)S(1)}, f32[512,1024]{1,0:T(8,128)}, u32[]{:S(2)}) copy-start(f32[512,1024]{1,0:T(8,128)} %param.9) | copy-start | bytes 6291460
  33.2 1.7 %copy-start = (f32[6,96,1024]{2,1,0:T(8,128)S(1)}, f32[6,96,1024]{2,1,0:T(8,128)}, u32[]{:S(2)}) copy-start(f32[6,96,1024]{2,1,0:T(8,128)} %param.11) | copy-start | bytes 7077892
  34.9 22.6 %copy-start.4 = (f32[64,1024]{1,0:T(8,128)}, f32[64,1024]{1,0:T(8,128)S(1)}, u32[]{:S(2)}) copy-start(f32[64,1024]{1,0:T(8,128)S(1)} %add.55) | copy-start | bytes 786436
  37.6 5.4 %collective-permute-start.5 = (f32[5,64,96]{2,1,0:T(8,128)S(1)}, f32[5,64,96]{2,1,0:T(8,128)S(1)}, u32[]{:S(2)}, u32[]{:S(2)}) collective-permute-start(f32[5,64,96]{2,1,0:T(8,128)S(1)} %fusion.51), channel_id=1, source_target_pairs={{0,1},{1,0},{2,3},{3,2},{4,5},{5,4},{6,7},{7,6},{8,9},{9,8},{10,11... | collective-permute-start | bytes 368648 | tf_op jit(solution)/shard_map/ppermute | solution.py:14
  43.0 7.3 %collective-permute-start.6 = (f32[4,64,96]{2,1,0:T(8,128)S(1)}, f32[4,64,96]{2,1,0:T(8,128)S(1)}, u32[]{:S(2)}, u32[]{:S(2)}) collective-permute-start(f32[4,64,96]{2,1,0:T(8,128)S(1)} %slice_add_fusion), channel_id=1, source_target_pairs={{0,2},{2,0},{1,3},{3,1},{4,6},{6,4},{5,7},{7,5},{8,10},{10,8},{9,1... | collective-permute-start | bytes 294920 | tf_op jit(solution)/shard_map/ppermute | solution.py:14
  45.2 14.8 %copy-start.3 = (f32[6,96,1024]{2,1,0:T(8,128)S(1)}, f32[6,96,1024]{2,1,0:T(8,128)}, u32[]{:S(2)}) copy-start(f32[6,96,1024]{2,1,0:T(8,128)} %param.10) | copy-start | bytes 7077892
  45.2 14.8 %copy-start.8 = (f32[64,1024]{1,0:T(8,128)S(1)}, f32[64,1024]{1,0:T(8,128)}, u32[]{:S(2)}) copy-start(f32[64,1024]{1,0:T(8,128)} %param.7) | copy-start | bytes 786436
  50.4 1.4 %collective-permute-start.7 = (f32[3,64,96]{2,1,0:T(8,128)S(1)}, f32[3,64,96]{2,1,0:T(8,128)S(1)}, u32[]{:S(2)}, u32[]{:S(2)}) collective-permute-start(f32[3,64,96]{2,1,0:T(8,128)S(1)} %slice_add_fusion.2), channel_id=1, source_target_pairs={{0,4},{4,0},{8,12},{12,8},{16,20},{20,16},{24,28},{28,24},{1,5},{5... | collective-permute-start | bytes 221192 | tf_op jit(solution)/shard_map/ppermute | solution.py:14
  51.7 4.3 %collective-permute-start.8 = (f32[2,64,96]{2,1,0:T(8,128)S(1)}, f32[2,64,96]{2,1,0:T(8,128)S(1)}, u32[]{:S(2)}, u32[]{:S(2)}) collective-permute-start(f32[2,64,96]{2,1,0:T(8,128)S(1)} %slice_add_fusion.4), channel_id=1, source_target_pairs={{0,8},{8,0},{4,12},{12,4},{16,24},{24,16},{20,28},{28,20},{1,9},{9... | collective-permute-start | bytes 147464 | tf_op jit(solution)/shard_map/ppermute | solution.py:14
  56.1 4.0 %collective-permute-start.9 = (f32[1,64,96]{2,1,0:T(8,128)S(1)}, f32[1,64,96]{2,1,0:T(8,128)S(1)}, u32[]{:S(2)}, u32[]{:S(2)}) collective-permute-start(f32[1,64,96]{2,1,0:T(8,128)S(1)} %get-tuple-element.2), channel_id=1, source_target_pairs={{0,16},{16,0},{4,20},{20,4},{8,24},{24,8},{12,28},{28,12},{1,17},{... | collective-permute-start | bytes 73736 | tf_op jit(solution)/shard_map/ppermute | solution.py:14
where the time goes:
time: 62.6 us; the launch traced here: 62.3 us
  waiting for transfers between devices  27.6 us (44%)
  matrix products  16.4 us (26%)
  starting transfers between devices  14.5 us (23%)
  local copies, waits for them, and re-layouts  1.77 us (3%)
  other arithmetic  1.09 us (2%)
  between operations  0.88 us (1%)
    ppermute x10, waiting for transfers between devices, from_partner(): return lax.ppermute(block, axis, route)  27.6 us
    ppermute x10, starting transfers between devices, from_partner(): return lax.ppermute(block, axis, route)  14.5 us
    dot_general x2, matrix products, operator(): jnp.einsum('pn,lrn->lpr', field, row_basis[1:], precision=lax.Precision.H...  6.42 us
    dot_general x3, matrix products, leaf_apply(): jnp.einsum('pkj,jki->pki', pieces, tables, precision=lax.Precision.HIGHEST)  4.2 us
    dot_general x2, matrix products, operator(): jnp.einsum('lpr,lrn->pn', sibling_coefs, col_basis[1:], precision=lax.Pre...  3.77 us
  transfers between devices with their start and end apart: 10, of which 10 were waited for; matrix products, arithmetic and copies ran while one was open for 9% of the time, Pallas kernels for 0%

commit v1 on v0

v1 whole, which is shorter than its diff:
```python
import jax
import jax.numpy as jnp
from jax import lax
from jax.sharding import PartitionSpec as P

AXES = ("wide", "grp")
DOT = lax.Precision.HIGH


def bits_of(axis):
    return lax.axis_size(axis).bit_length() - 1


def parity(number):
    return number.bit_count() & 1


def swap(block, masks):
    wides, grps = lax.axis_size("wide"), lax.axis_size("grp")
    route = []
    for w in range(wides):
        for g in range(grps):
            wide_mask, grp_mask = masks[parity(w) ^ parity(g)]
            route.append((w * grps + g, (w ^ wide_mask) * grps + (g ^ grp_mask)))
    return lax.ppermute(block, AXES, route)


def both(wide_mask, grp_mask):
    return ((wide_mask, grp_mask), (wide_mask, grp_mask))


def climb_tree(partials):
    gathered = []
    pending = partials
    masks = [both(0, 1 << b) for b in range(bits_of("grp"))]
    masks += [both(1 << b, 0) for b in range(bits_of("wide"))]
    for mask in masks:
        received = swap(pending, mask)
        gathered.append(received[0])
        pending = (pending + received)[1:]
    return jnp.stack(gathered)


def in_lanes(partials):
    low = partials[:3]
    wide, grp = lax.axis_index("wide"), lax.axis_index("grp")
    ones = wide ^ (wide >> 1) ^ (wide >> 2) ^ grp ^ (grp >> 1)
    first = (ones & 1) == 0
    fourth, fifth = partials[3], partials[4]
    mine = jnp.where(first, fourth, fifth) + swap(jnp.where(first, fifth, fourth), both(1, 0))
    low_got = swap(low, both(0, 1))
    low_next = (low + low_got)[1:]
    mine = mine + swap(mine, both(1, 1))
    mine = mine + swap(mine, both(1, 2))
    low_got_next = swap(low_next, both(0, 2))
    third = (low_next + low_got_next)[1]
    across = swap(mine, ((3, 0), (5, 0)))
    corner = swap(mine, both(6, 0))
    third = swap(third, both(1, 0))
    result = jnp.where(first, across, across + corner)
    other = swap(result, both(1, 0))
    return jnp.stack(
        [low_got[0], low_got_next[0], third, jnp.where(first, result, other), jnp.where(first, other, result)]
    )


def exchange(partials):
    if bits_of("grp") == 2 and bits_of("wide") == 3:
        return in_lanes(partials)
    return climb_tree(partials)


def leaf_apply(field, blocks):
    cols, rows = field.shape
    leaf = blocks.shape[0]
    count = rows // leaf
    pieces = field.reshape(cols, count, leaf)
    tables = blocks.reshape(leaf, count, leaf)
    image = jnp.einsum("pkj,jki->pki", pieces, tables, precision=DOT)
    return image.reshape(cols, rows)


def near_field(field, leaf_blocks, col_basis, row_basis):
    cols, rows = field.shape
    leaf = leaf_blocks.shape[0]
    image = leaf_apply(field, leaf_blocks)
    pieces = field.reshape(cols, 2, leaf)
    rights = row_basis[0].reshape(row_basis.shape[1], 2, leaf)
    lefts = col_basis[0].reshape(col_basis.shape[1], 2, leaf)
    leaf_coefs = jnp.einsum("pks,rks->kpr", pieces, rights, precision=DOT)[::-1]
    return image + jnp.einsum("kpr,rks->pks", leaf_coefs, lefts, precision=DOT).reshape(cols, rows)


def residual_of(field, incident, leaf_blocks, col_basis, row_basis):
    partials = jnp.einsum("pn,lrn->lpr", field, row_basis[1:], precision=DOT)
    coefs = exchange(partials)
    near = incident - near_field(field, leaf_blocks, col_basis, row_basis)
    return near - jnp.einsum("lpr,lrn->pn", coefs, col_basis[1:], precision=DOT)


def per_device(solution, incident, leaf_blocks, leaf_inverse, col_basis, row_basis):
    first_residual = residual_of(solution, incident, leaf_blocks, col_basis, row_basis)
    refined = solution + leaf_apply(first_residual, leaf_inverse)
    residual = residual_of(refined, incident, leaf_blocks, col_basis, row_basis)
    return (refined, residual)


def solution(mesh):
    in_specs = (
        P(None, ("wide", "grp")),
        P(None, ("wide", "grp")),
        P(None, ("wide", "grp")),
        P(None, ("wide", "grp")),
        P(None, None, ("wide", "grp")),
        P(None, None, ("wide", "grp")),
    )
    out_specs = (P(None, ("wide", "grp")), P(None, ("wide", "grp")))
    return jax.shard_map(
        per_device, mesh=mesh, in_specs=in_specs, out_specs=out_specs, check_vma=False
    )
```

time: 62.6 us -> 55.1 us (0.88)
  waiting for transfers between devices: 27.6 us -> 19.3 us
  matrix products: 16.4 us -> 9.84 us
  starting transfers between devices: 14.5 us -> 18.9 us
  local copies, waits for them, and re-layouts: 1.77 us -> 3.32 us
  other arithmetic: 1.09 us -> 2.43 us
    ppermute x10 -> x18, waiting for transfers between devices: 27.6 us -> 19.3 us  [swap(): return lax.ppermute(block, AXES, route)]
    dot_general x11, matrix products: 16.4 us -> 9.84 us  [the longest x2 3.73 us: residual_of(): partials = jnp.einsum('pn,lrn->lpr', field, row_basis[1:], precision=DOT)]
    ppermute x10 -> x18, starting transfers between devices: 14.5 us -> 18.9 us  [swap(): return lax.ppermute(block, AXES, route)]
    unnamed x24 -> x28, local copies, waits for them, and re-layouts: 1.02 us -> 1.92 us
    add x8, other arithmetic: 1.06 us -> 1.72 us  [the longest x2 0.89 us: in_lanes(): low_next = (low + low_got)[1:]]
    slice x4 -> x6, local copies, waits for them, and re-layouts: 0.01 us -> 0.67 us  [the longest x2 0.66 us: in_lanes(): low = partials[:3]]
    select_n x0 -> x4, other arithmetic: none -> 0.63 us  [the longest x2 0.62 us: in_lanes(): jnp.where(first, fifth, fourth)]
  transfers between devices with their start and end apart: 10 -> 18, of which waited for: 10 -> 11; matrix products, arithmetic and copies ran while one was open for 9% -> 12% of each run, Pallas kernels for 0% -> 0%
where the time goes in v1:
time: 55.1 us; the launch traced here: 54.8 us
  waiting for transfers between devices  19.3 us (35%)
  starting transfers between devices  18.9 us (34%)
  matrix products  9.84 us (18%)
  local copies, waits for them, and re-layouts  3.32 us (6%)
  other arithmetic  2.43 us (4%)
  between operations  0.96 us (2%)
    ppermute x18, waiting for transfers between devices, swap(): return lax.ppermute(block, AXES, route)  19.3 us
    ppermute x18, starting transfers between devices, swap(): return lax.ppermute(block, AXES, route)  18.9 us
    dot_general x2, matrix products, residual_of(): partials = jnp.einsum('pn,lrn->lpr', field, row_basis[1:], precision=DOT)  3.73 us
    dot_general x2, matrix products, residual_of(): return near - jnp.einsum('lpr,lrn->pn', coefs, col_basis[1:], precision=DOT)  2.45 us
    dot_general x3, matrix products, leaf_apply(): image = jnp.einsum('pkj,jki->pki', pieces, tables, precision=DOT)  2.31 us
    unnamed x28, local copies, waits for them, and re-layouts  1.92 us
  transfers between devices with their start and end apart: 18, of which 11 were waited for; matrix products, arithmetic and copies ran while one was open for 12% of the time, Pallas kernels for 0%

profile of v1, /device:TPU:0, one launch (start us, length us, event | category | flops | bytes accessed | tf_op | source)
XLA Modules:
  0.0 54.8 jit_solution(11985045414235252139)
XLA Ops:
  0.7 2.7 %convolution_bitcast_fusion.1 = f32[5,64,96]{2,1,0:T(8,128)S(1)} fusion(f32[6,96,1024]{2,1,0:T(8,128)} %param.11, f32[64,1024]{1,0:T(8,128)} %param.6), kind=kOutput, calls=%fused_computation.26 | convolution fusion | flops 188743680 | bytes 2744320 | tf_op jit(solution)/shard_map/pn,lrn->lpr/dot_general | solution.py:95
  3.4 0.6 %select_bitcast_fusion.1 = f32[64,96]{1,0:T(8,128)} fusion(f32[5,64,96]{2,1,0:T(8,128)S(1)} %convolution_bitcast_fusion.1, pred[]{:T(512)S(6)} %eq.4), kind=kLoop, calls=%fused_computation.68 | loop fusion | flops 6144 | bytes 73729 | tf_op jit(solution)/shard_map/jit(_where)/select_n | solution.py:50
  4.4 0.6 %slice.76 = f32[3,64,96]{2,1,0:T(8,128)} slice(f32[5,64,96]{2,1,0:T(8,128)S(1)} %convolution_bitcast_fusion.1), slice={[0:3], [0:64], [0:96]} | slice | bytes 147456 | tf_op jit(solution)/shard_map/slice | solution.py:45
  5.1 2.6 %collective-permute-start = (f32[3,64,96]{2,1,0:T(8,128)}, f32[3,64,96]{2,1,0:T(8,128)}, u32[]{:S(2)}, u32[]{:S(2)}) collective-permute-start(f32[3,64,96]{2,1,0:T(8,128)} %slice.76), channel_id=1, source_target_pairs={{0,1},{1,0},{2,3},{3,2},{4,5},{5,4},{6,7},{7,6},{8,9},{9,8},{10,11... | collective-permute-start | bytes 221192 | tf_op jit(solution)/shard_map/ppermute | solution.py:25
  9.1 0.8 %bitcast_add_fusion.1 = f32[64,96]{1,0:T(8,128)S(1)} fusion(f32[64,96]{1,0:T(8,128)} %collective-permute-done.3, f32[5,64,96]{2,1,0:T(8,128)} %copy-done.11, pred[]{:T(512)S(6)} %eq.4), kind=kLoop, calls=%fused_computation.65 | loop fusion | flops 12288 | bytes 98305 | tf_op jit(solution)/shard_map/add | solution.py:50
  10.4 2.9 %collective-permute-done.4 = f32[64,96]{1,0:T(8,128)S(1)} collective-permute-done((f32[64,96]{1,0:T(8,128)S(1)}, f32[64,96]{1,0:T(8,128)S(1)}, u32[]{:S(2)}, u32[]{:S(2)}) %collective-permute-start.4) | collective-permute-done | bytes 24608 | tf_op jit(solution)/shard_map/ppermute | solution.py:25
  13.2 2.4 %collective-permute-start.5 = (f32[64,96]{1,0:T(8,128)S(1)}, f32[64,96]{1,0:T(8,128)S(1)}, u32[]{:S(2)}, u32[]{:S(2)}) collective-permute-start(f32[64,96]{1,0:T(8,128)S(1)} %add.59), channel_id=1, source_target_pairs={{0,6},{1,7},{2,4},{3,5},{4,2},{5,3},{6,0},{7,1},{8,14},{9,15},{10,... | collective-permute-start | bytes 73736 | tf_op jit(solution)/shard_map/ppermute | solution.py:25
  15.7 0.7 %fusion.21 = f32[2,8,8,512]{3,2,1,0:T(8,128)S(1)} fusion(f32[64,2,512]{2,0,1:T(8,128)S(1)} %convolution_bitcast_fusion, f32[64,2,8,512]{3,2,1,0:T(8,128)S(1)} %bitcast.104, f32[8,2,8,512]{3,2,1,0:T(8,128)S(1)} %bitcast.109), kind=kOutput, calls=%fused_computation.17 | convolution fusion | flops 201392128 | bytes 2883584 | tf_op jit(solution)/shard_map/pkj,jki->pki/dot_general | solution.py:79
  16.5 1.6 %collective-permute-done.5 = f32[64,96]{1,0:T(8,128)S(1)} collective-permute-done((f32[64,96]{1,0:T(8,128)S(1)}, f32[64,96]{1,0:T(8,128)S(1)}, u32[]{:S(2)}, u32[]{:S(2)}) %collective-permute-start.5) | collective-permute-done | bytes 24608 | tf_op jit(solution)/shard_map/ppermute | solution.py:25
  18.1 2.7 %collective-permute-start.7 = (f32[64,96]{1,0:T(8,128)S(1)}, f32[64,96]{1,0:T(8,128)S(1)}, u32[]{:S(2)}, u32[]{:S(2)}) collective-permute-start(f32[64,96]{1,0:T(8,128)S(1)} %add.60), channel_id=1, source_target_pairs={{0,24},{1,25},{2,26},{3,27},{4,28},{5,29},{6,30},{7,31},{8,16},{9,... | collective-permute-start | bytes 73736 | tf_op jit(solution)/shard_map/ppermute | solution.py:25
  20.8 0.9 %slice_add_fusion.1 = f32[2,64,96]{2,1,0:T(8,128)S(1)} fusion(f32[3,64,96]{2,1,0:T(8,128)} %collective-permute-done, f32[3,64,96]{2,1,0:T(8,128)} %slice.76), kind=kLoop, calls=%fused_computation.48 | loop fusion | flops 12288 | bytes 147456 | tf_op jit(solution)/shard_map/add | solution.py:52
  21.7 1.8 %collective-permute-start.1 = (f32[2,64,96]{2,1,0:T(8,128)S(1)}, f32[2,64,96]{2,1,0:T(8,128)S(1)}, u32[]{:S(2)}, u32[]{:S(2)}) collective-permute-start(f32[2,64,96]{2,1,0:T(8,128)S(1)} %slice_add_fusion.1), channel_id=1, source_target_pairs={{0,2},{1,3},{2,0},{3,1},{4,6},{5,7},{6,4},{7,5},{8,10},{9,11},{10,... | collective-permute-start | bytes 147464 | tf_op jit(solution)/shard_map/ppermute | solution.py:25
  23.5 0.8 %slice_dynamic-update-slice_fusion.3 = f32[5,64,96]{2,1,0:T(8,128)S(1)} fusion(f32[3,64,96]{2,1,0:T(8,128)} %collective-permute-done), kind=kLoop, calls=%fused_computation.58 | loop fusion | bytes 57344
  24.3 3.5 %collective-permute-done.1 = f32[2,64,96]{2,1,0:T(8,128)S(1)} collective-permute-done((f32[2,64,96]{2,1,0:T(8,128)S(1)}, f32[2,64,96]{2,1,0:T(8,128)S(1)}, u32[]{:S(2)}, u32[]{:S(2)}) %collective-permute-start.1) | collective-permute-done | bytes 49184 | tf_op jit(solution)/shard_map/ppermute | solution.py:25
  27.9 0.5 collective-permute-start.8
  28.4 0.6 %collective-permute-done.2 = f32[64,96]{1,0:T(8,128)S(1)} collective-permute-done((f32[64,96]{1,0:T(8,128)S(1)}, f32[64,96]{1,0:T(8,128)S(1)}, u32[]{:S(2)}, u32[]{:S(2)}) %collective-permute-start.2) | collective-permute-done | bytes 24608 | tf_op jit(solution)/shard_map/ppermute | solution.py:25
  29.3 0.9 %fusion.42 = f32[64,1024]{1,0:T(8,128)S(1)} fusion(f32[5,64,96]{2,1,0:T(8,128)S(1)} %bitcast_dynamic-update-slice_fusion.3, f32[6,96,1024]{2,1,0:T(8,128)S(1)} %copy-done.2, f32[64,1024]{1,0:T(8,128)S(1)} %copy-done.9, f32[64,1024]{1,0:T(8,128)S(1)} %bitcast.113), kind=kOutput, calls=%fused_computation.25 | convolution fusion | flops 188874752 | bytes 2916352 | tf_op jit(solution)/shard_map/lpr,lrn->pn/dot_general | solution.py:98
  30.2 0.8 %fusion.30 = f32[2,8,8,512]{3,2,1,0:T(8,128)S(1)} fusion(f32[64,2,8,512]{3,2,1,0:T(8,128)S(1)} %bitcast.110, f32[8,2,8,512]{3,2,1,0:T(8,128)S(1)} %bitcast.111), kind=kOutput, calls=%fused_computation.20 | convolution fusion | flops 201326592 | bytes 2621440 | tf_op jit(solution)/shard_map/pkj,jki->pki/dot_general | solution.py:79
  31.2 0.7 %copy-done = f32[6,96,1024]{2,1,0:T(8,128)S(1)} copy-done((f32[6,96,1024]{2,1,0:T(8,128)S(1)}, f32[6,96,1024]{2,1,0:T(8,128)}, u32[]{:S(2)}) %copy-start) | copy-done | bytes 2359320
  31.9 1.1 %fusion.45 = f32[5,64,96]{2,1,0:T(8,128)S(1)} fusion(f32[6,96,1024]{2,1,0:T(8,128)S(1)} %copy-done, f32[64,1024]{1,0:T(8,128)S(1)} %add.62), kind=kOutput, calls=%fused_computation.27 | convolution fusion | flops 188743680 | bytes 2351104 | tf_op jit(solution)/shard_map/pn,lrn->lpr/dot_general | solution.py:95
  34.6 2.0 %collective-permute-start.9 = (f32[3,64,96]{2,1,0:T(8,128)S(1)}, f32[3,64,96]{2,1,0:T(8,128)S(1)}, u32[]{:S(2)}, u32[]{:S(2)}) collective-permute-start(f32[3,64,96]{2,1,0:T(8,128)S(1)} %slice.85), channel_id=1, source_target_pairs={{0,1},{1,0},{2,3},{3,2},{4,5},{5,4},{6,7},{7,6},{8,9},{9,8},{10,11... | collective-permute-start | bytes 221192 | tf_op jit(solution)/shard_map/ppermute | solution.py:25
  36.6 1.0 %collective-permute-done.13 = f32[64,96]{1,0:T(8,128)S(1)} collective-permute-done((f32[64,96]{1,0:T(8,128)S(1)}, f32[64,96]{1,0:T(8,128)S(1)}, u32[]{:S(2)}, u32[]{:S(2)}) %collective-permute-start.13) | collective-permute-done | bytes 24608 | tf_op jit(solution)/shard_map/ppermute | solution.py:25
  37.6 1.4 %collective-permute-start.14 = (f32[64,96]{1,0:T(8,128)S(1)}, f32[64,96]{1,0:T(8,128)S(1)}, u32[]{:S(2)}, u32[]{:S(2)}) collective-permute-start(f32[64,96]{1,0:T(8,128)S(1)} %add.69), channel_id=1, source_target_pairs={{0,6},{1,7},{2,4},{3,5},{4,2},{5,3},{6,0},{7,1},{8,14},{9,15},{10,... | collective-permute-start | bytes 73736 | tf_op jit(solution)/shard_map/ppermute | solution.py:25
  39.0 0.7 %fusion.27 = f32[2,8,8,512]{3,2,1,0:T(8,128)S(1)} fusion(f32[2,64,512]{2,1,0:T(8,128)S(1)} %fusion.52, f32[64,2,8,512]{3,2,1,0:T(8,128)S(1)} %bitcast.105, f32[8,2,8,512]{3,2,1,0:T(8,128)S(1)} %bitcast.107), kind=kOutput, calls=%fused_computation.19 | convolution fusion | flops 201392128 | bytes 2883584 | tf_op jit(solution)/shard_map/pkj,jki->pki/dot_general | solution.py:79
  39.8 2.3 %collective-permute-done.14 = f32[64,96]{1,0:T(8,128)S(1)} collective-permute-done((f32[64,96]{1,0:T(8,128)S(1)}, f32[64,96]{1,0:T(8,128)S(1)}, u32[]{:S(2)}, u32[]{:S(2)}) %collective-permute-start.14) | collective-permute-done | bytes 24608 | tf_op jit(solution)/shard_map/ppermute | solution.py:25
  42.1 1.4 %collective-permute-start.16 = (f32[64,96]{1,0:T(8,128)S(1)}, f32[64,96]{1,0:T(8,128)S(1)}, u32[]{:S(2)}, u32[]{:S(2)}) collective-permute-start(f32[64,96]{1,0:T(8,128)S(1)} %add.70), channel_id=1, source_target_pairs={{0,24},{1,25},{2,26},{3,27},{4,28},{5,29},{6,30},{7,31},{8,16},{9,... | collective-permute-start | bytes 73736 | tf_op jit(solution)/shard_map/ppermute | solution.py:25
  43.4 1.6 %collective-permute-start.15 = (f32[64,96]{1,0:T(8,128)S(1)}, f32[64,96]{1,0:T(8,128)S(1)}, u32[]{:S(2)}, u32[]{:S(2)}) collective-permute-start(f32[64,96]{1,0:T(8,128)S(1)} %add.70), channel_id=1, source_target_pairs={{0,12},{1,21},{2,22},{3,15},{4,16},{5,9},{6,10},{7,19},{8,28},{9,5... | collective-permute-start | bytes 73736 | tf_op jit(solution)/shard_map/ppermute | solution.py:25
  45.1 0.7 %collective-permute-start.10 = (f32[2,64,96]{2,1,0:T(8,128)S(1)}, f32[2,64,96]{2,1,0:T(8,128)S(1)}, u32[]{:S(2)}, u32[]{:S(2)}) collective-permute-start(f32[2,64,96]{2,1,0:T(8,128)S(1)} %slice_add_fusion), channel_id=1, source_target_pairs={{0,2},{1,3},{2,0},{3,1},{4,6},{5,7},{6,4},{7,5},{8,10},{9,11},{10,... | collective-permute-start | bytes 147464 | tf_op jit(solution)/shard_map/ppermute | solution.py:25
  45.7 5.9 %collective-permute-done.10 = f32[2,64,96]{2,1,0:T(8,128)S(1)} collective-permute-done((f32[2,64,96]{2,1,0:T(8,128)S(1)}, f32[2,64,96]{2,1,0:T(8,128)S(1)}, u32[]{:S(2)}, u32[]{:S(2)}) %collective-permute-start.10) | collective-permute-done | bytes 49184 | tf_op jit(solution)/shard_map/ppermute | solution.py:25
  51.8 0.5 collective-permute-start.17
  52.3 0.6 %collective-permute-done.11 = f32[64,96]{1,0:T(8,128)S(1)} collective-permute-done((f32[64,96]{1,0:T(8,128)S(1)}, f32[64,96]{1,0:T(8,128)S(1)}, u32[]{:S(2)}, u32[]{:S(2)}) %collective-permute-start.11) | collective-permute-done | bytes 24608 | tf_op jit(solution)/shard_map/ppermute | solution.py:25
  53.2 1.6 %fusion.39 = f32[64,1024]{1,0:T(8,128)} fusion(f32[5,64,96]{2,1,0:T(8,128)S(1)} %bitcast_dynamic-update-slice_fusion, f32[6,96,1024]{2,1,0:T(8,128)S(1)} %copy-done.3, f32[64,1024]{1,0:T(8,128)S(1)} %copy-done.10, f32[64,1024]{1,0:T(8,128)S(1)} %bitcast.112), kind=kOutput, calls=%fused_computation.24 | convolution fusion | flops 188874752 | bytes 2916352 | tf_op jit(solution)/shard_map/lpr,lrn->pn/dot_general | solution.py:98
  (75 shorter events, 4.9 us)
Async XLA Ops:
  0.6 7.0 %slice-start = ((f32[6,96,1024]{2,1,0:T(8,128)}), f32[1,96,1024]{2,1,0:T(8,128)S(1)}, s32[]{:S(2)}) async-start(f32[6,96,1024]{2,1,0:T(8,128)} %param.11), calls=%async_computation | async-start | bytes 786432 | tf_op jit(solution)/shard_map/slice | solution.py:88
  0.7 7.4 %copy-start.5 = (f32[64,1024]{1,0:T(8,128)S(1)}, f32[64,1024]{1,0:T(8,128)}, u32[]{:S(2)}) copy-start(f32[64,1024]{1,0:T(8,128)} %param.6) | copy-start | bytes 786436
  3.3 4.3 %copy-start.11 = (f32[5,64,96]{2,1,0:T(8,128)}, f32[5,64,96]{2,1,0:T(8,128)S(1)}, u32[]{:S(2)}) copy-start(f32[5,64,96]{2,1,0:T(8,128)S(1)} %convolution_bitcast_fusion.1) | copy-start | bytes 368644
  3.4 5.4 %slice-start.1 = ((f32[6,96,1024]{2,1,0:T(8,128)}), f32[1,96,1024]{2,1,0:T(8,128)S(1)}, s32[]{:S(2)}) async-start(f32[6,96,1024]{2,1,0:T(8,128)} %param.10), calls=%async_computation.1 | async-start | bytes 786432 | tf_op jit(solution)/shard_map/slice | solution.py:89
  4.0 5.1 %collective-permute-start.3 = (f32[64,96]{1,0:T(8,128)}, f32[64,96]{1,0:T(8,128)}, u32[]{:S(2)}, u32[]{:S(2)}) collective-permute-start(f32[64,96]{1,0:T(8,128)} %select_bitcast_fusion.1), channel_id=1, source_target_pairs={{0,4},{1,5},{2,6},{3,7},{4,0},{5,1},{6,2},{7,3},{8,12},{9,13},{10,... | collective-permute-start | bytes 73736 | tf_op jit(solution)/shard_map/ppermute | solution.py:25
  5.1 15.7 %collective-permute-start = (f32[3,64,96]{2,1,0:T(8,128)}, f32[3,64,96]{2,1,0:T(8,128)}, u32[]{:S(2)}, u32[]{:S(2)}) collective-permute-start(f32[3,64,96]{2,1,0:T(8,128)} %slice.76), channel_id=1, source_target_pairs={{0,1},{1,0},{2,3},{3,2},{4,5},{5,4},{6,7},{7,6},{8,9},{9,8},{10,11... | collective-permute-start | bytes 221192 | tf_op jit(solution)/shard_map/ppermute | solution.py:25
  7.7 8.0 %copy-start.1 = (f32[512,1024]{1,0:T(8,128)S(1)}, f32[512,1024]{1,0:T(8,128)}, u32[]{:S(2)}) copy-start(f32[512,1024]{1,0:T(8,128)} %param.8) | copy-start | bytes 6291460
  8.0 0.7 %copy-start.6 = (f32[96,2,512]{2,1,0:T(2,128)}, f32[96,2,512]{2,1,0:T(2,128)S(1)}, u32[]{:S(2)}) copy-start(f32[96,2,512]{2,1,0:T(2,128)S(1)} %reshape_squeeze.8) | copy-start | bytes 1179652
  9.9 3.3 %collective-permute-start.4 = (f32[64,96]{1,0:T(8,128)S(1)}, f32[64,96]{1,0:T(8,128)S(1)}, u32[]{:S(2)}, u32[]{:S(2)}) collective-permute-start(f32[64,96]{1,0:T(8,128)S(1)} %bitcast_add_fusion.1), channel_id=1, source_target_pairs={{0,5},{1,4},{2,7},{3,6},{4,1},{5,0},{6,3},{7,2},{8,13},{9,12},{10,... | collective-permute-start | bytes 73736 | tf_op jit(solution)/shard_map/ppermute | solution.py:25
  13.2 4.8 %collective-permute-start.5 = (f32[64,96]{1,0:T(8,128)S(1)}, f32[64,96]{1,0:T(8,128)S(1)}, u32[]{:S(2)}, u32[]{:S(2)}) collective-permute-start(f32[64,96]{1,0:T(8,128)S(1)} %add.59), channel_id=1, source_target_pairs={{0,6},{1,7},{2,4},{3,5},{4,2},{5,3},{6,0},{7,1},{8,14},{9,15},{10,... | collective-permute-start | bytes 73736 | tf_op jit(solution)/shard_map/ppermute | solution.py:25
  15.7 13.6 %copy-start.2 = (f32[6,96,1024]{2,1,0:T(8,128)S(1)}, f32[6,96,1024]{2,1,0:T(8,128)}, u32[]{:S(2)}) copy-start(f32[6,96,1024]{2,1,0:T(8,128)} %param.10) | copy-start | bytes 7077892
  15.7 13.6 %copy-start.9 = (f32[64,1024]{1,0:T(8,128)S(1)}, f32[64,1024]{1,0:T(8,128)}, u32[]{:S(2)}) copy-start(f32[64,1024]{1,0:T(8,128)} %param.7) | copy-start | bytes 786436
  16.4 13.8 %copy-start.8 = (f32[512,1024]{1,0:T(8,128)S(1)}, f32[512,1024]{1,0:T(8,128)}, u32[]{:S(2)}) copy-start(f32[512,1024]{1,0:T(8,128)} %param.9) | copy-start | bytes 6291460
  18.1 9.8 %collective-permute-start.7 = (f32[64,96]{1,0:T(8,128)S(1)}, f32[64,96]{1,0:T(8,128)S(1)}, u32[]{:S(2)}, u32[]{:S(2)}) collective-permute-start(f32[64,96]{1,0:T(8,128)S(1)} %add.60), channel_id=1, source_target_pairs={{0,24},{1,25},{2,26},{3,27},{4,28},{5,29},{6,30},{7,31},{8,16},{9,... | collective-permute-start | bytes 73736 | tf_op jit(solution)/shard_map/ppermute | solution.py:25
  20.8 7.1 %collective-permute-start.6 = (f32[64,96]{1,0:T(8,128)S(1)}, f32[64,96]{1,0:T(8,128)S(1)}, u32[]{:S(2)}, u32[]{:S(2)}) collective-permute-start(f32[64,96]{1,0:T(8,128)S(1)} %add.60), channel_id=1, source_target_pairs={{0,12},{1,21},{2,22},{3,15},{4,16},{5,9},{6,10},{7,19},{8,28},{9,5... | collective-permute-start | bytes 73736 | tf_op jit(solution)/shard_map/ppermute | solution.py:25
  21.7 6.1 %collective-permute-start.1 = (f32[2,64,96]{2,1,0:T(8,128)S(1)}, f32[2,64,96]{2,1,0:T(8,128)S(1)}, u32[]{:S(2)}, u32[]{:S(2)}) collective-permute-start(f32[2,64,96]{2,1,0:T(8,128)S(1)} %slice_add_fusion.1), channel_id=1, source_target_pairs={{0,2},{1,3},{2,0},{3,1},{4,6},{5,7},{6,4},{7,5},{8,10},{9,11},{10,... | collective-permute-start | bytes 147464 | tf_op jit(solution)/shard_map/ppermute | solution.py:25
  27.8 1.3 %collective-permute-start.2 = (f32[64,96]{1,0:T(8,128)S(1)}, f32[64,96]{1,0:T(8,128)S(1)}, u32[]{:S(2)}, u32[]{:S(2)}) collective-permute-start(f32[64,96]{1,0:T(8,128)S(1)} %get-tuple-element.4), channel_id=1, source_target_pairs={{0,4},{1,5},{2,6},{3,7},{4,0},{5,1},{6,2},{7,3},{8,12},{9,13},{10,... | collective-permute-start | bytes 73736 | tf_op jit(solution)/shard_map/ppermute | solution.py:25
  27.9 1.4 %collective-permute-start.8 = (f32[64,96]{1,0:T(8,128)S(1)}, f32[64,96]{1,0:T(8,128)S(1)}, u32[]{:S(2)}, u32[]{:S(2)}) collective-permute-start(f32[64,96]{1,0:T(8,128)S(1)} %add_select_fusion.1), channel_id=1, source_target_pairs={{0,4},{1,5},{2,6},{3,7},{4,0},{5,1},{6,2},{7,3},{8,12},{9,13},{10,... | collective-permute-start | bytes 73736 | tf_op jit(solution)/shard_map/ppermute | solution.py:25
  30.2 1.7 %copy-start = (f32[6,96,1024]{2,1,0:T(8,128)S(1)}, f32[6,96,1024]{2,1,0:T(8,128)}, u32[]{:S(2)}) copy-start(f32[6,96,1024]{2,1,0:T(8,128)} %param.11) | copy-start | bytes 7077892
  31.1 2.3 %copy-start.7 = (f32[96,2,512]{2,1,0:T(2,128)S(1)}, f32[96,2,512]{2,1,0:T(2,128)}, u32[]{:S(2)}) copy-start(f32[96,2,512]{2,1,0:T(2,128)} %copy-done.6) | copy-start | bytes 1179652
  31.9 7.1 %copy-start.4 = (f32[64,1024]{1,0:T(8,128)}, f32[64,1024]{1,0:T(8,128)S(1)}, u32[]{:S(2)}) copy-start(f32[64,1024]{1,0:T(8,128)S(1)} %add.62) | copy-start | bytes 786436
  33.0 1.3 %collective-permute-start.12 = (f32[64,96]{1,0:T(8,128)S(1)}, f32[64,96]{1,0:T(8,128)S(1)}, u32[]{:S(2)}, u32[]{:S(2)}) collective-permute-start(f32[64,96]{1,0:T(8,128)S(1)} %select_bitcast_fusion), channel_id=1, source_target_pairs={{0,4},{1,5},{2,6},{3,7},{4,0},{5,1},{6,2},{7,3},{8,12},{9,13},{10,... | collective-permute-start | bytes 73736 | tf_op jit(solution)/shard_map/ppermute | solution.py:25
  34.3 3.3 %collective-permute-start.13 = (f32[64,96]{1,0:T(8,128)S(1)}, f32[64,96]{1,0:T(8,128)S(1)}, u32[]{:S(2)}, u32[]{:S(2)}) collective-permute-start(f32[64,96]{1,0:T(8,128)S(1)} %bitcast_add_fusion), channel_id=1, source_target_pairs={{0,5},{1,4},{2,7},{3,6},{4,1},{5,0},{6,3},{7,2},{8,13},{9,12},{10,... | collective-permute-start | bytes 73736 | tf_op jit(solution)/shard_map/ppermute | solution.py:25
  34.6 10.4 %collective-permute-start.9 = (f32[3,64,96]{2,1,0:T(8,128)S(1)}, f32[3,64,96]{2,1,0:T(8,128)S(1)}, u32[]{:S(2)}, u32[]{:S(2)}) collective-permute-start(f32[3,64,96]{2,1,0:T(8,128)S(1)} %slice.85), channel_id=1, source_target_pairs={{0,1},{1,0},{2,3},{3,2},{4,5},{5,4},{6,7},{7,6},{8,9},{9,8},{10,11... | collective-permute-start | bytes 221192 | tf_op jit(solution)/shard_map/ppermute | solution.py:25
  37.6 15.6 %copy-start.3 = (f32[6,96,1024]{2,1,0:T(8,128)S(1)}, f32[6,96,1024]{2,1,0:T(8,128)}, u32[]{:S(2)}) copy-start(f32[6,96,1024]{2,1,0:T(8,128)} %param.10) | copy-start | bytes 7077892
  37.6 15.6 %copy-start.10 = (f32[64,1024]{1,0:T(8,128)S(1)}, f32[64,1024]{1,0:T(8,128)}, u32[]{:S(2)}) copy-start(f32[64,1024]{1,0:T(8,128)} %param.7) | copy-start | bytes 786436
  37.6 4.4 %collective-permute-start.14 = (f32[64,96]{1,0:T(8,128)S(1)}, f32[64,96]{1,0:T(8,128)S(1)}, u32[]{:S(2)}, u32[]{:S(2)}) collective-permute-start(f32[64,96]{1,0:T(8,128)S(1)} %add.69), channel_id=1, source_target_pairs={{0,6},{1,7},{2,4},{3,5},{4,2},{5,3},{6,0},{7,1},{8,14},{9,15},{10,... | collective-permute-start | bytes 73736 | tf_op jit(solution)/shard_map/ppermute | solution.py:25
  42.1 9.7 %collective-permute-start.16 = (f32[64,96]{1,0:T(8,128)S(1)}, f32[64,96]{1,0:T(8,128)S(1)}, u32[]{:S(2)}, u32[]{:S(2)}) collective-permute-start(f32[64,96]{1,0:T(8,128)S(1)} %add.70), channel_id=1, source_target_pairs={{0,24},{1,25},{2,26},{3,27},{4,28},{5,29},{6,30},{7,31},{8,16},{9,... | collective-permute-start | bytes 73736 | tf_op jit(solution)/shard_map/ppermute | solution.py:25
  43.4 8.3 %collective-permute-start.15 = (f32[64,96]{1,0:T(8,128)S(1)}, f32[64,96]{1,0:T(8,128)S(1)}, u32[]{:S(2)}, u32[]{:S(2)}) collective-permute-start(f32[64,96]{1,0:T(8,128)S(1)} %add.70), channel_id=1, source_target_pairs={{0,12},{1,21},{2,22},{3,15},{4,16},{5,9},{6,10},{7,19},{8,28},{9,5... | collective-permute-start | bytes 73736 | tf_op jit(solution)/shard_map/ppermute | solution.py:25
  45.1 6.6 %collective-permute-start.10 = (f32[2,64,96]{2,1,0:T(8,128)S(1)}, f32[2,64,96]{2,1,0:T(8,128)S(1)}, u32[]{:S(2)}, u32[]{:S(2)}) collective-permute-start(f32[2,64,96]{2,1,0:T(8,128)S(1)} %slice_add_fusion), channel_id=1, source_target_pairs={{0,2},{1,3},{2,0},{3,1},{4,6},{5,7},{6,4},{7,5},{8,10},{9,11},{10,... | collective-permute-start | bytes 147464 | tf_op jit(solution)/shard_map/ppermute | solution.py:25
  51.6 1.3 %collective-permute-start.11 = (f32[64,96]{1,0:T(8,128)S(1)}, f32[64,96]{1,0:T(8,128)S(1)}, u32[]{:S(2)}, u32[]{:S(2)}) collective-permute-start(f32[64,96]{1,0:T(8,128)S(1)} %get-tuple-element.2), channel_id=1, source_target_pairs={{0,4},{1,5},{2,6},{3,7},{4,0},{5,1},{6,2},{7,3},{8,12},{9,13},{10,... | collective-permute-start | bytes 73736 | tf_op jit(solution)/shard_map/ppermute | solution.py:25
  51.8 1.4 %collective-permute-start.17 = (f32[64,96]{1,0:T(8,128)S(1)}, f32[64,96]{1,0:T(8,128)S(1)}, u32[]{:S(2)}, u32[]{:S(2)}) collective-permute-start(f32[64,96]{1,0:T(8,128)S(1)} %add_select_fusion), channel_id=1, source_target_pairs={{0,4},{1,5},{2,6},{3,7},{4,0},{5,1},{6,2},{7,3},{8,12},{9,13},{10,... | collective-permute-start | bytes 73736 | tf_op jit(solution)/shard_map/ppermute | solution.py:25

commit v2 on v1

v2 whole, which is shorter than its diff:
```python
import functools

import jax
import jax.numpy as jnp
from jax import lax
from jax.experimental import pallas as pl
from jax.experimental.pallas import tpu as pltpu
from jax.sharding import PartitionSpec as P

AXES = ("wide", "grp")
LANES = 128
TOP = 2
VMEM = pltpu.VMEM
F32 = jnp.float32
ROWS_OF_BOTH = (((1,), (1,)), ((), ()))
PLAIN = (((1,), (0,)), ((), ()))


def bits_of(axis):
    return lax.axis_size(axis).bit_length() - 1


def parity(number):
    return number.bit_count() & 1


def swap(block, masks):
    wides, grps = lax.axis_size("wide"), lax.axis_size("grp")
    route = []
    for w in range(wides):
        for g in range(grps):
            wide_mask, grp_mask = masks[parity(w) ^ parity(g)]
            route.append((w * grps + g, (w ^ wide_mask) * grps + (g ^ grp_mask)))
    return lax.ppermute(block, AXES, route)


def both(wide_mask, grp_mask):
    return ((wide_mask, grp_mask), (wide_mask, grp_mask))


def climb_tree(low, top, near_of, apply):
    gathered = []
    pending = jnp.concatenate([low, top])
    masks = [both(0, 1 << b) for b in range(bits_of("grp"))]
    masks += [both(1 << b, 0) for b in range(bits_of("wide"))]
    for mask in masks:
        received = swap(pending, mask)
        gathered.append(received[0])
        pending = (pending + received)[1:]
    near, *others = near_of()
    near = apply(1, near, jnp.stack(gathered[:-TOP]))
    return near, 1 + len(gathered) - TOP, jnp.stack(gathered[-TOP:]), others


def in_lanes(low, top, near_of, apply):
    wide, grp = lax.axis_index("wide"), lax.axis_index("grp")
    ones = wide ^ (wide >> 1) ^ (wide >> 2) ^ grp ^ (grp >> 1)
    first = (ones & 1) == 0
    fourth, fifth = top[0], top[1]
    mine = jnp.where(first, fourth, fifth) + swap(jnp.where(first, fifth, fourth), both(1, 0))
    low_got = swap(low, both(0, 1))
    low_next = (low + low_got)[1:]
    mine = mine + swap(mine, both(1, 1))
    near, *others = near_of()
    mine = mine + swap(mine, both(1, 2))
    low_got_next = swap(low_next, both(0, 2))
    third = (low_next + low_got_next)[1]
    across = swap(mine, ((3, 0), (5, 0)))
    corner = swap(mine, both(6, 0))
    across, third = lax.optimization_barrier((across, third))
    near = apply(1, near, jnp.stack([low_got[0], low_got_next[0]]))
    result = jnp.where(first, across, across + corner)
    other, third = swap(jnp.stack([result, third]), both(1, 0))
    return near, 3, jnp.stack([third, jnp.where(first, result, other), jnp.where(first, other, result)]), others


def exchange(low, top, near_of, apply):
    if bits_of("grp") == 2 and bits_of("wide") == 3:
        return in_lanes(low, top, near_of, apply)
    return climb_tree(low, top, near_of, apply)


def split(x):
    high = x.astype(jnp.bfloat16)
    return high, (x - high.astype(F32)).astype(jnp.bfloat16)


def dot(x, table, dims):
    count = x.shape[0]
    x_high, x_low = split(x)
    t_high, t_low = split(table)
    main = lax.dot_general(jnp.concatenate([x_high, x_low]), t_high, dims, preferred_element_type=F32)
    rest = lax.dot_general(x_high, t_low, dims, preferred_element_type=F32)
    return main[:count] + (main[count:] + rest)


def merged(basis):
    return basis.reshape(-1, basis.shape[-1])


def chunks_of(rank):
    widths = [LANES] * (rank // LANES)
    return widths + [w for w in (1 << b for b in reversed(range(LANES.bit_length() - 1))) if rank % LANES & w]


def packed_rows(cols, rank):
    return cols * rank // LANES


def pack(block):
    cols, rank = block.shape
    out, at = [], 0
    for w in chunks_of(rank):
        rows = cols * w // LANES
        piece = block[:, at : at + w]
        out.append(jnp.concatenate([piece[r : r + rows] for r in range(0, cols, rows)], axis=1))
        at += w
    return jnp.concatenate(out)


def unpack(dense, cols):
    out, at = [], 0
    for w in chunks_of(dense.shape[0] * LANES // cols):
        rows = cols * w // LANES
        piece = dense[at : at + rows]
        out.append(jnp.concatenate([piece[:, l : l + w] for l in range(0, LANES, w)]))
        at += rows
    return jnp.concatenate(out, axis=1)


def side_by_side(coefs, cols):
    return jnp.concatenate([unpack(coefs[l], cols) for l in range(coefs.shape[0])], axis=1)


def store_levels(ref, wide_block):
    rank = wide_block.shape[1] // ref.shape[0]
    for l in range(ref.shape[0]):
        ref[l] = pack(wide_block[:, l * rank : (l + 1) * rank])


def leaf_slices(blocks):
    leaf, rows = blocks.shape
    return [slice(s, s + leaf) for s in range(0, rows, leaf)]


def near_kernel(field, incident, leaf_blocks, col_basis, row_basis, near):
    pieces = leaf_slices(leaf_blocks)
    coefs = [dot(field[:, s], row_basis[0, :, s], ROWS_OF_BOTH) for s in pieces]
    for k, s in enumerate(pieces):
        image = dot(field[:, s], leaf_blocks[:, s], PLAIN)
        near[:, s] = incident[:, s] - image - dot(coefs[k ^ 1], col_basis[0, :, s], PLAIN)


def near_and_copy_kernel(field, incident, leaf_blocks, col_basis, row_basis, near, copy):
    copy[...] = field[...]
    near_kernel(field, incident, leaf_blocks, col_basis, row_basis, near)


def first_top_kernel(field_hbm, row_hbm, top, field, row, sems):
    levels = row_hbm.shape[0]
    copies = [pltpu.make_async_copy(field_hbm, field, sems.at[levels])]
    copies += [pltpu.make_async_copy(row_hbm.at[l], row.at[l], sems.at[l]) for l in reversed(range(levels))]
    for c in copies:
        c.start()
    for c in copies[: TOP + 1]:
        c.wait()
    store_levels(top, dot(field[...], merged(row[levels - TOP :]), ROWS_OF_BOTH))
    for c in copies[TOP + 1 :]:
        c.wait()


def low_kernel(field, row_basis, low):
    store_levels(low, dot(field[...], merged(row_basis[1 : row_basis.shape[0] - TOP]), ROWS_OF_BOTH))


def apply_kernel(start, near, coefs, col_basis, out):
    table = merged(col_basis[start : start + coefs.shape[0]])
    out[...] = near[...] - dot(side_by_side(coefs, near.shape[0]), table, PLAIN)


def refine_kernel(start, near, coefs, field, col_basis, leaf_inverse, row_basis, refined, top):
    levels = col_basis.shape[0]
    table = merged(col_basis[start:])
    first = near[...] - dot(side_by_side(coefs, near.shape[0]), table, PLAIN)
    for s in leaf_slices(leaf_inverse):
        refined[:, s] = field[:, s] + dot(first[:, s], leaf_inverse[:, s], PLAIN)
    store_levels(top, dot(refined[...], merged(row_basis[levels - TOP :]), ROWS_OF_BOTH))


def last_kernel(start, near, coefs, col_basis, out_hbm, out, sems):
    coefs = side_by_side(coefs, near.shape[0])
    rows = near.shape[1]
    step = rows // sems.shape[0]
    copies = []
    for k in range(sems.shape[0]):
        s = slice(k * step, k * step + step)
        out[:, s] = near[:, s] - dot(coefs, merged(col_basis[start:, :, s]), PLAIN)
        copies.append(pltpu.make_async_copy(out.at[:, s], out_hbm.at[:, s], sems.at[k]))
        copies[-1].start()
    for c in copies:
        c.wait()


def run(kernel, outs, *args, cycles=None):
    whole = pl.BlockSpec(memory_space=VMEM)
    return pl.pallas_call(
        kernel,
        out_shape=[VMEM(shape, F32) if inside else jax.ShapeDtypeStruct(shape, F32) for shape, inside in outs],
        in_specs=[whole] * len(args),
        out_specs=[whole] * len(outs),
        compiler_params=pltpu.CompilerParams(vmem_limit_bytes=24 << 20),
    )(*[pltpu.with_memory_space_constraint(a, VMEM) for a in args])


def per_device(solution, incident, leaf_blocks, leaf_inverse, col_basis, row_basis):
    levels, rank, rows = row_basis.shape
    cols = solution.shape[0]
    dense = (packed_rows(cols, rank), LANES)
    in_field = ((cols, rows), True)
    low_out = ((levels - 1 - TOP, *dense), True)
    top_out = ((TOP, *dense), True)
    in_vmem = pl.BlockSpec(memory_space=VMEM)
    in_hbm = pl.BlockSpec(memory_space=pltpu.HBM)
    params = pltpu.CompilerParams(vmem_limit_bytes=24 << 20)
    top, field, row_basis = pl.pallas_call(
        first_top_kernel,
        out_shape=[VMEM(top_out[0], F32), VMEM(solution.shape, F32), VMEM(row_basis.shape, F32)],
        in_specs=[in_hbm] * 2,
        out_specs=[in_vmem] * 3,
        scratch_shapes=[pltpu.SemaphoreType.DMA((levels + 1,))],
        compiler_params=params,
    )(*[pltpu.with_memory_space_constraint(a, pltpu.HBM) for a in (solution, row_basis)])
    (low,) = run(low_kernel, [low_out], field, row_basis)

    def near_of(field):
        return run(near_kernel, [in_field], field, incident, leaf_blocks, col_basis, row_basis)

    def near_and_copy(field):
        outs = [in_field, ((cols, rows), False)]
        return run(near_and_copy_kernel, outs, field, incident, leaf_blocks, col_basis, row_basis)

    def apply(start, near, coefs):
        return run(functools.partial(apply_kernel, start), [in_field], near, coefs, col_basis)[0]

    near, start, coefs, _ = exchange(low, top, functools.partial(near_of, field), apply)
    refined, top = run(
        functools.partial(refine_kernel, start),
        [in_field, top_out],
        near,
        coefs,
        field,
        col_basis,
        leaf_inverse,
        row_basis,
    )
    (low,) = run(low_kernel, [low_out], refined, row_basis)
    near, start, coefs, others = exchange(low, top, functools.partial(near_and_copy, refined), apply)
    residual = pl.pallas_call(
        functools.partial(last_kernel, start),
        out_shape=jax.ShapeDtypeStruct((cols, rows), F32),
        in_specs=[in_vmem] * 3,
        out_specs=in_hbm,
        scratch_shapes=[VMEM((cols, rows), F32), pltpu.SemaphoreType.DMA((4,))],
        compiler_params=params,
    )(*[pltpu.with_memory_space_constraint(a, VMEM) for a in (near, coefs, col_basis)])
    return (others[0], residual)


def solution(mesh):
    in_specs = (
        P(None, ("wide", "grp")),
        P(None, ("wide", "grp")),
        P(None, ("wide", "grp")),
        P(None, ("wide", "grp")),
        P(None, None, ("wide", "grp")),
        P(None, None, ("wide", "grp")),
    )
    out_specs = (P(None, ("wide", "grp")), P(None, ("wide", "grp")))
    return jax.shard_map(
        per_device, mesh=mesh, in_specs=in_specs, out_specs=out_specs, check_vma=False
    )
```

time: 55.1 us -> 44 us (0.80)
  matrix products: 9.84 us -> 0 us
  Pallas kernels: 0 us -> 9.42 us
  starting transfers between devices: 18.9 us -> 14.7 us
  local copies, waits for them, and re-layouts: 3.32 us -> 0.03 us
  other arithmetic: 2.43 us -> 0.14 us
  waiting for transfers between devices: 19.3 us -> 18.7 us
    dot_general x11 -> x0, matrix products: 9.84 us -> none  [the longest x2 3.73 us: residual_of(): partials = jnp.einsum('pn,lrn->lpr', field, row_basis[1:], precision=DOT)]
    pallas_call x0 -> x9, Pallas kernels: none -> 9.42 us  [the longest x7 6.24 us: run(): pl.pallas_call(kernel, out_shape=[VMEM(shape, F32) if inside else jax.Sha...]
    ppermute x18 -> x16, starting transfers between devices: 18.9 us -> 14.7 us  [swap(): return lax.ppermute(block, AXES, route)]
    unnamed x28 -> x8, local copies, waits for them, and re-layouts: 1.92 us -> 0.02 us
    add x2, other arithmetic: 0.89 us -> 0.01 us  [in_lanes(): low_next = (low + low_got)[1:]]
    add x2, other arithmetic: 0.81 us -> 0.01 us  [in_lanes(): jnp.where(first, fourth, fifth)]
    slice x6 -> x2, local copies, waits for them, and re-layouts: 0.67 us -> 0.01 us  [in_lanes(): near = apply(1, near, jnp.stack([low_got[0], low_got_next[0]]))]
    another operation x2, local copies, waits for them, and re-layouts: 0.65 us -> 0.01 us  [in_lanes(): other, third = swap(jnp.stack([result, third]), both(1, 0))]
  transfers between devices with their start and end apart: 18 -> 16, of which waited for: 11 -> 8; matrix products, arithmetic and copies ran while one was open for 12% -> 0% of each run, Pallas kernels for 0% -> 11%
where the time goes in v2:
time: 44 us; the launch traced here: 43.9 us
  waiting for transfers between devices  18.7 us (42%)
  starting transfers between devices  14.7 us (33%)
  Pallas kernels  9.42 us (21%)
  between operations  0.9 us (2%)
    ppermute x16, waiting for transfers between devices, swap(): return lax.ppermute(block, AXES, route)  18.7 us
    ppermute x16, starting transfers between devices, swap(): return lax.ppermute(block, AXES, route)  14.7 us
    pallas_call x7, Pallas kernels, run(): pl.pallas_call(kernel, out_shape=[VMEM(shape, F32) if inside else jax.Sha...  6.24 us
    pallas_call x1, Pallas kernels, per_device(): pl.pallas_call(first_top_kernel, out_shape=[VMEM(top_out[0], F32), VMEM(s...  1.88 us
    pallas_call x1, Pallas kernels, per_device(): pl.pallas_call(functools.partial(last_kernel, start), out_shape=jax.Shape...  1.3 us
  transfers between devices with their start and end apart: 16, of which 8 were waited for; matrix products, arithmetic and copies ran while one was open for 0% of the time, Pallas kernels for 11%

profile of v2, /device:TPU:0, one launch (start us, length us, event | category | flops | bytes accessed | tf_op | source)
XLA Modules:
  0.0 43.9 jit_solution(7101356722514137988)
XLA Ops:
  0.7 1.9 %shard_map.77 = (f32[2,48,128]{2,1,0:T(8,128)S(1)}, f32[64,1024]{1,0:T(8,128)S(1)}, f32[6,96,1024]{2,1,0:T(8,128)S(1)}) custom-call(f32[64,1024]{1,0:T(8,128)} %field_hbm.1, f32[6,96,1024]{2,1,0:T(8,128)} %row_hbm.1), custom_call_target="tpu_custom_call" | custom-call | tf_op jit(solution)/shard_map/pallas_call | solution.py:225
  2.6 0.5 %collective-permute-start.2 = (f32[48,128]{1,0:T(8,128)S(1)}, f32[48,128]{1,0:T(8,128)S(1)}, u32[]{:S(2)}, u32[]{:S(2)}) collective-permute-start(f32[48,128]{1,0:T(8,128)S(1)} %select_bitcast_fusion.5), channel_id=1, source_target_pairs={{0,4},{1,5},{2,6},{3,7},{4,0},{5,1},{6,2},{7,3},{8,12},{9,13},{10,... | collective-permute-start | bytes 73736 | tf_op jit(solution)/shard_map/ppermute | solution.py:34
  3.1 0.7 %shard_map.79 = f32[3,48,128]{2,1,0:T(8,128)S(1)} custom-call(f32[64,1024]{1,0:T(8,128)S(1)} %get-tuple-element.13.field, f32[6,96,1024]{2,1,0:T(8,128)S(1)} %get-tuple-element.14.row_basis), custom_call_target="tpu_custom_call" | custom-call | tf_op jit(solution)/shard_map/pallas_call | solution.py:206
  3.8 2.7 %collective-permute-start = (f32[3,48,128]{2,1,0:T(8,128)S(1)}, f32[3,48,128]{2,1,0:T(8,128)S(1)}, u32[]{:S(2)}, u32[]{:S(2)}) collective-permute-start(f32[3,48,128]{2,1,0:T(8,128)S(1)} %shard_map.79), channel_id=1, source_target_pairs={{0,1},{1,0},{2,3},{3,2},{4,5},{5,4},{6,7},{7,6},{8,9},{9,8},{10,11... | collective-permute-start | bytes 221192 | tf_op jit(solution)/shard_map/ppermute | solution.py:34
  6.5 0.2 collective-permute-start.3
  6.6 2.7 %collective-permute-done = f32[3,48,128]{2,1,0:T(8,128)S(1)} collective-permute-done((f32[3,48,128]{2,1,0:T(8,128)S(1)}, f32[3,48,128]{2,1,0:T(8,128)S(1)}, u32[]{:S(2)}, u32[]{:S(2)}) %collective-permute-start) | collective-permute-done | bytes 73760 | tf_op jit(solution)/shard_map/ppermute | solution.py:34
  9.4 2.8 %collective-permute-start.1 = (f32[2,48,128]{2,1,0:T(8,128)S(1)}, f32[2,48,128]{2,1,0:T(8,128)S(1)}, u32[]{:S(2)}, u32[]{:S(2)}) collective-permute-start(f32[2,48,128]{2,1,0:T(8,128)S(1)} %slice_add_fusion.1), channel_id=1, source_target_pairs={{0,2},{1,3},{2,0},{3,1},{4,6},{5,7},{6,4},{7,5},{8,10},{9,11},{10,... | collective-permute-start | bytes 147464 | tf_op jit(solution)/shard_map/ppermute | solution.py:34
  12.2 0.1 collective-permute-start.4
  12.3 0.9 %shard_map.78.near = f32[64,1024]{1,0:T(8,128)S(1)} custom-call(f32[64,1024]{1,0:T(8,128)S(1)} %get-tuple-element.13.field, f32[64,1024]{1,0:T(8,128)S(1)} %copy-done.3, f32[512,1024]{1,0:T(8,128)S(1)} %copy-done.1, f32[6,96,1024]{2,1,0:T(8,128)S(1)} %copy-done, f32[6,96,1024]{2,1,0:T(8,128)S(1)} %get-tuple-element.14.row_basis), custom_call_target="tpu_custom_call" | custom-call | tf_op jit(solution)/shard_map/pallas_call | solution.py:206
  13.3 3.2 %collective-permute-done.4 = f32[48,128]{1,0:T(8,128)S(1)} collective-permute-done((f32[48,128]{1,0:T(8,128)S(1)}, f32[48,128]{1,0:T(8,128)S(1)}, u32[]{:S(2)}, u32[]{:S(2)}) %collective-permute-start.4) | collective-permute-done | bytes 24608 | tf_op jit(solution)/shard_map/ppermute | solution.py:34
  16.4 2.4 %collective-permute-start.6 = (f32[48,128]{1,0:T(8,128)S(1)}, f32[48,128]{1,0:T(8,128)S(1)}, u32[]{:S(2)}, u32[]{:S(2)}) collective-permute-start(f32[48,128]{1,0:T(8,128)S(1)} %add.39), channel_id=1, source_target_pairs={{0,24},{1,25},{2,26},{3,27},{4,28},{5,29},{6,30},{7,31},{8,16},{9,... | collective-permute-start | bytes 73736 | tf_op jit(solution)/shard_map/ppermute | solution.py:34
  18.9 3.2 %collective-permute-done.5 = f32[48,128]{1,0:T(8,128)S(1)} collective-permute-done((f32[48,128]{1,0:T(8,128)S(1)}, f32[48,128]{1,0:T(8,128)S(1)}, u32[]{:S(2)}, u32[]{:S(2)}) %collective-permute-start.5) | collective-permute-done | bytes 24608 | tf_op jit(solution)/shard_map/ppermute | solution.py:34
  22.2 0.1 collective-permute-start.7
  22.3 0.5 %shard_map.80.near = f32[64,1024]{1,0:T(8,128)S(1)} custom-call(f32[64,1024]{1,0:T(8,128)S(1)} %shard_map.78.near, f32[2,48,128]{2,1,0:T(8,128)S(1)} %pad_maximum_fusion.2.coefs, f32[6,96,1024]{2,1,0:T(8,128)S(1)} %copy-done), custom_call_target="tpu_custom_call" | custom-call | tf_op jit(solution)/shard_map/pallas_call | solution.py:206
  22.7 0.7 %collective-permute-done.7 = f32[2,48,128]{2,1,0:T(8,128)S(1)} collective-permute-done((f32[2,48,128]{2,1,0:T(8,128)S(1)}, f32[2,48,128]{2,1,0:T(8,128)S(1)}, u32[]{:S(2)}, u32[]{:S(2)}) %collective-permute-start.7) | collective-permute-done | bytes 49184 | tf_op jit(solution)/shard_map/ppermute | solution.py:34
  23.5 1.5 %shard_map.81 = (f32[64,1024]{1,0:T(8,128)S(1)}, f32[2,48,128]{2,1,0:T(8,128)S(1)}) custom-call(f32[64,1024]{1,0:T(8,128)S(1)} %shard_map.80.near, f32[3,48,128]{2,1,0:T(8,128)S(1)} %pad_maximum_fusion.coefs, f32[64,1024]{1,0:T(8,128)S(1)} %get-tuple-element.13.field, f32[6,96,1024]{2,1,0:T(8,128)S(1)} %copy-done, f32[512,1024]{1,0:T(8,128)S(1)} %copy-done.2, ...), custom_call_target="tpu_custom_call" | custom-call | tf_op jit(solution)/shard_map/pallas_call | solution.py:206
  25.1 0.2 collective-permute-start.10
  25.3 0.7 %shard_map.83 = f32[3,48,128]{2,1,0:T(8,128)S(1)} custom-call(f32[64,1024]{1,0:T(8,128)S(1)} %get-tuple-element.18.field, f32[6,96,1024]{2,1,0:T(8,128)S(1)} %get-tuple-element.14.row_basis), custom_call_target="tpu_custom_call" | custom-call | tf_op jit(solution)/shard_map/pallas_call | solution.py:206
  26.0 1.9 %collective-permute-start.8 = (f32[3,48,128]{2,1,0:T(8,128)S(1)}, f32[3,48,128]{2,1,0:T(8,128)S(1)}, u32[]{:S(2)}, u32[]{:S(2)}) collective-permute-start(f32[3,48,128]{2,1,0:T(8,128)S(1)} %shard_map.83), channel_id=1, source_target_pairs={{0,1},{1,0},{2,3},{3,2},{4,5},{5,4},{6,7},{7,6},{8,9},{9,8},{10,11... | collective-permute-start | bytes 221192 | tf_op jit(solution)/shard_map/ppermute | solution.py:34
  27.9 0.1 collective-permute-start.11
  28.0 2.7 %collective-permute-done.8 = f32[3,48,128]{2,1,0:T(8,128)S(1)} collective-permute-done((f32[3,48,128]{2,1,0:T(8,128)S(1)}, f32[3,48,128]{2,1,0:T(8,128)S(1)}, u32[]{:S(2)}, u32[]{:S(2)}) %collective-permute-start.8) | collective-permute-done | bytes 73760 | tf_op jit(solution)/shard_map/ppermute | solution.py:34
  30.7 1.4 %collective-permute-start.9 = (f32[2,48,128]{2,1,0:T(8,128)S(1)}, f32[2,48,128]{2,1,0:T(8,128)S(1)}, u32[]{:S(2)}, u32[]{:S(2)}) collective-permute-start(f32[2,48,128]{2,1,0:T(8,128)S(1)} %slice_add_fusion), channel_id=1, source_target_pairs={{0,2},{1,3},{2,0},{3,1},{4,6},{5,7},{6,4},{7,5},{8,10},{9,11},{10,... | collective-permute-start | bytes 147464 | tf_op jit(solution)/shard_map/ppermute | solution.py:34
  32.0 0.6 %collective-permute-start.12 = (f32[48,128]{1,0:T(8,128)S(1)}, f32[48,128]{1,0:T(8,128)S(1)}, u32[]{:S(2)}, u32[]{:S(2)}) collective-permute-start(f32[48,128]{1,0:T(8,128)S(1)} %add.44), channel_id=1, source_target_pairs={{0,6},{1,7},{2,4},{3,5},{4,2},{5,3},{6,0},{7,1},{8,14},{9,15},{10,... | collective-permute-start | bytes 73736 | tf_op jit(solution)/shard_map/ppermute | solution.py:34
  32.7 1.5 %shard_map.82 = (f32[64,1024]{1,0:T(8,128)S(1)}, f32[64,1024]{1,0:T(8,128)}) custom-call(f32[64,1024]{1,0:T(8,128)S(1)} %get-tuple-element.18.field, f32[64,1024]{1,0:T(8,128)S(1)} %copy-done.3, f32[512,1024]{1,0:T(8,128)S(1)} %copy-done.1, f32[6,96,1024]{2,1,0:T(8,128)S(1)} %copy-done, f32[6,96,1024]{2,1,0:T(8,128)S(1)} %get-tuple-element.14.row_basis), custom_call_target="tpu_custom_call" | custom-call | tf_op jit(solution)/shard_map/pallas_call | solution.py:206
  34.2 2.3 %collective-permute-done.12 = f32[48,128]{1,0:T(8,128)S(1)} collective-permute-done((f32[48,128]{1,0:T(8,128)S(1)}, f32[48,128]{1,0:T(8,128)S(1)}, u32[]{:S(2)}, u32[]{:S(2)}) %collective-permute-start.12) | collective-permute-done | bytes 24608 | tf_op jit(solution)/shard_map/ppermute | solution.py:34
  36.5 1.5 %collective-permute-start.14 = (f32[48,128]{1,0:T(8,128)S(1)}, f32[48,128]{1,0:T(8,128)S(1)}, u32[]{:S(2)}, u32[]{:S(2)}) collective-permute-start(f32[48,128]{1,0:T(8,128)S(1)} %add.45), channel_id=1, source_target_pairs={{0,24},{1,25},{2,26},{3,27},{4,28},{5,29},{6,30},{7,31},{8,16},{9,... | collective-permute-start | bytes 73736 | tf_op jit(solution)/shard_map/ppermute | solution.py:34
  38.0 3.2 %collective-permute-done.13 = f32[48,128]{1,0:T(8,128)S(1)} collective-permute-done((f32[48,128]{1,0:T(8,128)S(1)}, f32[48,128]{1,0:T(8,128)S(1)}, u32[]{:S(2)}, u32[]{:S(2)}) %collective-permute-start.13) | collective-permute-done | bytes 24608 | tf_op jit(solution)/shard_map/ppermute | solution.py:34
  41.2 0.0 collective-permute-done.14
  41.3 0.2 collective-permute-start.15
  41.4 0.5 %shard_map.84.near = f32[64,1024]{1,0:T(8,128)S(1)} custom-call(f32[64,1024]{1,0:T(8,128)S(1)} %get-tuple-element.20.near, f32[2,48,128]{2,1,0:T(8,128)S(1)} %pad_maximum_fusion.4.coefs, f32[6,96,1024]{2,1,0:T(8,128)S(1)} %copy-done), custom_call_target="tpu_custom_call" | custom-call | tf_op jit(solution)/shard_map/pallas_call | solution.py:206
  41.9 0.6 %collective-permute-done.15 = f32[2,48,128]{2,1,0:T(8,128)S(1)} collective-permute-done((f32[2,48,128]{2,1,0:T(8,128)S(1)}, f32[2,48,128]{2,1,0:T(8,128)S(1)}, u32[]{:S(2)}, u32[]{:S(2)}) %collective-permute-start.15) | collective-permute-done | bytes 49184 | tf_op jit(solution)/shard_map/ppermute | solution.py:34
  42.6 1.3 %shard_map.85 = f32[64,1024]{1,0:T(8,128)} custom-call(f32[64,1024]{1,0:T(8,128)S(1)} %shard_map.84.near, f32[3,48,128]{2,1,0:T(8,128)S(1)} %pad_maximum_fusion.1.coefs, f32[6,96,1024]{2,1,0:T(8,128)S(1)} %copy-done), custom_call_target="tpu_custom_call" | custom-call | tf_op jit(solution)/shard_map/pallas_call | solution.py:258
  (43 shorter events, 0.2 us)
Async XLA Ops:
  0.6 11.7 %copy-start = (f32[6,96,1024]{2,1,0:T(8,128)S(1)}, f32[6,96,1024]{2,1,0:T(8,128)}, u32[]{:S(2)}) copy-start(f32[6,96,1024]{2,1,0:T(8,128)} %col_basis.11) | copy-start | bytes 7077892
  0.7 11.7 %copy-start.1 = (f32[512,1024]{1,0:T(8,128)S(1)}, f32[512,1024]{1,0:T(8,128)}, u32[]{:S(2)}) copy-start(f32[512,1024]{1,0:T(8,128)} %leaf_blocks.3) | copy-start | bytes 6291460
  0.7 11.7 %copy-start.3 = (f32[64,1024]{1,0:T(8,128)S(1)}, f32[64,1024]{1,0:T(8,128)}, u32[]{:S(2)}) copy-start(f32[64,1024]{1,0:T(8,128)} %incident.3) | copy-start | bytes 786436
  2.6 3.9 %collective-permute-start.2 = (f32[48,128]{1,0:T(8,128)S(1)}, f32[48,128]{1,0:T(8,128)S(1)}, u32[]{:S(2)}, u32[]{:S(2)}) collective-permute-start(f32[48,128]{1,0:T(8,128)S(1)} %select_bitcast_fusion.5), channel_id=1, source_target_pairs={{0,4},{1,5},{2,6},{3,7},{4,0},{5,1},{6,2},{7,3},{8,12},{9,13},{10,... | collective-permute-start | bytes 73736 | tf_op jit(solution)/shard_map/ppermute | solution.py:34
  3.8 5.6 %collective-permute-start = (f32[3,48,128]{2,1,0:T(8,128)S(1)}, f32[3,48,128]{2,1,0:T(8,128)S(1)}, u32[]{:S(2)}, u32[]{:S(2)}) collective-permute-start(f32[3,48,128]{2,1,0:T(8,128)S(1)} %shard_map.79), channel_id=1, source_target_pairs={{0,1},{1,0},{2,3},{3,2},{4,5},{5,4},{6,7},{7,6},{8,9},{9,8},{10,11... | collective-permute-start | bytes 221192 | tf_op jit(solution)/shard_map/ppermute | solution.py:34
  6.5 5.8 %collective-permute-start.3 = (f32[48,128]{1,0:T(8,128)S(1)}, f32[48,128]{1,0:T(8,128)S(1)}, u32[]{:S(2)}, u32[]{:S(2)}) collective-permute-start(f32[48,128]{1,0:T(8,128)S(1)} %bitcast_add_fusion.1), channel_id=1, source_target_pairs={{0,5},{1,4},{2,7},{3,6},{4,1},{5,0},{6,3},{7,2},{8,13},{9,12},{10,... | collective-permute-start | bytes 73736 | tf_op jit(solution)/shard_map/ppermute | solution.py:34
  9.4 9.5 %collective-permute-start.1 = (f32[2,48,128]{2,1,0:T(8,128)S(1)}, f32[2,48,128]{2,1,0:T(8,128)S(1)}, u32[]{:S(2)}, u32[]{:S(2)}) collective-permute-start(f32[2,48,128]{2,1,0:T(8,128)S(1)} %slice_add_fusion.1), channel_id=1, source_target_pairs={{0,2},{1,3},{2,0},{3,1},{4,6},{5,7},{6,4},{7,5},{8,10},{9,11},{10,... | collective-permute-start | bytes 147464 | tf_op jit(solution)/shard_map/ppermute | solution.py:34
  12.2 4.2 %collective-permute-start.4 = (f32[48,128]{1,0:T(8,128)S(1)}, f32[48,128]{1,0:T(8,128)S(1)}, u32[]{:S(2)}, u32[]{:S(2)}) collective-permute-start(f32[48,128]{1,0:T(8,128)S(1)} %add.38), channel_id=1, source_target_pairs={{0,6},{1,7},{2,4},{3,5},{4,2},{5,3},{6,0},{7,1},{8,14},{9,15},{10,... | collective-permute-start | bytes 73736 | tf_op jit(solution)/shard_map/ppermute | solution.py:34
  13.2 10.3 %copy-start.2 = (f32[512,1024]{1,0:T(8,128)S(1)}, f32[512,1024]{1,0:T(8,128)}, u32[]{:S(2)}) copy-start(f32[512,1024]{1,0:T(8,128)} %leaf_inverse.1) | copy-start | bytes 6291460
  16.4 5.7 %collective-permute-start.6 = (f32[48,128]{1,0:T(8,128)S(1)}, f32[48,128]{1,0:T(8,128)S(1)}, u32[]{:S(2)}, u32[]{:S(2)}) collective-permute-start(f32[48,128]{1,0:T(8,128)S(1)} %add.39), channel_id=1, source_target_pairs={{0,24},{1,25},{2,26},{3,27},{4,28},{5,29},{6,30},{7,31},{8,16},{9,... | collective-permute-start | bytes 73736 | tf_op jit(solution)/shard_map/ppermute | solution.py:34
  18.9 3.3 %collective-permute-start.5 = (f32[48,128]{1,0:T(8,128)S(1)}, f32[48,128]{1,0:T(8,128)S(1)}, u32[]{:S(2)}, u32[]{:S(2)}) collective-permute-start(f32[48,128]{1,0:T(8,128)S(1)} %add.39), channel_id=1, source_target_pairs={{0,12},{1,21},{2,22},{3,15},{4,16},{5,9},{6,10},{7,19},{8,28},{9,5... | collective-permute-start | bytes 73736 | tf_op jit(solution)/shard_map/ppermute | solution.py:34
  22.2 1.3 %collective-permute-start.7 = (f32[2,48,128]{2,1,0:T(8,128)S(1)}, f32[2,48,128]{2,1,0:T(8,128)S(1)}, u32[]{:S(2)}, u32[]{:S(2)}) collective-permute-start(f32[2,48,128]{2,1,0:T(8,128)S(1)} %pad_maximum_fusion.3), channel_id=1, source_target_pairs={{0,4},{1,5},{2,6},{3,7},{4,0},{5,1},{6,2},{7,3},{8,12},{9,13},{10,... | collective-permute-start | bytes 147464 | tf_op jit(solution)/shard_map/ppermute | solution.py:34
  25.1 2.8 %collective-permute-start.10 = (f32[48,128]{1,0:T(8,128)S(1)}, f32[48,128]{1,0:T(8,128)S(1)}, u32[]{:S(2)}, u32[]{:S(2)}) collective-permute-start(f32[48,128]{1,0:T(8,128)S(1)} %select_bitcast_fusion.2), channel_id=1, source_target_pairs={{0,4},{1,5},{2,6},{3,7},{4,0},{5,1},{6,2},{7,3},{8,12},{9,13},{10,... | collective-permute-start | bytes 73736 | tf_op jit(solution)/shard_map/ppermute | solution.py:34
  26.0 4.7 %collective-permute-start.8 = (f32[3,48,128]{2,1,0:T(8,128)S(1)}, f32[3,48,128]{2,1,0:T(8,128)S(1)}, u32[]{:S(2)}, u32[]{:S(2)}) collective-permute-start(f32[3,48,128]{2,1,0:T(8,128)S(1)} %shard_map.83), channel_id=1, source_target_pairs={{0,1},{1,0},{2,3},{3,2},{4,5},{5,4},{6,7},{7,6},{8,9},{9,8},{10,11... | collective-permute-start | bytes 221192 | tf_op jit(solution)/shard_map/ppermute | solution.py:34
  27.9 4.1 %collective-permute-start.11 = (f32[48,128]{1,0:T(8,128)S(1)}, f32[48,128]{1,0:T(8,128)S(1)}, u32[]{:S(2)}, u32[]{:S(2)}) collective-permute-start(f32[48,128]{1,0:T(8,128)S(1)} %bitcast_add_fusion), channel_id=1, source_target_pairs={{0,5},{1,4},{2,7},{3,6},{4,1},{5,0},{6,3},{7,2},{8,13},{9,12},{10,... | collective-permute-start | bytes 73736 | tf_op jit(solution)/shard_map/ppermute | solution.py:34
  30.7 7.3 %collective-permute-start.9 = (f32[2,48,128]{2,1,0:T(8,128)S(1)}, f32[2,48,128]{2,1,0:T(8,128)S(1)}, u32[]{:S(2)}, u32[]{:S(2)}) collective-permute-start(f32[2,48,128]{2,1,0:T(8,128)S(1)} %slice_add_fusion), channel_id=1, source_target_pairs={{0,2},{1,3},{2,0},{3,1},{4,6},{5,7},{6,4},{7,5},{8,10},{9,11},{10,... | collective-permute-start | bytes 147464 | tf_op jit(solution)/shard_map/ppermute | solution.py:34
  32.0 4.5 %collective-permute-start.12 = (f32[48,128]{1,0:T(8,128)S(1)}, f32[48,128]{1,0:T(8,128)S(1)}, u32[]{:S(2)}, u32[]{:S(2)}) collective-permute-start(f32[48,128]{1,0:T(8,128)S(1)} %add.44), channel_id=1, source_target_pairs={{0,6},{1,7},{2,4},{3,5},{4,2},{5,3},{6,0},{7,1},{8,14},{9,15},{10,... | collective-permute-start | bytes 73736 | tf_op jit(solution)/shard_map/ppermute | solution.py:34
  36.5 4.7 %collective-permute-start.14 = (f32[48,128]{1,0:T(8,128)S(1)}, f32[48,128]{1,0:T(8,128)S(1)}, u32[]{:S(2)}, u32[]{:S(2)}) collective-permute-start(f32[48,128]{1,0:T(8,128)S(1)} %add.45), channel_id=1, source_target_pairs={{0,24},{1,25},{2,26},{3,27},{4,28},{5,29},{6,30},{7,31},{8,16},{9,... | collective-permute-start | bytes 73736 | tf_op jit(solution)/shard_map/ppermute | solution.py:34
  38.0 3.3 %collective-permute-start.13 = (f32[48,128]{1,0:T(8,128)S(1)}, f32[48,128]{1,0:T(8,128)S(1)}, u32[]{:S(2)}, u32[]{:S(2)}) collective-permute-start(f32[48,128]{1,0:T(8,128)S(1)} %add.45), channel_id=1, source_target_pairs={{0,12},{1,21},{2,22},{3,15},{4,16},{5,9},{6,10},{7,19},{8,28},{9,5... | collective-permute-start | bytes 73736 | tf_op jit(solution)/shard_map/ppermute | solution.py:34
  41.3 1.3 %collective-permute-start.15 = (f32[2,48,128]{2,1,0:T(8,128)S(1)}, f32[2,48,128]{2,1,0:T(8,128)S(1)}, u32[]{:S(2)}, u32[]{:S(2)}) collective-permute-start(f32[2,48,128]{2,1,0:T(8,128)S(1)} %pad_maximum_fusion.5), channel_id=1, source_target_pairs={{0,4},{1,5},{2,6},{3,7},{4,0},{5,1},{6,2},{7,3},{8,12},{9,13},{10,... | collective-permute-start | bytes 147464 | tf_op jit(solution)/shard_map/ppermute | solution.py:34

commit v3 on v2

--- a/solution.py
+++ b/solution.py
@@ -52,31 +52,41 @@
     return near, 1 + len(gathered) - TOP, jnp.stack(gathered[-TOP:]), others
 
 
-def in_lanes(low, top, near_of, apply):
-    wide, grp = lax.axis_index("wide"), lax.axis_index("grp")
-    ones = wide ^ (wide >> 1) ^ (wide >> 2) ^ grp ^ (grp >> 1)
-    first = (ones & 1) == 0
-    fourth, fifth = top[0], top[1]
-    mine = jnp.where(first, fourth, fifth) + swap(jnp.where(first, fifth, fourth), both(1, 0))
-    low_got = swap(low, both(0, 1))
-    low_next = (low + low_got)[1:]
-    mine = mine + swap(mine, both(1, 1))
+def in_first_lane():
+    ones = lax.axis_index("wide") ^ lax.axis_index("grp")
+    for shift in range(1, max(bits_of("wide"), bits_of("grp"))):
+        ones ^= (lax.axis_index("wide") >> shift) ^ (lax.axis_index("grp") >> shift)
+    return (ones & 1) == 0
+
+
+def in_lanes(first, low, top, near_of, apply):
+    core = both(1, 0)
+    top = top + swap(top, core)
+    next_low = swap(jnp.stack([low[0], low[2]]), both(0, 1))
+    top = top + swap(top, both(1, 1))
+    top, next_low = lax.optimization_barrier((top, next_low))
     near, *others = near_of()
-    mine = mine + swap(mine, both(1, 2))
-    low_got_next = swap(low_next, both(0, 2))
-    third = (low_next + low_got_next)[1]
-    across = swap(mine, ((3, 0), (5, 0)))
-    corner = swap(mine, both(6, 0))
-    across, third = lax.optimization_barrier((across, third))
-    near = apply(1, near, jnp.stack([low_got[0], low_got_next[0]]))
-    result = jnp.where(first, across, across + corner)
-    other, third = swap(jnp.stack([result, third]), both(1, 0))
-    return near, 3, jnp.stack([third, jnp.where(first, result, other), jnp.where(first, other, result)]), others
-
-
-def exchange(low, top, near_of, apply):
+    own = jnp.where(first, top[0], top[1])
+    far_low = swap(low[1:], both(0, 2))
+    last_low = swap(low[1:], both(0, 3))
+    far = swap(own, ((2, 2), (4, 2)))
+    corner = swap(top[1], ((6, 0), (7, 2)))
+    own, far_low = lax.optimization_barrier((own, far_low))
+    beside = swap(own, ((3, 0), (5, 0)))
+    far_low, last_low, far, corner, beside = lax.optimization_barrier((far_low, last_low, far, corner, beside))
+    both_low = far_low + last_low
+    near = apply(1, near, jnp.stack([next_low[0], both_low[0]]))
+    mine = beside + far
+    third = low[2] + next_low[1] + both_low[1]
+    third, other, corner_other = swap(jnp.stack([third, mine, corner]), core)
+    fourth = jnp.where(first, mine, other)
+    fifth = jnp.where(first, other, mine) + (corner + corner_other)
+    return near, 3, jnp.stack([third, fourth, fifth]), others
+
+
+def exchange(first, low, top, near_of, apply):
     if bits_of("grp") == 2 and bits_of("wide") == 3:
-        return in_lanes(low, top, near_of, apply)
+        return in_lanes(first, low, top, near_of, apply)
     return climb_tree(low, top, near_of, apply)
 
 
@@ -213,6 +223,7 @@
 
 
 def per_device(solution, incident, leaf_blocks, leaf_inverse, col_basis, row_basis):
+    solution, first = lax.optimization_barrier((solution, in_first_lane()))
     levels, rank, rows = row_basis.shape
     cols = solution.shape[0]
     dense = (packed_rows(cols, rank), LANES)
@@ -242,7 +253,7 @@
     def apply(start, near, coefs):
         return run(functools.partial(apply_kernel, start), [in_field], near, coefs, col_basis)[0]
 
-    near, start, coefs, _ = exchange(low, top, functools.partial(near_of, field), apply)
+    near, start, coefs, _ = exchange(first, low, top, functools.partial(near_of, field), apply)
     refined, top = run(
         functools.partial(refine_kernel, start),
         [in_field, top_out],
@@ -254,7 +265,7 @@
         row_basis,
     )
     (low,) = run(low_kernel, [low_out], refined, row_basis)
-    near, start, coefs, others = exchange(low, top, functools.partial(near_and_copy, refined), apply)
+    near, start, coefs, others = exchange(first, low, top, functools.partial(near_and_copy, refined), apply)
     residual = pl.pallas_call(
         functools.partial(last_kernel, start),
         out_shape=jax.ShapeDtypeStruct((cols, rows), F32),

time: 44 us -> 40.5 us (0.920)
  waiting for transfers between devices: 18.7 us -> 6.44 us
  starting transfers between devices: 14.7 us -> 23.4 us
    ppermute x16 -> x18, waiting for transfers between devices: 18.7 us -> 6.44 us  [swap(): return lax.ppermute(block, AXES, route)]
    ppermute x16 -> x18, starting transfers between devices: 14.7 us -> 23.4 us  [swap(): return lax.ppermute(block, AXES, route)]
  transfers between devices with their start and end apart: 16 -> 18, of which waited for: 8 -> 10; matrix products, arithmetic and copies ran while one was open for 0% -> 0% of each run, Pallas kernels for 11% -> 12%
where the time goes in v3:
time: 40.5 us; the launch traced here: 40.3 us
  starting transfers between devices  23.4 us (58%)
  Pallas kernels  9.44 us (23%)
  waiting for transfers between devices  6.44 us (16%)
  between operations  0.9 us (2%)
    ppermute x18, starting transfers between devices, swap(): return lax.ppermute(block, AXES, route)  23.4 us
    ppermute x18, waiting for transfers between devices, swap(): return lax.ppermute(block, AXES, route)  6.44 us
    pallas_call x7, Pallas kernels, run(): pl.pallas_call(kernel, out_shape=[VMEM(shape, F32) if inside else jax.Sha...  6.26 us
    pallas_call x1, Pallas kernels, per_device(): pl.pallas_call(first_top_kernel, out_shape=[VMEM(top_out[0], F32), VMEM(s...  1.88 us
    pallas_call x1, Pallas kernels, per_device(): pl.pallas_call(functools.partial(last_kernel, start), out_shape=jax.Shape...  1.3 us
  transfers between devices with their start and end apart: 18, of which 10 were waited for; matrix products, arithmetic and copies ran while one was open for 0% of the time, Pallas kernels for 12%

profile of v3, /device:TPU:0, one launch (start us, length us, event | category | flops | bytes accessed | tf_op | source)
XLA Modules:
  0.0 40.3 jit_solution(6429651492718756799)
XLA Ops:
  0.7 1.9 %shard_map.77 = (f32[2,48,128]{2,1,0:T(8,128)S(1)}, f32[64,1024]{1,0:T(8,128)S(1)}, f32[6,96,1024]{2,1,0:T(8,128)S(1)}) custom-call(f32[64,1024]{1,0:T(8,128)} %field_hbm, f32[6,96,1024]{2,1,0:T(8,128)} %row_hbm.1), custom_call_target="tpu_custom_call" | custom-call | tf_op jit(solution)/shard_map/pallas_call | solution.py:236
  2.6 0.5 %collective-permute-start = (f32[2,48,128]{2,1,0:T(8,128)S(1)}, f32[2,48,128]{2,1,0:T(8,128)S(1)}, u32[]{:S(2)}, u32[]{:S(2)}) collective-permute-start(f32[2,48,128]{2,1,0:T(8,128)S(1)} %get-tuple-element.32), channel_id=1, source_target_pairs={{0,4},{1,5},{2,6},{3,7},{4,0},{5,1},{6,2},{7,3},{8,12},{9,13},{10,... | collective-permute-start | bytes 147464 | tf_op jit(solution)/shard_map/ppermute | solution.py:34
  3.1 0.7 %shard_map.79 = f32[3,48,128]{2,1,0:T(8,128)S(1)} custom-call(f32[64,1024]{1,0:T(8,128)S(1)} %get-tuple-element.30.field, f32[6,96,1024]{2,1,0:T(8,128)S(1)} %get-tuple-element.31.row_basis), custom_call_target="tpu_custom_call" | custom-call | tf_op jit(solution)/shard_map/pallas_call | solution.py:216
  4.0 2.7 %collective-permute-start.1 = (f32[2,48,128]{2,1,0:T(8,128)S(1)}, f32[2,48,128]{2,1,0:T(8,128)S(1)}, u32[]{:S(2)}, u32[]{:S(2)}) collective-permute-start(f32[2,48,128]{2,1,0:T(8,128)S(1)} %add.52), channel_id=1, source_target_pairs={{0,5},{1,4},{2,7},{3,6},{4,1},{5,0},{6,3},{7,2},{8,13},{9,12},{10,... | collective-permute-start | bytes 147464 | tf_op jit(solution)/shard_map/ppermute | solution.py:34
  6.7 0.4 collective-permute-start.2
  7.0 3.7 %collective-permute-start.4 = (f32[2,48,128]{2,1,0:T(8,128)S(1)}, f32[2,48,128]{2,1,0:T(8,128)S(1)}, u32[]{:S(2)}, u32[]{:S(2)}) collective-permute-start(f32[2,48,128]{2,1,0:T(8,128)S(1)} %slice.80), channel_id=1, source_target_pairs={{0,3},{1,2},{2,1},{3,0},{4,7},{5,6},{6,5},{7,4},{8,11},{9,10},{10,... | collective-permute-start | bytes 147464 | tf_op jit(solution)/shard_map/ppermute | solution.py:34
  10.8 2.5 %collective-permute-start.6 = (f32[48,128]{1,0:T(8,128)S(1)}, f32[48,128]{1,0:T(8,128)S(1)}, u32[]{:S(2)}, u32[]{:S(2)}) collective-permute-start(f32[48,128]{1,0:T(8,128)S(1)} %slice_bitcast_fusion.5), channel_id=1, source_target_pairs={{0,24},{1,31},{2,28},{3,27},{4,26},{5,29},{6,30},{7,25},{8,22},{9,... | collective-permute-start | bytes 73736 | tf_op jit(solution)/shard_map/ppermute | solution.py:34
  13.3 3.0 %collective-permute-start.5 = (f32[48,128]{1,0:T(8,128)S(1)}, f32[48,128]{1,0:T(8,128)S(1)}, u32[]{:S(2)}, u32[]{:S(2)}) collective-permute-start(f32[48,128]{1,0:T(8,128)S(1)} %bitcast_select_fusion.1), channel_id=1, source_target_pairs={{0,10},{1,19},{2,16},{3,9},{4,22},{5,15},{6,12},{7,21},{8,26},{9,3... | collective-permute-start | bytes 73736 | tf_op jit(solution)/shard_map/ppermute | solution.py:34
  16.3 0.5 %collective-permute-start.7 = (f32[48,128]{1,0:T(8,128)S(1)}, f32[48,128]{1,0:T(8,128)S(1)}, u32[]{:S(2)}, u32[]{:S(2)}) collective-permute-start(f32[48,128]{1,0:T(8,128)S(1)} %bitcast_select_fusion.1), channel_id=1, source_target_pairs={{0,12},{1,21},{2,22},{3,15},{4,16},{5,9},{6,10},{7,19},{8,28},{9,5... | collective-permute-start | bytes 73736 | tf_op jit(solution)/shard_map/ppermute | solution.py:34
  16.8 0.9 %shard_map.78.near = f32[64,1024]{1,0:T(8,128)S(1)} custom-call(f32[64,1024]{1,0:T(8,128)S(1)} %get-tuple-element.30.field, f32[64,1024]{1,0:T(8,128)S(1)} %copy-done.3, f32[512,1024]{1,0:T(8,128)S(1)} %copy-done.1, f32[6,96,1024]{2,1,0:T(8,128)S(1)} %copy-done, f32[6,96,1024]{2,1,0:T(8,128)S(1)} %get-tuple-element.31.row_basis), custom_call_target="tpu_custom_call" | custom-call | tf_op jit(solution)/shard_map/pallas_call | solution.py:216
  17.8 1.1 %collective-permute-done.5 = f32[48,128]{1,0:T(8,128)S(1)} collective-permute-done((f32[48,128]{1,0:T(8,128)S(1)}, f32[48,128]{1,0:T(8,128)S(1)}, u32[]{:S(2)}, u32[]{:S(2)}) %collective-permute-start.5) | collective-permute-done | bytes 24608 | tf_op jit(solution)/shard_map/ppermute | solution.py:34
  18.9 0.6 %collective-permute-done.7 = f32[48,128]{1,0:T(8,128)S(1)} collective-permute-done((f32[48,128]{1,0:T(8,128)S(1)}, f32[48,128]{1,0:T(8,128)S(1)}, u32[]{:S(2)}, u32[]{:S(2)}) %collective-permute-start.7) | collective-permute-done | bytes 24608 | tf_op jit(solution)/shard_map/ppermute | solution.py:34
  19.6 0.9 %collective-permute-start.8 = (f32[3,48,128]{2,1,0:T(8,128)S(1)}, f32[3,48,128]{2,1,0:T(8,128)S(1)}, u32[]{:S(2)}, u32[]{:S(2)}) collective-permute-start(f32[3,48,128]{2,1,0:T(8,128)S(1)} %pad_maximum_fusion), channel_id=1, source_target_pairs={{0,4},{1,5},{2,6},{3,7},{4,0},{5,1},{6,2},{7,3},{8,12},{9,13},{10,... | collective-permute-start | bytes 221192 | tf_op jit(solution)/shard_map/ppermute | solution.py:34
  20.5 0.5 %shard_map.80.near = f32[64,1024]{1,0:T(8,128)S(1)} custom-call(f32[64,1024]{1,0:T(8,128)S(1)} %shard_map.78.near, f32[2,48,128]{2,1,0:T(8,128)S(1)} %pad_maximum_fusion.5.coefs, f32[6,96,1024]{2,1,0:T(8,128)S(1)} %copy-done), custom_call_target="tpu_custom_call" | custom-call | tf_op jit(solution)/shard_map/pallas_call | solution.py:216
  21.0 0.4 %collective-permute-done.8 = f32[3,48,128]{2,1,0:T(8,128)S(1)} collective-permute-done((f32[3,48,128]{2,1,0:T(8,128)S(1)}, f32[3,48,128]{2,1,0:T(8,128)S(1)}, u32[]{:S(2)}, u32[]{:S(2)}) %collective-permute-start.8) | collective-permute-done | bytes 73760 | tf_op jit(solution)/shard_map/ppermute | solution.py:34
  21.4 1.5 %shard_map.81 = (f32[64,1024]{1,0:T(8,128)S(1)}, f32[2,48,128]{2,1,0:T(8,128)S(1)}) custom-call(f32[64,1024]{1,0:T(8,128)S(1)} %shard_map.80.near, f32[3,48,128]{2,1,0:T(8,128)S(1)} %pad_maximum_fusion.1.coefs, f32[64,1024]{1,0:T(8,128)S(1)} %get-tuple-element.30.field, f32[6,96,1024]{2,1,0:T(8,128)S(1)} %copy-done, f32[512,1024]{1,0:T(8,128)S(1)} %copy-done.2, ...), custom_call_target="tpu_custom_call" | custom-call | tf_op jit(solution)/shard_map/pallas_call | solution.py:216
  23.0 0.4 %collective-permute-start.9 = (f32[2,48,128]{2,1,0:T(8,128)S(1)}, f32[2,48,128]{2,1,0:T(8,128)S(1)}, u32[]{:S(2)}, u32[]{:S(2)}) collective-permute-start(f32[2,48,128]{2,1,0:T(8,128)S(1)} %get-tuple-element.46), channel_id=1, source_target_pairs={{0,4},{1,5},{2,6},{3,7},{4,0},{5,1},{6,2},{7,3},{8,12},{9,13},{10,... | collective-permute-start | bytes 147464 | tf_op jit(solution)/shard_map/ppermute | solution.py:34
  23.4 0.7 %shard_map.83 = f32[3,48,128]{2,1,0:T(8,128)S(1)} custom-call(f32[64,1024]{1,0:T(8,128)S(1)} %get-tuple-element.43.field, f32[6,96,1024]{2,1,0:T(8,128)S(1)} %get-tuple-element.31.row_basis), custom_call_target="tpu_custom_call" | custom-call | tf_op jit(solution)/shard_map/pallas_call | solution.py:216
  24.3 1.5 %collective-permute-start.10 = (f32[2,48,128]{2,1,0:T(8,128)S(1)}, f32[2,48,128]{2,1,0:T(8,128)S(1)}, u32[]{:S(2)}, u32[]{:S(2)}) collective-permute-start(f32[2,48,128]{2,1,0:T(8,128)S(1)} %add.60), channel_id=1, source_target_pairs={{0,5},{1,4},{2,7},{3,6},{4,1},{5,0},{6,3},{7,2},{8,13},{9,12},{10,... | collective-permute-start | bytes 147464 | tf_op jit(solution)/shard_map/ppermute | solution.py:34
  25.8 0.6 %collective-permute-start.11 = (f32[2,48,128]{2,1,0:T(8,128)S(1)}, f32[2,48,128]{2,1,0:T(8,128)S(1)}, u32[]{:S(2)}, u32[]{:S(2)}) collective-permute-start(f32[2,48,128]{2,1,0:T(8,128)S(1)} %pad_maximum_fusion.6), channel_id=1, source_target_pairs={{0,1},{1,0},{2,3},{3,2},{4,5},{5,4},{6,7},{7,6},{8,9},{9,8},{10,11... | collective-permute-start | bytes 147464 | tf_op jit(solution)/shard_map/ppermute | solution.py:34
  26.3 2.0 %collective-permute-start.13 = (f32[2,48,128]{2,1,0:T(8,128)S(1)}, f32[2,48,128]{2,1,0:T(8,128)S(1)}, u32[]{:S(2)}, u32[]{:S(2)}) collective-permute-start(f32[2,48,128]{2,1,0:T(8,128)S(1)} %slice.85), channel_id=1, source_target_pairs={{0,3},{1,2},{2,1},{3,0},{4,7},{5,6},{6,5},{7,4},{8,11},{9,10},{10,... | collective-permute-start | bytes 147464 | tf_op jit(solution)/shard_map/ppermute | solution.py:34
  28.4 0.9 %collective-permute-start.12 = (f32[2,48,128]{2,1,0:T(8,128)S(1)}, f32[2,48,128]{2,1,0:T(8,128)S(1)}, u32[]{:S(2)}, u32[]{:S(2)}) collective-permute-start(f32[2,48,128]{2,1,0:T(8,128)S(1)} %slice.85), channel_id=1, source_target_pairs={{0,2},{1,3},{2,0},{3,1},{4,6},{5,7},{6,4},{7,5},{8,10},{9,11},{10,... | collective-permute-start | bytes 147464 | tf_op jit(solution)/shard_map/ppermute | solution.py:34
  29.3 0.6 %collective-permute-done.11 = f32[2,48,128]{2,1,0:T(8,128)S(1)} collective-permute-done((f32[2,48,128]{2,1,0:T(8,128)S(1)}, f32[2,48,128]{2,1,0:T(8,128)S(1)}, u32[]{:S(2)}, u32[]{:S(2)}) %collective-permute-start.11) | collective-permute-done | bytes 49184 | tf_op jit(solution)/shard_map/ppermute | solution.py:34
  29.9 1.8 %collective-permute-start.15 = (f32[48,128]{1,0:T(8,128)S(1)}, f32[48,128]{1,0:T(8,128)S(1)}, u32[]{:S(2)}, u32[]{:S(2)}) collective-permute-start(f32[48,128]{1,0:T(8,128)S(1)} %slice_bitcast_fusion.4), channel_id=1, source_target_pairs={{0,24},{1,31},{2,28},{3,27},{4,26},{5,29},{6,30},{7,25},{8,22},{9,... | collective-permute-start | bytes 73736 | tf_op jit(solution)/shard_map/ppermute | solution.py:34
  31.7 1.6 %collective-permute-start.14 = (f32[48,128]{1,0:T(8,128)S(1)}, f32[48,128]{1,0:T(8,128)S(1)}, u32[]{:S(2)}, u32[]{:S(2)}) collective-permute-start(f32[48,128]{1,0:T(8,128)S(1)} %bitcast_select_fusion), channel_id=1, source_target_pairs={{0,10},{1,19},{2,16},{3,9},{4,22},{5,15},{6,12},{7,21},{8,26},{9,3... | collective-permute-start | bytes 73736 | tf_op jit(solution)/shard_map/ppermute | solution.py:34
  33.3 1.0 %collective-permute-done.12 = f32[2,48,128]{2,1,0:T(8,128)S(1)} collective-permute-done((f32[2,48,128]{2,1,0:T(8,128)S(1)}, f32[2,48,128]{2,1,0:T(8,128)S(1)}, u32[]{:S(2)}, u32[]{:S(2)}) %collective-permute-start.12) | collective-permute-done | bytes 49184 | tf_op jit(solution)/shard_map/ppermute | solution.py:34
  34.3 0.3 collective-permute-start.16
  34.6 1.5 %shard_map.82 = (f32[64,1024]{1,0:T(8,128)S(1)}, f32[64,1024]{1,0:T(8,128)}) custom-call(f32[64,1024]{1,0:T(8,128)S(1)} %get-tuple-element.43.field, f32[64,1024]{1,0:T(8,128)S(1)} %copy-done.3, f32[512,1024]{1,0:T(8,128)S(1)} %copy-done.1, f32[6,96,1024]{2,1,0:T(8,128)S(1)} %copy-done, f32[6,96,1024]{2,1,0:T(8,128)S(1)} %get-tuple-element.31.row_basis), custom_call_target="tpu_custom_call" | custom-call | tf_op jit(solution)/shard_map/pallas_call | solution.py:216
  36.1 1.3 %collective-permute-done.14 = f32[48,128]{1,0:T(8,128)S(1)} collective-permute-done((f32[48,128]{1,0:T(8,128)S(1)}, f32[48,128]{1,0:T(8,128)S(1)}, u32[]{:S(2)}, u32[]{:S(2)}) %collective-permute-start.14) | collective-permute-done | bytes 24608 | tf_op jit(solution)/shard_map/ppermute | solution.py:34
  37.8 0.5 %shard_map.84.near = f32[64,1024]{1,0:T(8,128)S(1)} custom-call(f32[64,1024]{1,0:T(8,128)S(1)} %get-tuple-element.45.near, f32[2,48,128]{2,1,0:T(8,128)S(1)} %pad_maximum_fusion.7.coefs, f32[6,96,1024]{2,1,0:T(8,128)S(1)} %copy-done), custom_call_target="tpu_custom_call" | custom-call | tf_op jit(solution)/shard_map/pallas_call | solution.py:216
  38.2 0.8 %collective-permute-done.17 = f32[3,48,128]{2,1,0:T(8,128)S(1)} collective-permute-done((f32[3,48,128]{2,1,0:T(8,128)S(1)}, f32[3,48,128]{2,1,0:T(8,128)S(1)}, u32[]{:S(2)}, u32[]{:S(2)}) %collective-permute-start.17) | collective-permute-done | bytes 73760 | tf_op jit(solution)/shard_map/ppermute | solution.py:34
  39.0 1.3 %shard_map.85 = f32[64,1024]{1,0:T(8,128)} custom-call(f32[64,1024]{1,0:T(8,128)S(1)} %shard_map.84.near, f32[3,48,128]{2,1,0:T(8,128)S(1)} %pad_maximum_fusion.3.coefs, f32[6,96,1024]{2,1,0:T(8,128)S(1)} %copy-done), custom_call_target="tpu_custom_call" | custom-call | tf_op jit(solution)/shard_map/pallas_call | solution.py:269
  (51 shorter events, 0.9 us)
Async XLA Ops:
  0.6 16.2 %copy-start.1 = (f32[512,1024]{1,0:T(8,128)S(1)}, f32[512,1024]{1,0:T(8,128)}, u32[]{:S(2)}) copy-start(f32[512,1024]{1,0:T(8,128)} %leaf_blocks.3) | copy-start | bytes 6291460
  2.5 14.3 %copy-start = (f32[6,96,1024]{2,1,0:T(8,128)S(1)}, f32[6,96,1024]{2,1,0:T(8,128)}, u32[]{:S(2)}) copy-start(f32[6,96,1024]{2,1,0:T(8,128)} %col_basis.11) | copy-start | bytes 7077892
  2.5 14.3 %copy-start.3 = (f32[64,1024]{1,0:T(8,128)S(1)}, f32[64,1024]{1,0:T(8,128)}, u32[]{:S(2)}) copy-start(f32[64,1024]{1,0:T(8,128)} %incident.3) | copy-start | bytes 786436
  2.6 1.4 %collective-permute-start = (f32[2,48,128]{2,1,0:T(8,128)S(1)}, f32[2,48,128]{2,1,0:T(8,128)S(1)}, u32[]{:S(2)}, u32[]{:S(2)}) collective-permute-start(f32[2,48,128]{2,1,0:T(8,128)S(1)} %get-tuple-element.32), channel_id=1, source_target_pairs={{0,4},{1,5},{2,6},{3,7},{4,0},{5,1},{6,2},{7,3},{8,12},{9,13},{10,... | collective-permute-start | bytes 147464 | tf_op jit(solution)/shard_map/ppermute | solution.py:34
  4.0 6.8 %collective-permute-start.1 = (f32[2,48,128]{2,1,0:T(8,128)S(1)}, f32[2,48,128]{2,1,0:T(8,128)S(1)}, u32[]{:S(2)}, u32[]{:S(2)}) collective-permute-start(f32[2,48,128]{2,1,0:T(8,128)S(1)} %add.52), channel_id=1, source_target_pairs={{0,5},{1,4},{2,7},{3,6},{4,1},{5,0},{6,3},{7,2},{8,13},{9,12},{10,... | collective-permute-start | bytes 147464 | tf_op jit(solution)/shard_map/ppermute | solution.py:34
  6.7 4.1 %collective-permute-start.2 = (f32[2,48,128]{2,1,0:T(8,128)S(1)}, f32[2,48,128]{2,1,0:T(8,128)S(1)}, u32[]{:S(2)}, u32[]{:S(2)}) collective-permute-start(f32[2,48,128]{2,1,0:T(8,128)S(1)} %pad_maximum_fusion.4), channel_id=1, source_target_pairs={{0,1},{1,0},{2,3},{3,2},{4,5},{5,4},{6,7},{7,6},{8,9},{9,8},{10,11... | collective-permute-start | bytes 147464 | tf_op jit(solution)/shard_map/ppermute | solution.py:34
  7.0 10.7 %collective-permute-start.4 = (f32[2,48,128]{2,1,0:T(8,128)S(1)}, f32[2,48,128]{2,1,0:T(8,128)S(1)}, u32[]{:S(2)}, u32[]{:S(2)}) collective-permute-start(f32[2,48,128]{2,1,0:T(8,128)S(1)} %slice.80), channel_id=1, source_target_pairs={{0,3},{1,2},{2,1},{3,0},{4,7},{5,6},{6,5},{7,4},{8,11},{9,10},{10,... | collective-permute-start | bytes 147464 | tf_op jit(solution)/shard_map/ppermute | solution.py:34
  10.7 5.6 %collective-permute-start.3 = (f32[2,48,128]{2,1,0:T(8,128)S(1)}, f32[2,48,128]{2,1,0:T(8,128)S(1)}, u32[]{:S(2)}, u32[]{:S(2)}) collective-permute-start(f32[2,48,128]{2,1,0:T(8,128)S(1)} %slice.80), channel_id=1, source_target_pairs={{0,2},{1,3},{2,0},{3,1},{4,6},{5,7},{6,4},{7,5},{8,10},{9,11},{10,... | collective-permute-start | bytes 147464 | tf_op jit(solution)/shard_map/ppermute | solution.py:34
  10.8 7.0 %collective-permute-start.6 = (f32[48,128]{1,0:T(8,128)S(1)}, f32[48,128]{1,0:T(8,128)S(1)}, u32[]{:S(2)}, u32[]{:S(2)}) collective-permute-start(f32[48,128]{1,0:T(8,128)S(1)} %slice_bitcast_fusion.5), channel_id=1, source_target_pairs={{0,24},{1,31},{2,28},{3,27},{4,26},{5,29},{6,30},{7,25},{8,22},{9,... | collective-permute-start | bytes 73736 | tf_op jit(solution)/shard_map/ppermute | solution.py:34
  13.3 5.6 %collective-permute-start.5 = (f32[48,128]{1,0:T(8,128)S(1)}, f32[48,128]{1,0:T(8,128)S(1)}, u32[]{:S(2)}, u32[]{:S(2)}) collective-permute-start(f32[48,128]{1,0:T(8,128)S(1)} %bitcast_select_fusion.1), channel_id=1, source_target_pairs={{0,10},{1,19},{2,16},{3,9},{4,22},{5,15},{6,12},{7,21},{8,26},{9,3... | collective-permute-start | bytes 73736 | tf_op jit(solution)/shard_map/ppermute | solution.py:34
  16.3 3.3 %collective-permute-start.7 = (f32[48,128]{1,0:T(8,128)S(1)}, f32[48,128]{1,0:T(8,128)S(1)}, u32[]{:S(2)}, u32[]{:S(2)}) collective-permute-start(f32[48,128]{1,0:T(8,128)S(1)} %bitcast_select_fusion.1), channel_id=1, source_target_pairs={{0,12},{1,21},{2,22},{3,15},{4,16},{5,9},{6,10},{7,19},{8,28},{9,5... | collective-permute-start | bytes 73736 | tf_op jit(solution)/shard_map/ppermute | solution.py:34
  17.7 3.7 %copy-start.2 = (f32[512,1024]{1,0:T(8,128)S(1)}, f32[512,1024]{1,0:T(8,128)}, u32[]{:S(2)}) copy-start(f32[512,1024]{1,0:T(8,128)} %leaf_inverse.1) | copy-start | bytes 6291460
  19.6 1.8 %collective-permute-start.8 = (f32[3,48,128]{2,1,0:T(8,128)S(1)}, f32[3,48,128]{2,1,0:T(8,128)S(1)}, u32[]{:S(2)}, u32[]{:S(2)}) collective-permute-start(f32[3,48,128]{2,1,0:T(8,128)S(1)} %pad_maximum_fusion), channel_id=1, source_target_pairs={{0,4},{1,5},{2,6},{3,7},{4,0},{5,1},{6,2},{7,3},{8,12},{9,13},{10,... | collective-permute-start | bytes 221192 | tf_op jit(solution)/shard_map/ppermute | solution.py:34
  23.0 1.3 %collective-permute-start.9 = (f32[2,48,128]{2,1,0:T(8,128)S(1)}, f32[2,48,128]{2,1,0:T(8,128)S(1)}, u32[]{:S(2)}, u32[]{:S(2)}) collective-permute-start(f32[2,48,128]{2,1,0:T(8,128)S(1)} %get-tuple-element.46), channel_id=1, source_target_pairs={{0,4},{1,5},{2,6},{3,7},{4,0},{5,1},{6,2},{7,3},{8,12},{9,13},{10,... | collective-permute-start | bytes 147464 | tf_op jit(solution)/shard_map/ppermute | solution.py:34
  24.3 5.0 %collective-permute-start.10 = (f32[2,48,128]{2,1,0:T(8,128)S(1)}, f32[2,48,128]{2,1,0:T(8,128)S(1)}, u32[]{:S(2)}, u32[]{:S(2)}) collective-permute-start(f32[2,48,128]{2,1,0:T(8,128)S(1)} %add.60), channel_id=1, source_target_pairs={{0,5},{1,4},{2,7},{3,6},{4,1},{5,0},{6,3},{7,2},{8,13},{9,12},{10,... | collective-permute-start | bytes 147464 | tf_op jit(solution)/shard_map/ppermute | solution.py:34
  25.8 4.1 %collective-permute-start.11 = (f32[2,48,128]{2,1,0:T(8,128)S(1)}, f32[2,48,128]{2,1,0:T(8,128)S(1)}, u32[]{:S(2)}, u32[]{:S(2)}) collective-permute-start(f32[2,48,128]{2,1,0:T(8,128)S(1)} %pad_maximum_fusion.6), channel_id=1, source_target_pairs={{0,1},{1,0},{2,3},{3,2},{4,5},{5,4},{6,7},{7,6},{8,9},{9,8},{10,11... | collective-permute-start | bytes 147464 | tf_op jit(solution)/shard_map/ppermute | solution.py:34
  26.3 9.7 %collective-permute-start.13 = (f32[2,48,128]{2,1,0:T(8,128)S(1)}, f32[2,48,128]{2,1,0:T(8,128)S(1)}, u32[]{:S(2)}, u32[]{:S(2)}) collective-permute-start(f32[2,48,128]{2,1,0:T(8,128)S(1)} %slice.85), channel_id=1, source_target_pairs={{0,3},{1,2},{2,1},{3,0},{4,7},{5,6},{6,5},{7,4},{8,11},{9,10},{10,... | collective-permute-start | bytes 147464 | tf_op jit(solution)/shard_map/ppermute | solution.py:34
  28.4 5.9 %collective-permute-start.12 = (f32[2,48,128]{2,1,0:T(8,128)S(1)}, f32[2,48,128]{2,1,0:T(8,128)S(1)}, u32[]{:S(2)}, u32[]{:S(2)}) collective-permute-start(f32[2,48,128]{2,1,0:T(8,128)S(1)} %slice.85), channel_id=1, source_target_pairs={{0,2},{1,3},{2,0},{3,1},{4,6},{5,7},{6,4},{7,5},{8,10},{9,11},{10,... | collective-permute-start | bytes 147464 | tf_op jit(solution)/shard_map/ppermute | solution.py:34
  29.9 6.2 %collective-permute-start.15 = (f32[48,128]{1,0:T(8,128)S(1)}, f32[48,128]{1,0:T(8,128)S(1)}, u32[]{:S(2)}, u32[]{:S(2)}) collective-permute-start(f32[48,128]{1,0:T(8,128)S(1)} %slice_bitcast_fusion.4), channel_id=1, source_target_pairs={{0,24},{1,31},{2,28},{3,27},{4,26},{5,29},{6,30},{7,25},{8,22},{9,... | collective-permute-start | bytes 73736 | tf_op jit(solution)/shard_map/ppermute | solution.py:34
  31.7 5.7 %collective-permute-start.14 = (f32[48,128]{1,0:T(8,128)S(1)}, f32[48,128]{1,0:T(8,128)S(1)}, u32[]{:S(2)}, u32[]{:S(2)}) collective-permute-start(f32[48,128]{1,0:T(8,128)S(1)} %bitcast_select_fusion), channel_id=1, source_target_pairs={{0,10},{1,19},{2,16},{3,9},{4,22},{5,15},{6,12},{7,21},{8,26},{9,3... | collective-permute-start | bytes 73736 | tf_op jit(solution)/shard_map/ppermute | solution.py:34
  34.3 3.3 %collective-permute-start.16 = (f32[48,128]{1,0:T(8,128)S(1)}, f32[48,128]{1,0:T(8,128)S(1)}, u32[]{:S(2)}, u32[]{:S(2)}) collective-permute-start(f32[48,128]{1,0:T(8,128)S(1)} %bitcast_select_fusion), channel_id=1, source_target_pairs={{0,12},{1,21},{2,22},{3,15},{4,16},{5,9},{6,10},{7,19},{8,28},{9,5... | collective-permute-start | bytes 73736 | tf_op jit(solution)/shard_map/ppermute | solution.py:34
  37.7 1.3 %collective-permute-start.17 = (f32[3,48,128]{2,1,0:T(8,128)S(1)}, f32[3,48,128]{2,1,0:T(8,128)S(1)}, u32[]{:S(2)}, u32[]{:S(2)}) collective-permute-start(f32[3,48,128]{2,1,0:T(8,128)S(1)} %pad_maximum_fusion.2), channel_id=1, source_target_pairs={{0,4},{1,5},{2,6},{3,7},{4,0},{5,1},{6,2},{7,3},{8,12},{9,13},{10,... | collective-permute-start | bytes 221192 | tf_op jit(solution)/shard_map/ppermute | solution.py:34

commit v4 on v3

--- a/solution.py
+++ b/solution.py
@@ -63,21 +63,22 @@
     core = both(1, 0)
     top = top + swap(top, core)
     next_low = swap(jnp.stack([low[0], low[2]]), both(0, 1))
-    top = top + swap(top, both(1, 1))
+    top_got = swap(top, both(1, 1))
+    top = top + top_got
+    near, *others = near_of()
     top, next_low = lax.optimization_barrier((top, next_low))
-    near, *others = near_of()
     own = jnp.where(first, top[0], top[1])
     far_low = swap(low[1:], both(0, 2))
     last_low = swap(low[1:], both(0, 3))
+    corner = swap(top[1], ((6, 0), (7, 2)))
     far = swap(own, ((2, 2), (4, 2)))
-    corner = swap(top[1], ((6, 0), (7, 2)))
-    own, far_low = lax.optimization_barrier((own, far_low))
+    own, last_low = lax.optimization_barrier((own, last_low))
     beside = swap(own, ((3, 0), (5, 0)))
     far_low, last_low, far, corner, beside = lax.optimization_barrier((far_low, last_low, far, corner, beside))
     both_low = far_low + last_low
     near = apply(1, near, jnp.stack([next_low[0], both_low[0]]))
+    third = low[2] + next_low[1] + both_low[1]
     mine = beside + far
-    third = low[2] + next_low[1] + both_low[1]
     third, other, corner_other = swap(jnp.stack([third, mine, corner]), core)
     fourth = jnp.where(first, mine, other)
     fifth = jnp.where(first, other, mine) + (corner + corner_other)

time: 40.5 us -> 39.6 us (0.978)
  starting transfers between devices: 23.4 us -> 22.9 us
  waiting for transfers between devices: 6.44 us -> 6.01 us
    ppermute x18, starting transfers between devices: 23.4 us -> 22.9 us  [swap(): return lax.ppermute(block, AXES, route)]
    ppermute x18, waiting for transfers between devices: 6.44 us -> 6.01 us  [swap(): return lax.ppermute(block, AXES, route)]
  transfers between devices with their start and end apart: 18 -> 18, of which waited for: 10 -> 9; matrix products, arithmetic and copies ran while one was open for 0% -> 0% of each run, Pallas kernels for 12% -> 12%
where the time goes in v4:
time: 39.6 us; the launch traced here: 39.4 us
  starting transfers between devices  22.9 us (58%)
  Pallas kernels  9.45 us (24%)
  waiting for transfers between devices  6.01 us (15%)
  between operations  0.89 us (2%)
    ppermute x18, starting transfers between devices, swap(): return lax.ppermute(block, AXES, route)  22.9 us
    pallas_call x7, Pallas kernels, run(): pl.pallas_call(kernel, out_shape=[VMEM(shape, F32) if inside else jax.Sha...  6.28 us
    ppermute x18, waiting for transfers between devices, swap(): return lax.ppermute(block, AXES, route)  6.01 us
    pallas_call x1, Pallas kernels, per_device(): pl.pallas_call(first_top_kernel, out_shape=[VMEM(top_out[0], F32), VMEM(s...  1.88 us
    pallas_call x1, Pallas kernels, per_device(): pl.pallas_call(functools.partial(last_kernel, start), out_shape=jax.Shape...  1.3 us
  transfers between devices with their start and end apart: 18, of which 9 were waited for; matrix products, arithmetic and copies ran while one was open for 0% of the time, Pallas kernels for 12%

profile of v4, /device:TPU:0, one launch (start us, length us, event | category | flops | bytes accessed | tf_op | source)
XLA Modules:
  0.0 39.4 jit_solution(3416720386045997301)
XLA Ops:
  0.7 1.9 %shard_map.77 = (f32[2,48,128]{2,1,0:T(8,128)S(1)}, f32[64,1024]{1,0:T(8,128)S(1)}, f32[6,96,1024]{2,1,0:T(8,128)S(1)}) custom-call(f32[64,1024]{1,0:T(8,128)} %field_hbm, f32[6,96,1024]{2,1,0:T(8,128)} %row_hbm.1), custom_call_target="tpu_custom_call" | custom-call | tf_op jit(solution)/shard_map/pallas_call | solution.py:237
  2.6 0.5 %collective-permute-start = (f32[2,48,128]{2,1,0:T(8,128)S(1)}, f32[2,48,128]{2,1,0:T(8,128)S(1)}, u32[]{:S(2)}, u32[]{:S(2)}) collective-permute-start(f32[2,48,128]{2,1,0:T(8,128)S(1)} %get-tuple-element.32), channel_id=1, source_target_pairs={{0,4},{1,5},{2,6},{3,7},{4,0},{5,1},{6,2},{7,3},{8,12},{9,13},{10,... | collective-permute-start | bytes 147464 | tf_op jit(solution)/shard_map/ppermute | solution.py:34
  3.1 0.7 %shard_map.79 = f32[3,48,128]{2,1,0:T(8,128)S(1)} custom-call(f32[64,1024]{1,0:T(8,128)S(1)} %get-tuple-element.30.field, f32[6,96,1024]{2,1,0:T(8,128)S(1)} %get-tuple-element.31.row_basis), custom_call_target="tpu_custom_call" | custom-call | tf_op jit(solution)/shard_map/pallas_call | solution.py:217
  3.8 0.2 collective-permute-done
  4.0 2.7 %collective-permute-start.1 = (f32[2,48,128]{2,1,0:T(8,128)S(1)}, f32[2,48,128]{2,1,0:T(8,128)S(1)}, u32[]{:S(2)}, u32[]{:S(2)}) collective-permute-start(f32[2,48,128]{2,1,0:T(8,128)S(1)} %add.52), channel_id=1, source_target_pairs={{0,5},{1,4},{2,7},{3,6},{4,1},{5,0},{6,3},{7,2},{8,13},{9,12},{10,... | collective-permute-start | bytes 147464 | tf_op jit(solution)/shard_map/ppermute | solution.py:34
  6.7 0.4 collective-permute-start.2
  7.0 3.7 %collective-permute-start.4 = (f32[2,48,128]{2,1,0:T(8,128)S(1)}, f32[2,48,128]{2,1,0:T(8,128)S(1)}, u32[]{:S(2)}, u32[]{:S(2)}) collective-permute-start(f32[2,48,128]{2,1,0:T(8,128)S(1)} %slice.80), channel_id=1, source_target_pairs={{0,3},{1,2},{2,1},{3,0},{4,7},{5,6},{6,5},{7,4},{8,11},{9,10},{10,... | collective-permute-start | bytes 147464 | tf_op jit(solution)/shard_map/ppermute | solution.py:34
  10.8 2.5 %collective-permute-start.6 = (f32[48,128]{1,0:T(8,128)S(1)}, f32[48,128]{1,0:T(8,128)S(1)}, u32[]{:S(2)}, u32[]{:S(2)}) collective-permute-start(f32[48,128]{1,0:T(8,128)S(1)} %slice_bitcast_fusion.5), channel_id=1, source_target_pairs={{0,24},{1,31},{2,28},{3,27},{4,26},{5,29},{6,30},{7,25},{8,22},{9,... | collective-permute-start | bytes 73736 | tf_op jit(solution)/shard_map/ppermute | solution.py:34
  13.3 3.0 %collective-permute-start.5 = (f32[48,128]{1,0:T(8,128)S(1)}, f32[48,128]{1,0:T(8,128)S(1)}, u32[]{:S(2)}, u32[]{:S(2)}) collective-permute-start(f32[48,128]{1,0:T(8,128)S(1)} %bitcast_select_fusion.1), channel_id=1, source_target_pairs={{0,10},{1,19},{2,16},{3,9},{4,22},{5,15},{6,12},{7,21},{8,26},{9,3... | collective-permute-start | bytes 73736 | tf_op jit(solution)/shard_map/ppermute | solution.py:34
  16.3 0.9 %shard_map.78.near = f32[64,1024]{1,0:T(8,128)S(1)} custom-call(f32[64,1024]{1,0:T(8,128)S(1)} %get-tuple-element.30.field, f32[64,1024]{1,0:T(8,128)S(1)} %copy-done.3, f32[512,1024]{1,0:T(8,128)S(1)} %copy-done.1, f32[6,96,1024]{2,1,0:T(8,128)S(1)} %copy-done, f32[6,96,1024]{2,1,0:T(8,128)S(1)} %get-tuple-element.31.row_basis), custom_call_target="tpu_custom_call" | custom-call | tf_op jit(solution)/shard_map/pallas_call | solution.py:217
  17.3 1.6 %collective-permute-done.5 = f32[48,128]{1,0:T(8,128)S(1)} collective-permute-done((f32[48,128]{1,0:T(8,128)S(1)}, f32[48,128]{1,0:T(8,128)S(1)}, u32[]{:S(2)}, u32[]{:S(2)}) %collective-permute-start.5) | collective-permute-done | bytes 24608 | tf_op jit(solution)/shard_map/ppermute | solution.py:34
  18.9 0.6 %collective-permute-done.7 = f32[48,128]{1,0:T(8,128)S(1)} collective-permute-done((f32[48,128]{1,0:T(8,128)S(1)}, f32[48,128]{1,0:T(8,128)S(1)}, u32[]{:S(2)}, u32[]{:S(2)}) %collective-permute-start.7) | collective-permute-done | bytes 24608 | tf_op jit(solution)/shard_map/ppermute | solution.py:34
  19.6 0.9 %collective-permute-start.8 = (f32[3,48,128]{2,1,0:T(8,128)S(1)}, f32[3,48,128]{2,1,0:T(8,128)S(1)}, u32[]{:S(2)}, u32[]{:S(2)}) collective-permute-start(f32[3,48,128]{2,1,0:T(8,128)S(1)} %pad_maximum_fusion), channel_id=1, source_target_pairs={{0,4},{1,5},{2,6},{3,7},{4,0},{5,1},{6,2},{7,3},{8,12},{9,13},{10,... | collective-permute-start | bytes 221192 | tf_op jit(solution)/shard_map/ppermute | solution.py:34
  20.5 0.5 %shard_map.80.near = f32[64,1024]{1,0:T(8,128)S(1)} custom-call(f32[64,1024]{1,0:T(8,128)S(1)} %shard_map.78.near, f32[2,48,128]{2,1,0:T(8,128)S(1)} %pad_maximum_fusion.5.coefs, f32[6,96,1024]{2,1,0:T(8,128)S(1)} %copy-done), custom_call_target="tpu_custom_call" | custom-call | tf_op jit(solution)/shard_map/pallas_call | solution.py:217
  21.0 0.4 %collective-permute-done.8 = f32[3,48,128]{2,1,0:T(8,128)S(1)} collective-permute-done((f32[3,48,128]{2,1,0:T(8,128)S(1)}, f32[3,48,128]{2,1,0:T(8,128)S(1)}, u32[]{:S(2)}, u32[]{:S(2)}) %collective-permute-start.8) | collective-permute-done | bytes 73760 | tf_op jit(solution)/shard_map/ppermute | solution.py:34
  21.4 1.5 %shard_map.81 = (f32[64,1024]{1,0:T(8,128)S(1)}, f32[2,48,128]{2,1,0:T(8,128)S(1)}) custom-call(f32[64,1024]{1,0:T(8,128)S(1)} %shard_map.80.near, f32[3,48,128]{2,1,0:T(8,128)S(1)} %pad_maximum_fusion.1.coefs, f32[64,1024]{1,0:T(8,128)S(1)} %get-tuple-element.30.field, f32[6,96,1024]{2,1,0:T(8,128)S(1)} %copy-done, f32[512,1024]{1,0:T(8,128)S(1)} %copy-done.2, ...), custom_call_target="tpu_custom_call" | custom-call | tf_op jit(solution)/shard_map/pallas_call | solution.py:217
  23.0 0.4 %collective-permute-start.9 = (f32[2,48,128]{2,1,0:T(8,128)S(1)}, f32[2,48,128]{2,1,0:T(8,128)S(1)}, u32[]{:S(2)}, u32[]{:S(2)}) collective-permute-start(f32[2,48,128]{2,1,0:T(8,128)S(1)} %get-tuple-element.46), channel_id=1, source_target_pairs={{0,4},{1,5},{2,6},{3,7},{4,0},{5,1},{6,2},{7,3},{8,12},{9,13},{10,... | collective-permute-start | bytes 147464 | tf_op jit(solution)/shard_map/ppermute | solution.py:34
  23.4 0.7 %shard_map.83 = f32[3,48,128]{2,1,0:T(8,128)S(1)} custom-call(f32[64,1024]{1,0:T(8,128)S(1)} %get-tuple-element.43.field, f32[6,96,1024]{2,1,0:T(8,128)S(1)} %get-tuple-element.31.row_basis), custom_call_target="tpu_custom_call" | custom-call | tf_op jit(solution)/shard_map/pallas_call | solution.py:217
  24.3 1.5 %collective-permute-start.10 = (f32[2,48,128]{2,1,0:T(8,128)S(1)}, f32[2,48,128]{2,1,0:T(8,128)S(1)}, u32[]{:S(2)}, u32[]{:S(2)}) collective-permute-start(f32[2,48,128]{2,1,0:T(8,128)S(1)} %add.60), channel_id=1, source_target_pairs={{0,5},{1,4},{2,7},{3,6},{4,1},{5,0},{6,3},{7,2},{8,13},{9,12},{10,... | collective-permute-start | bytes 147464 | tf_op jit(solution)/shard_map/ppermute | solution.py:34
  25.8 0.6 %collective-permute-start.11 = (f32[2,48,128]{2,1,0:T(8,128)S(1)}, f32[2,48,128]{2,1,0:T(8,128)S(1)}, u32[]{:S(2)}, u32[]{:S(2)}) collective-permute-start(f32[2,48,128]{2,1,0:T(8,128)S(1)} %pad_maximum_fusion.6), channel_id=1, source_target_pairs={{0,1},{1,0},{2,3},{3,2},{4,5},{5,4},{6,7},{7,6},{8,9},{9,8},{10,11... | collective-permute-start | bytes 147464 | tf_op jit(solution)/shard_map/ppermute | solution.py:34
  26.3 2.0 %collective-permute-start.13 = (f32[2,48,128]{2,1,0:T(8,128)S(1)}, f32[2,48,128]{2,1,0:T(8,128)S(1)}, u32[]{:S(2)}, u32[]{:S(2)}) collective-permute-start(f32[2,48,128]{2,1,0:T(8,128)S(1)} %slice.85), channel_id=1, source_target_pairs={{0,3},{1,2},{2,1},{3,0},{4,7},{5,6},{6,5},{7,4},{8,11},{9,10},{10,... | collective-permute-start | bytes 147464 | tf_op jit(solution)/shard_map/ppermute | solution.py:34
  28.4 0.9 %collective-permute-start.12 = (f32[2,48,128]{2,1,0:T(8,128)S(1)}, f32[2,48,128]{2,1,0:T(8,128)S(1)}, u32[]{:S(2)}, u32[]{:S(2)}) collective-permute-start(f32[2,48,128]{2,1,0:T(8,128)S(1)} %slice.85), channel_id=1, source_target_pairs={{0,2},{1,3},{2,0},{3,1},{4,6},{5,7},{6,4},{7,5},{8,10},{9,11},{10,... | collective-permute-start | bytes 147464 | tf_op jit(solution)/shard_map/ppermute | solution.py:34
  29.3 0.6 %collective-permute-done.11 = f32[2,48,128]{2,1,0:T(8,128)S(1)} collective-permute-done((f32[2,48,128]{2,1,0:T(8,128)S(1)}, f32[2,48,128]{2,1,0:T(8,128)S(1)}, u32[]{:S(2)}, u32[]{:S(2)}) %collective-permute-start.11) | collective-permute-done | bytes 49184 | tf_op jit(solution)/shard_map/ppermute | solution.py:34
  29.9 0.6 %collective-permute-start.15 = (f32[48,128]{1,0:T(8,128)S(1)}, f32[48,128]{1,0:T(8,128)S(1)}, u32[]{:S(2)}, u32[]{:S(2)}) collective-permute-start(f32[48,128]{1,0:T(8,128)S(1)} %slice_bitcast_fusion.4), channel_id=1, source_target_pairs={{0,24},{1,31},{2,28},{3,27},{4,26},{5,29},{6,30},{7,25},{8,22},{9,... | collective-permute-start | bytes 73736 | tf_op jit(solution)/shard_map/ppermute | solution.py:34
  30.5 2.9 %collective-permute-start.14 = (f32[48,128]{1,0:T(8,128)S(1)}, f32[48,128]{1,0:T(8,128)S(1)}, u32[]{:S(2)}, u32[]{:S(2)}) collective-permute-start(f32[48,128]{1,0:T(8,128)S(1)} %bitcast_select_fusion), channel_id=1, source_target_pairs={{0,10},{1,19},{2,16},{3,9},{4,22},{5,15},{6,12},{7,21},{8,26},{9,3... | collective-permute-start | bytes 73736 | tf_op jit(solution)/shard_map/ppermute | solution.py:34
  33.4 1.5 %shard_map.82 = (f32[64,1024]{1,0:T(8,128)S(1)}, f32[64,1024]{1,0:T(8,128)}) custom-call(f32[64,1024]{1,0:T(8,128)S(1)} %get-tuple-element.43.field, f32[64,1024]{1,0:T(8,128)S(1)} %copy-done.3, f32[512,1024]{1,0:T(8,128)S(1)} %copy-done.1, f32[6,96,1024]{2,1,0:T(8,128)S(1)} %copy-done, f32[6,96,1024]{2,1,0:T(8,128)S(1)} %get-tuple-element.31.row_basis), custom_call_target="tpu_custom_call" | custom-call | tf_op jit(solution)/shard_map/pallas_call | solution.py:217
  35.0 1.2 %collective-permute-done.14 = f32[48,128]{1,0:T(8,128)S(1)} collective-permute-done((f32[48,128]{1,0:T(8,128)S(1)}, f32[48,128]{1,0:T(8,128)S(1)}, u32[]{:S(2)}, u32[]{:S(2)}) %collective-permute-start.14) | collective-permute-done | bytes 24608 | tf_op jit(solution)/shard_map/ppermute | solution.py:34
  36.1 0.6 %collective-permute-done.16 = f32[48,128]{1,0:T(8,128)S(1)} collective-permute-done((f32[48,128]{1,0:T(8,128)S(1)}, f32[48,128]{1,0:T(8,128)S(1)}, u32[]{:S(2)}, u32[]{:S(2)}) %collective-permute-start.16) | collective-permute-done | bytes 24608 | tf_op jit(solution)/shard_map/ppermute | solution.py:34
  36.7 0.2 collective-permute-start.17
  37.0 0.5 %shard_map.84.near = f32[64,1024]{1,0:T(8,128)S(1)} custom-call(f32[64,1024]{1,0:T(8,128)S(1)} %get-tuple-element.45.near, f32[2,48,128]{2,1,0:T(8,128)S(1)} %pad_maximum_fusion.7.coefs, f32[6,96,1024]{2,1,0:T(8,128)S(1)} %copy-done), custom_call_target="tpu_custom_call" | custom-call | tf_op jit(solution)/shard_map/pallas_call | solution.py:217
  37.5 0.6 %collective-permute-done.17 = f32[3,48,128]{2,1,0:T(8,128)S(1)} collective-permute-done((f32[3,48,128]{2,1,0:T(8,128)S(1)}, f32[3,48,128]{2,1,0:T(8,128)S(1)}, u32[]{:S(2)}, u32[]{:S(2)}) %collective-permute-start.17) | collective-permute-done | bytes 73760 | tf_op jit(solution)/shard_map/ppermute | solution.py:34
  38.1 1.3 %shard_map.85 = f32[64,1024]{1,0:T(8,128)} custom-call(f32[64,1024]{1,0:T(8,128)S(1)} %shard_map.84.near, f32[3,48,128]{2,1,0:T(8,128)S(1)} %pad_maximum_fusion.3.coefs, f32[6,96,1024]{2,1,0:T(8,128)S(1)} %copy-done), custom_call_target="tpu_custom_call" | custom-call | tf_op jit(solution)/shard_map/pallas_call | solution.py:270
  (51 shorter events, 0.4 us)
Async XLA Ops:
  0.6 15.7 %copy-start.1 = (f32[512,1024]{1,0:T(8,128)S(1)}, f32[512,1024]{1,0:T(8,128)}, u32[]{:S(2)}) copy-start(f32[512,1024]{1,0:T(8,128)} %leaf_blocks.3) | copy-start | bytes 6291460
  2.5 13.8 %copy-start = (f32[6,96,1024]{2,1,0:T(8,128)S(1)}, f32[6,96,1024]{2,1,0:T(8,128)}, u32[]{:S(2)}) copy-start(f32[6,96,1024]{2,1,0:T(8,128)} %col_basis.11) | copy-start | bytes 7077892
  2.5 13.8 %copy-start.3 = (f32[64,1024]{1,0:T(8,128)S(1)}, f32[64,1024]{1,0:T(8,128)}, u32[]{:S(2)}) copy-start(f32[64,1024]{1,0:T(8,128)} %incident.3) | copy-start | bytes 786436
  2.6 1.4 %collective-permute-start = (f32[2,48,128]{2,1,0:T(8,128)S(1)}, f32[2,48,128]{2,1,0:T(8,128)S(1)}, u32[]{:S(2)}, u32[]{:S(2)}) collective-permute-start(f32[2,48,128]{2,1,0:T(8,128)S(1)} %get-tuple-element.32), channel_id=1, source_target_pairs={{0,4},{1,5},{2,6},{3,7},{4,0},{5,1},{6,2},{7,3},{8,12},{9,13},{10,... | collective-permute-start | bytes 147464 | tf_op jit(solution)/shard_map/ppermute | solution.py:34
  4.0 6.8 %collective-permute-start.1 = (f32[2,48,128]{2,1,0:T(8,128)S(1)}, f32[2,48,128]{2,1,0:T(8,128)S(1)}, u32[]{:S(2)}, u32[]{:S(2)}) collective-permute-start(f32[2,48,128]{2,1,0:T(8,128)S(1)} %add.52), channel_id=1, source_target_pairs={{0,5},{1,4},{2,7},{3,6},{4,1},{5,0},{6,3},{7,2},{8,13},{9,12},{10,... | collective-permute-start | bytes 147464 | tf_op jit(solution)/shard_map/ppermute | solution.py:34
  6.7 4.1 %collective-permute-start.2 = (f32[2,48,128]{2,1,0:T(8,128)S(1)}, f32[2,48,128]{2,1,0:T(8,128)S(1)}, u32[]{:S(2)}, u32[]{:S(2)}) collective-permute-start(f32[2,48,128]{2,1,0:T(8,128)S(1)} %pad_maximum_fusion.4), channel_id=1, source_target_pairs={{0,1},{1,0},{2,3},{3,2},{4,5},{5,4},{6,7},{7,6},{8,9},{9,8},{10,11... | collective-permute-start | bytes 147464 | tf_op jit(solution)/shard_map/ppermute | solution.py:34
  7.0 9.2 %collective-permute-start.4 = (f32[2,48,128]{2,1,0:T(8,128)S(1)}, f32[2,48,128]{2,1,0:T(8,128)S(1)}, u32[]{:S(2)}, u32[]{:S(2)}) collective-permute-start(f32[2,48,128]{2,1,0:T(8,128)S(1)} %slice.80), channel_id=1, source_target_pairs={{0,3},{1,2},{2,1},{3,0},{4,7},{5,6},{6,5},{7,4},{8,11},{9,10},{10,... | collective-permute-start | bytes 147464 | tf_op jit(solution)/shard_map/ppermute | solution.py:34
  10.7 6.5 %collective-permute-start.3 = (f32[2,48,128]{2,1,0:T(8,128)S(1)}, f32[2,48,128]{2,1,0:T(8,128)S(1)}, u32[]{:S(2)}, u32[]{:S(2)}) collective-permute-start(f32[2,48,128]{2,1,0:T(8,128)S(1)} %slice.80), channel_id=1, source_target_pairs={{0,2},{1,3},{2,0},{3,1},{4,6},{5,7},{6,4},{7,5},{8,10},{9,11},{10,... | collective-permute-start | bytes 147464 | tf_op jit(solution)/shard_map/ppermute | solution.py:34
  10.8 6.5 %collective-permute-start.6 = (f32[48,128]{1,0:T(8,128)S(1)}, f32[48,128]{1,0:T(8,128)S(1)}, u32[]{:S(2)}, u32[]{:S(2)}) collective-permute-start(f32[48,128]{1,0:T(8,128)S(1)} %slice_bitcast_fusion.5), channel_id=1, source_target_pairs={{0,24},{1,31},{2,28},{3,27},{4,26},{5,29},{6,30},{7,25},{8,22},{9,... | collective-permute-start | bytes 73736 | tf_op jit(solution)/shard_map/ppermute | solution.py:34
  13.3 5.6 %collective-permute-start.5 = (f32[48,128]{1,0:T(8,128)S(1)}, f32[48,128]{1,0:T(8,128)S(1)}, u32[]{:S(2)}, u32[]{:S(2)}) collective-permute-start(f32[48,128]{1,0:T(8,128)S(1)} %bitcast_select_fusion.1), channel_id=1, source_target_pairs={{0,10},{1,19},{2,16},{3,9},{4,22},{5,15},{6,12},{7,21},{8,26},{9,3... | collective-permute-start | bytes 73736 | tf_op jit(solution)/shard_map/ppermute | solution.py:34
  16.3 3.3 %collective-permute-start.7 = (f32[48,128]{1,0:T(8,128)S(1)}, f32[48,128]{1,0:T(8,128)S(1)}, u32[]{:S(2)}, u32[]{:S(2)}) collective-permute-start(f32[48,128]{1,0:T(8,128)S(1)} %bitcast_select_fusion.1), channel_id=1, source_target_pairs={{0,12},{1,21},{2,22},{3,15},{4,16},{5,9},{6,10},{7,19},{8,28},{9,5... | collective-permute-start | bytes 73736 | tf_op jit(solution)/shard_map/ppermute | solution.py:34
  17.2 4.2 %copy-start.2 = (f32[512,1024]{1,0:T(8,128)S(1)}, f32[512,1024]{1,0:T(8,128)}, u32[]{:S(2)}) copy-start(f32[512,1024]{1,0:T(8,128)} %leaf_inverse.1) | copy-start | bytes 6291460
  19.6 1.8 %collective-permute-start.8 = (f32[3,48,128]{2,1,0:T(8,128)S(1)}, f32[3,48,128]{2,1,0:T(8,128)S(1)}, u32[]{:S(2)}, u32[]{:S(2)}) collective-permute-start(f32[3,48,128]{2,1,0:T(8,128)S(1)} %pad_maximum_fusion), channel_id=1, source_target_pairs={{0,4},{1,5},{2,6},{3,7},{4,0},{5,1},{6,2},{7,3},{8,12},{9,13},{10,... | collective-permute-start | bytes 221192 | tf_op jit(solution)/shard_map/ppermute | solution.py:34
  23.0 1.3 %collective-permute-start.9 = (f32[2,48,128]{2,1,0:T(8,128)S(1)}, f32[2,48,128]{2,1,0:T(8,128)S(1)}, u32[]{:S(2)}, u32[]{:S(2)}) collective-permute-start(f32[2,48,128]{2,1,0:T(8,128)S(1)} %get-tuple-element.46), channel_id=1, source_target_pairs={{0,4},{1,5},{2,6},{3,7},{4,0},{5,1},{6,2},{7,3},{8,12},{9,13},{10,... | collective-permute-start | bytes 147464 | tf_op jit(solution)/shard_map/ppermute | solution.py:34
  24.3 5.0 %collective-permute-start.10 = (f32[2,48,128]{2,1,0:T(8,128)S(1)}, f32[2,48,128]{2,1,0:T(8,128)S(1)}, u32[]{:S(2)}, u32[]{:S(2)}) collective-permute-start(f32[2,48,128]{2,1,0:T(8,128)S(1)} %add.60), channel_id=1, source_target_pairs={{0,5},{1,4},{2,7},{3,6},{4,1},{5,0},{6,3},{7,2},{8,13},{9,12},{10,... | collective-permute-start | bytes 147464 | tf_op jit(solution)/shard_map/ppermute | solution.py:34
  25.8 4.1 %collective-permute-start.11 = (f32[2,48,128]{2,1,0:T(8,128)S(1)}, f32[2,48,128]{2,1,0:T(8,128)S(1)}, u32[]{:S(2)}, u32[]{:S(2)}) collective-permute-start(f32[2,48,128]{2,1,0:T(8,128)S(1)} %pad_maximum_fusion.6), channel_id=1, source_target_pairs={{0,1},{1,0},{2,3},{3,2},{4,5},{5,4},{6,7},{7,6},{8,9},{9,8},{10,11... | collective-permute-start | bytes 147464 | tf_op jit(solution)/shard_map/ppermute | solution.py:34
  26.3 7.1 %collective-permute-start.13 = (f32[2,48,128]{2,1,0:T(8,128)S(1)}, f32[2,48,128]{2,1,0:T(8,128)S(1)}, u32[]{:S(2)}, u32[]{:S(2)}) collective-permute-start(f32[2,48,128]{2,1,0:T(8,128)S(1)} %slice.85), channel_id=1, source_target_pairs={{0,3},{1,2},{2,1},{3,0},{4,7},{5,6},{6,5},{7,4},{8,11},{9,10},{10,... | collective-permute-start | bytes 147464 | tf_op jit(solution)/shard_map/ppermute | solution.py:34
  28.4 6.6 %collective-permute-start.12 = (f32[2,48,128]{2,1,0:T(8,128)S(1)}, f32[2,48,128]{2,1,0:T(8,128)S(1)}, u32[]{:S(2)}, u32[]{:S(2)}) collective-permute-start(f32[2,48,128]{2,1,0:T(8,128)S(1)} %slice.85), channel_id=1, source_target_pairs={{0,2},{1,3},{2,0},{3,1},{4,6},{5,7},{6,4},{7,5},{8,10},{9,11},{10,... | collective-permute-start | bytes 147464 | tf_op jit(solution)/shard_map/ppermute | solution.py:34
  29.9 5.1 %collective-permute-start.15 = (f32[48,128]{1,0:T(8,128)S(1)}, f32[48,128]{1,0:T(8,128)S(1)}, u32[]{:S(2)}, u32[]{:S(2)}) collective-permute-start(f32[48,128]{1,0:T(8,128)S(1)} %slice_bitcast_fusion.4), channel_id=1, source_target_pairs={{0,24},{1,31},{2,28},{3,27},{4,26},{5,29},{6,30},{7,25},{8,22},{9,... | collective-permute-start | bytes 73736 | tf_op jit(solution)/shard_map/ppermute | solution.py:34
  30.5 5.6 %collective-permute-start.14 = (f32[48,128]{1,0:T(8,128)S(1)}, f32[48,128]{1,0:T(8,128)S(1)}, u32[]{:S(2)}, u32[]{:S(2)}) collective-permute-start(f32[48,128]{1,0:T(8,128)S(1)} %bitcast_select_fusion), channel_id=1, source_target_pairs={{0,10},{1,19},{2,16},{3,9},{4,22},{5,15},{6,12},{7,21},{8,26},{9,3... | collective-permute-start | bytes 73736 | tf_op jit(solution)/shard_map/ppermute | solution.py:34
  33.4 3.3 %collective-permute-start.16 = (f32[48,128]{1,0:T(8,128)S(1)}, f32[48,128]{1,0:T(8,128)S(1)}, u32[]{:S(2)}, u32[]{:S(2)}) collective-permute-start(f32[48,128]{1,0:T(8,128)S(1)} %bitcast_select_fusion), channel_id=1, source_target_pairs={{0,12},{1,21},{2,22},{3,15},{4,16},{5,9},{6,10},{7,19},{8,28},{9,5... | collective-permute-start | bytes 73736 | tf_op jit(solution)/shard_map/ppermute | solution.py:34
  36.7 1.3 %collective-permute-start.17 = (f32[3,48,128]{2,1,0:T(8,128)S(1)}, f32[3,48,128]{2,1,0:T(8,128)S(1)}, u32[]{:S(2)}, u32[]{:S(2)}) collective-permute-start(f32[3,48,128]{2,1,0:T(8,128)S(1)} %pad_maximum_fusion.2), channel_id=1, source_target_pairs={{0,4},{1,5},{2,6},{3,7},{4,0},{5,1},{6,2},{7,3},{8,12},{9,13},{10,... | collective-permute-start | bytes 221192 | tf_op jit(solution)/shard_map/ppermute | solution.py:34

commit v5 on v4

--- a/solution.py
+++ b/solution.py
@@ -48,7 +48,7 @@
         gathered.append(received[0])
         pending = (pending + received)[1:]
     near, *others = near_of()
-    near = apply(1, near, jnp.stack(gathered[:-TOP]))
+    near = apply(1, near, jnp.stack(gathered[:-TOP]), *others)
     return near, 1 + len(gathered) - TOP, jnp.stack(gathered[-TOP:]), others
 
 
@@ -76,7 +76,7 @@
     beside = swap(own, ((3, 0), (5, 0)))
     far_low, last_low, far, corner, beside = lax.optimization_barrier((far_low, last_low, far, corner, beside))
     both_low = far_low + last_low
-    near = apply(1, near, jnp.stack([next_low[0], both_low[0]]))
+    near = apply(1, near, jnp.stack([next_low[0], both_low[0]]), *others)
     third = low[2] + next_low[1] + both_low[1]
     mine = beside + far
     third, other, corner_other = swap(jnp.stack([third, mine, corner]), core)
@@ -85,8 +85,12 @@
     return near, 3, jnp.stack([third, fourth, fifth]), others
 
 
+def goes_in_lanes():
+    return bits_of("grp") == 2 and bits_of("wide") == 3
+
+
 def exchange(first, low, top, near_of, apply):
-    if bits_of("grp") == 2 and bits_of("wide") == 3:
+    if goes_in_lanes():
         return in_lanes(first, low, top, near_of, apply)
     return climb_tree(low, top, near_of, apply)
 
@@ -97,9 +101,12 @@
 
 
 def dot(x, table, dims):
+    return dot_split(x, *split(table), dims)
+
+
+def dot_split(x, t_high, t_low, dims):
     count = x.shape[0]
     x_high, x_low = split(x)
-    t_high, t_low = split(table)
     main = lax.dot_general(jnp.concatenate([x_high, x_low]), t_high, dims, preferred_element_type=F32)
     rest = lax.dot_general(x_high, t_low, dims, preferred_element_type=F32)
     return main[:count] + (main[count:] + rest)
@@ -189,13 +196,44 @@
     out[...] = near[...] - dot(side_by_side(coefs, near.shape[0]), table, PLAIN)
 
 
-def refine_kernel(start, near, coefs, field, col_basis, leaf_inverse, row_basis, refined, top):
-    levels = col_basis.shape[0]
-    table = merged(col_basis[start:])
+def near_and_tables_kernel(
+    start,
+    field,
+    incident,
+    leaf_blocks,
+    col_basis,
+    row_basis,
+    inverse_hbm,
+    near,
+    leaf_inverse,
+    mixed_high,
+    mixed_low,
+    top_high,
+    top_low,
+    sem,
+):
+    copy = pltpu.make_async_copy(inverse_hbm, leaf_inverse, sem)
+    copy.start()
+    near_kernel(field, incident, leaf_blocks, col_basis, row_basis, near)
+    copy.wait()
+    for s in leaf_slices(leaf_inverse):
+        mixed = dot(merged(col_basis[start:, :, s]), leaf_inverse[:, s], PLAIN)
+        mixed_high[:, s], mixed_low[:, s] = split(mixed)
+    top_high[...], top_low[...] = split(merged(row_basis[row_basis.shape[0] - TOP :]))
+
+
+def apply_and_base_kernel(start, near, coefs, col_basis, field, leaf_inverse, base):
+    table = merged(col_basis[start : start + coefs.shape[0]])
     first = near[...] - dot(side_by_side(coefs, near.shape[0]), table, PLAIN)
     for s in leaf_slices(leaf_inverse):
-        refined[:, s] = field[:, s] + dot(first[:, s], leaf_inverse[:, s], PLAIN)
-    store_levels(top, dot(refined[...], merged(row_basis[levels - TOP :]), ROWS_OF_BOTH))
+        base[:, s] = field[:, s] + dot(first[:, s], leaf_inverse[:, s], PLAIN)
+
+
+def refine_kernel(base, coefs, mixed_high, mixed_low, top_high, top_low, refined, top):
+    refined[...] = base[...] - dot_split(
+        side_by_side(coefs, base.shape[0]), mixed_high[...], mixed_low[...], PLAIN
+    )
+    store_levels(top, dot_split(refined[...], top_high[...], top_low[...], ROWS_OF_BOTH))
 
 
 def last_kernel(start, near, coefs, col_basis, out_hbm, out, sems):
@@ -216,7 +254,7 @@
     whole = pl.BlockSpec(memory_space=VMEM)
     return pl.pallas_call(
         kernel,
-        out_shape=[VMEM(shape, F32) if inside else jax.ShapeDtypeStruct(shape, F32) for shape, inside in outs],
+        out_shape=[VMEM(shape, kind) if inside else jax.ShapeDtypeStruct(shape, kind) for shape, inside, kind in outs],
         in_specs=[whole] * len(args),
         out_specs=[whole] * len(outs),
         compiler_params=pltpu.CompilerParams(vmem_limit_bytes=24 << 20),
@@ -228,9 +266,9 @@
     levels, rank, rows = row_basis.shape
     cols = solution.shape[0]
     dense = (packed_rows(cols, rank), LANES)
-    in_field = ((cols, rows), True)
-    low_out = ((levels - 1 - TOP, *dense), True)
-    top_out = ((TOP, *dense), True)
+    in_field = ((cols, rows), True, F32)
+    low_out = ((levels - 1 - TOP, *dense), True, F32)
+    top_out = ((TOP, *dense), True, F32)
     in_vmem = pl.BlockSpec(memory_space=VMEM)
     in_hbm = pl.BlockSpec(memory_space=pltpu.HBM)
     params = pltpu.CompilerParams(vmem_limit_bytes=24 << 20)
@@ -244,29 +282,37 @@
     )(*[pltpu.with_memory_space_constraint(a, pltpu.HBM) for a in (solution, row_basis)])
     (low,) = run(low_kernel, [low_out], field, row_basis)
 
-    def near_of(field):
-        return run(near_kernel, [in_field], field, incident, leaf_blocks, col_basis, row_basis)
-
-    def near_and_copy(field):
-        outs = [in_field, ((cols, rows), False)]
-        return run(near_and_copy_kernel, outs, field, incident, leaf_blocks, col_basis, row_basis)
-
-    def apply(start, near, coefs):
+    late = 3 if goes_in_lanes() else levels - TOP
+    mixed_out = (((levels - late) * rank, rows), True, jnp.bfloat16)
+    split_out = ((TOP * rank, rows), True, jnp.bfloat16)
+
+    def near_and_tables():
+        outs = [in_field, (leaf_inverse.shape, True, F32), mixed_out, mixed_out, split_out, split_out]
+        in_place = [pltpu.with_memory_space_constraint(a, VMEM) for a in (field, incident, leaf_blocks, col_basis, row_basis)]
+        return pl.pallas_call(
+            functools.partial(near_and_tables_kernel, late),
+            out_shape=[VMEM(shape, kind) for shape, _, kind in outs],
+            in_specs=[in_vmem] * 5 + [in_hbm],
+            out_specs=[in_vmem] * len(outs),
+            scratch_shapes=[pltpu.SemaphoreType.DMA],
+            compiler_params=params,
+        )(*in_place, pltpu.with_memory_space_constraint(leaf_inverse, pltpu.HBM))
+
+    def apply_and_base(start, near, coefs, inverse, *_):
+        kernel = functools.partial(apply_and_base_kernel, start)
+        return run(kernel, [in_field], near, coefs, col_basis, field, inverse)[0]
+
+    def near_and_copy():
+        outs = [in_field, ((cols, rows), False, F32)]
+        return run(near_and_copy_kernel, outs, refined, incident, leaf_blocks, col_basis, row_basis)
+
+    def apply(start, near, coefs, *_):
         return run(functools.partial(apply_kernel, start), [in_field], near, coefs, col_basis)[0]
 
-    near, start, coefs, _ = exchange(first, low, top, functools.partial(near_of, field), apply)
-    refined, top = run(
-        functools.partial(refine_kernel, start),
-        [in_field, top_out],
-        near,
-        coefs,
-        field,
-        col_basis,
-        leaf_inverse,
-        row_basis,
-    )
+    base, start, coefs, tables = exchange(first, low, top, near_and_tables, apply_and_base)
+    refined, top = run(refine_kernel, [in_field, top_out], base, coefs, *tables[1:])
     (low,) = run(low_kernel, [low_out], refined, row_basis)
-    near, start, coefs, others = exchange(first, low, top, functools.partial(near_and_copy, refined), apply)
+    near, start, coefs, others = exchange(first, low, top, near_and_copy, apply)
     residual = pl.pallas_call(
         functools.partial(last_kernel, start),
         out_shape=jax.ShapeDtypeStruct((cols, rows), F32),

time: 39.6 us -> 39.1 us (0.987)
  waiting for transfers between devices: 6.01 us -> 3.59 us
  Pallas kernels: 9.45 us -> 11.2 us
    ppermute x18, waiting for transfers between devices: 6.01 us -> 3.59 us  [swap(): return lax.ppermute(block, AXES, route)]
    pallas_call x7, Pallas kernels: 6.28 us -> 8.01 us  [the longest x6 5.11 us: run(): pl.pallas_call(kernel, out_shape=[VMEM(shape, kind) if inside else jax.Sh...]
  transfers between devices with their start and end apart: 18 -> 18, of which waited for: 9 -> 8; matrix products, arithmetic and copies ran while one was open for 0% -> 0% of each run, Pallas kernels for 12% -> 18%
where the time goes in v5:
time: 39.1 us; the launch traced here: 38.9 us
  starting transfers between devices  23.1 us (59%)
  Pallas kernels  11.2 us (29%)
  waiting for transfers between devices  3.59 us (9%)
  between operations  0.9 us (2%)
    ppermute x18, starting transfers between devices, swap(): return lax.ppermute(block, AXES, route)  23.1 us
    pallas_call x6, Pallas kernels, run(): pl.pallas_call(kernel, out_shape=[VMEM(shape, kind) if inside else jax.Sh...  5.11 us
    ppermute x18, waiting for transfers between devices, swap(): return lax.ppermute(block, AXES, route)  3.59 us
    pallas_call x1, Pallas kernels, near_and_tables(): pl.pallas_call(functools.partial(near_and_tables_kernel, late), out_shape...  2.89 us
    pallas_call x1, Pallas kernels, per_device(): pl.pallas_call(first_top_kernel, out_shape=[VMEM(top_out[0], F32), VMEM(s...  1.88 us
    pallas_call x1, Pallas kernels, per_device(): pl.pallas_call(functools.partial(last_kernel, start), out_shape=jax.Shape...  1.3 us
  transfers between devices with their start and end apart: 18, of which 8 were waited for; matrix products, arithmetic and copies ran while one was open for 0% of the time, Pallas kernels for 18%

profile of v5, /device:TPU:0, one launch (start us, length us, event | category | flops | bytes accessed | tf_op | source)
XLA Modules:
  0.0 38.9 jit_solution(8761670383342573709)
XLA Ops:
  0.7 1.9 %shard_map.77 = (f32[2,48,128]{2,1,0:T(8,128)S(1)}, f32[64,1024]{1,0:T(8,128)S(1)}, f32[6,96,1024]{2,1,0:T(8,128)S(1)}) custom-call(f32[64,1024]{1,0:T(8,128)} %field_hbm, f32[6,96,1024]{2,1,0:T(8,128)} %row_hbm.1), custom_call_target="tpu_custom_call" | custom-call | tf_op jit(solution)/shard_map/pallas_call | solution.py:275
  2.6 0.5 %collective-permute-start = (f32[2,48,128]{2,1,0:T(8,128)S(1)}, f32[2,48,128]{2,1,0:T(8,128)S(1)}, u32[]{:S(2)}, u32[]{:S(2)}) collective-permute-start(f32[2,48,128]{2,1,0:T(8,128)S(1)} %get-tuple-element.39), channel_id=1, source_target_pairs={{0,4},{1,5},{2,6},{3,7},{4,0},{5,1},{6,2},{7,3},{8,12},{9,13},{10,... | collective-permute-start | bytes 147464 | tf_op jit(solution)/shard_map/ppermute | solution.py:34
  3.1 0.7 %shard_map.79 = f32[3,48,128]{2,1,0:T(8,128)S(1)} custom-call(f32[64,1024]{1,0:T(8,128)S(1)} %get-tuple-element.36.field, f32[6,96,1024]{2,1,0:T(8,128)S(1)} %get-tuple-element.37.row_basis), custom_call_target="tpu_custom_call" | custom-call | tf_op jit(solution)/shard_map/pallas_call | solution.py:255
  3.8 0.2 collective-permute-done
  4.0 2.7 %collective-permute-start.1 = (f32[2,48,128]{2,1,0:T(8,128)S(1)}, f32[2,48,128]{2,1,0:T(8,128)S(1)}, u32[]{:S(2)}, u32[]{:S(2)}) collective-permute-start(f32[2,48,128]{2,1,0:T(8,128)S(1)} %add.52), channel_id=1, source_target_pairs={{0,5},{1,4},{2,7},{3,6},{4,1},{5,0},{6,3},{7,2},{8,13},{9,12},{10,... | collective-permute-start | bytes 147464 | tf_op jit(solution)/shard_map/ppermute | solution.py:34
  6.7 0.4 collective-permute-start.2
  7.0 3.7 %collective-permute-start.4 = (f32[2,48,128]{2,1,0:T(8,128)S(1)}, f32[2,48,128]{2,1,0:T(8,128)S(1)}, u32[]{:S(2)}, u32[]{:S(2)}) collective-permute-start(f32[2,48,128]{2,1,0:T(8,128)S(1)} %slice.80), channel_id=1, source_target_pairs={{0,3},{1,2},{2,1},{3,0},{4,7},{5,6},{6,5},{7,4},{8,11},{9,10},{10,... | collective-permute-start | bytes 147464 | tf_op jit(solution)/shard_map/ppermute | solution.py:34
  10.8 2.5 %collective-permute-start.6 = (f32[48,128]{1,0:T(8,128)S(1)}, f32[48,128]{1,0:T(8,128)S(1)}, u32[]{:S(2)}, u32[]{:S(2)}) collective-permute-start(f32[48,128]{1,0:T(8,128)S(1)} %slice_bitcast_fusion.5), channel_id=1, source_target_pairs={{0,24},{1,31},{2,28},{3,27},{4,26},{5,29},{6,30},{7,25},{8,22},{9,... | collective-permute-start | bytes 73736 | tf_op jit(solution)/shard_map/ppermute | solution.py:34
  13.3 3.0 %collective-permute-start.5 = (f32[48,128]{1,0:T(8,128)S(1)}, f32[48,128]{1,0:T(8,128)S(1)}, u32[]{:S(2)}, u32[]{:S(2)}) collective-permute-start(f32[48,128]{1,0:T(8,128)S(1)} %bitcast_select_fusion.1), channel_id=1, source_target_pairs={{0,10},{1,19},{2,16},{3,9},{4,22},{5,15},{6,12},{7,21},{8,26},{9,3... | collective-permute-start | bytes 73736 | tf_op jit(solution)/shard_map/ppermute | solution.py:34
  16.3 2.9 %shard_map.78 = (f32[64,1024]{1,0:T(8,128)S(1)}, f32[512,1024]{1,0:T(8,128)S(1)}, bf16[288,1024]{1,0:T(8,128)(2,1)S(1)}, bf16[288,1024]{1,0:T(8,128)(2,1)S(1)}, ...) custom-call(f32[64,1024]{1,0:T(8,128)S(1)} %get-tuple-element.36.field, f32[64,1024]{1,0:T(8,128)S(1)} %copy-done.2, ...), custom_call_target="tpu_custom_call" | custom-call | tf_op jit(solution)/shard_map/pallas_call | solution.py:292
  19.3 0.3 collective-permute-done.7
  19.6 0.9 %collective-permute-start.8 = (f32[3,48,128]{2,1,0:T(8,128)S(1)}, f32[3,48,128]{2,1,0:T(8,128)S(1)}, u32[]{:S(2)}, u32[]{:S(2)}) collective-permute-start(f32[3,48,128]{2,1,0:T(8,128)S(1)} %pad_maximum_fusion), channel_id=1, source_target_pairs={{0,4},{1,5},{2,6},{3,7},{4,0},{5,1},{6,2},{7,3},{8,12},{9,13},{10,... | collective-permute-start | bytes 221192 | tf_op jit(solution)/shard_map/ppermute | solution.py:34
  20.5 0.9 %shard_map.80.base = f32[64,1024]{1,0:T(8,128)S(1)} custom-call(f32[64,1024]{1,0:T(8,128)S(1)} %get-tuple-element.38.near, f32[2,48,128]{2,1,0:T(8,128)S(1)} %pad_maximum_fusion.5.coefs, f32[6,96,1024]{2,1,0:T(8,128)S(1)} %copy-done, f32[64,1024]{1,0:T(8,128)S(1)} %get-tuple-element.36.field, f32[512,1024]{1,0:T(8,128)S(1)} %get-tuple-element.47.leaf_inverse), custom_call_target="tpu_custom_call" | custom-call | tf_op jit(solution)/shard_map/pallas_call | solution.py:255
  21.4 1.0 %shard_map.81 = (f32[64,1024]{1,0:T(8,128)S(1)}, f32[2,48,128]{2,1,0:T(8,128)S(1)}) custom-call(f32[64,1024]{1,0:T(8,128)S(1)} %shard_map.80.base, f32[3,48,128]{2,1,0:T(8,128)S(1)} %pad_maximum_fusion.1.coefs, bf16[288,1024]{1,0:T(8,128)(2,1)S(1)} %get-tuple-element.51.mixed_high, bf16[288,1024]{1,0:T(8,128)(2,1)S(1)} %get-tuple-element.52.mixed_low, ...), custom_call_target="tpu_custom_call" | custom-call | tf_op jit(solution)/shard_map/pallas_call | solution.py:255
  22.5 0.4 %collective-permute-start.9 = (f32[2,48,128]{2,1,0:T(8,128)S(1)}, f32[2,48,128]{2,1,0:T(8,128)S(1)}, u32[]{:S(2)}, u32[]{:S(2)}) collective-permute-start(f32[2,48,128]{2,1,0:T(8,128)S(1)} %get-tuple-element.58), channel_id=1, source_target_pairs={{0,4},{1,5},{2,6},{3,7},{4,0},{5,1},{6,2},{7,3},{8,12},{9,13},{10,... | collective-permute-start | bytes 147464 | tf_op jit(solution)/shard_map/ppermute | solution.py:34
  22.9 0.7 %shard_map.83 = f32[3,48,128]{2,1,0:T(8,128)S(1)} custom-call(f32[64,1024]{1,0:T(8,128)S(1)} %get-tuple-element.55.field, f32[6,96,1024]{2,1,0:T(8,128)S(1)} %get-tuple-element.37.row_basis), custom_call_target="tpu_custom_call" | custom-call | tf_op jit(solution)/shard_map/pallas_call | solution.py:255
  23.5 0.2 collective-permute-done.9
  23.8 1.5 %collective-permute-start.10 = (f32[2,48,128]{2,1,0:T(8,128)S(1)}, f32[2,48,128]{2,1,0:T(8,128)S(1)}, u32[]{:S(2)}, u32[]{:S(2)}) collective-permute-start(f32[2,48,128]{2,1,0:T(8,128)S(1)} %add.60), channel_id=1, source_target_pairs={{0,5},{1,4},{2,7},{3,6},{4,1},{5,0},{6,3},{7,2},{8,13},{9,12},{10,... | collective-permute-start | bytes 147464 | tf_op jit(solution)/shard_map/ppermute | solution.py:34
  25.3 0.5 %collective-permute-start.11 = (f32[2,48,128]{2,1,0:T(8,128)S(1)}, f32[2,48,128]{2,1,0:T(8,128)S(1)}, u32[]{:S(2)}, u32[]{:S(2)}) collective-permute-start(f32[2,48,128]{2,1,0:T(8,128)S(1)} %pad_maximum_fusion.6), channel_id=1, source_target_pairs={{0,1},{1,0},{2,3},{3,2},{4,5},{5,4},{6,7},{7,6},{8,9},{9,8},{10,11... | collective-permute-start | bytes 147464 | tf_op jit(solution)/shard_map/ppermute | solution.py:34
  25.8 2.6 %collective-permute-start.13 = (f32[2,48,128]{2,1,0:T(8,128)S(1)}, f32[2,48,128]{2,1,0:T(8,128)S(1)}, u32[]{:S(2)}, u32[]{:S(2)}) collective-permute-start(f32[2,48,128]{2,1,0:T(8,128)S(1)} %slice.85), channel_id=1, source_target_pairs={{0,3},{1,2},{2,1},{3,0},{4,7},{5,6},{6,5},{7,4},{8,11},{9,10},{10,... | collective-permute-start | bytes 147464 | tf_op jit(solution)/shard_map/ppermute | solution.py:34
  28.4 0.4 collective-permute-start.12
  28.8 0.6 %collective-permute-done.11 = f32[2,48,128]{2,1,0:T(8,128)S(1)} collective-permute-done((f32[2,48,128]{2,1,0:T(8,128)S(1)}, f32[2,48,128]{2,1,0:T(8,128)S(1)}, u32[]{:S(2)}, u32[]{:S(2)}) %collective-permute-start.11) | collective-permute-done | bytes 49184 | tf_op jit(solution)/shard_map/ppermute | solution.py:34
  29.4 0.6 %collective-permute-start.15 = (f32[48,128]{1,0:T(8,128)S(1)}, f32[48,128]{1,0:T(8,128)S(1)}, u32[]{:S(2)}, u32[]{:S(2)}) collective-permute-start(f32[48,128]{1,0:T(8,128)S(1)} %slice_bitcast_fusion.4), channel_id=1, source_target_pairs={{0,24},{1,31},{2,28},{3,27},{4,26},{5,29},{6,30},{7,25},{8,22},{9,... | collective-permute-start | bytes 73736 | tf_op jit(solution)/shard_map/ppermute | solution.py:34
  29.9 2.9 %collective-permute-start.14 = (f32[48,128]{1,0:T(8,128)S(1)}, f32[48,128]{1,0:T(8,128)S(1)}, u32[]{:S(2)}, u32[]{:S(2)}) collective-permute-start(f32[48,128]{1,0:T(8,128)S(1)} %bitcast_select_fusion), channel_id=1, source_target_pairs={{0,10},{1,19},{2,16},{3,9},{4,22},{5,15},{6,12},{7,21},{8,26},{9,3... | collective-permute-start | bytes 73736 | tf_op jit(solution)/shard_map/ppermute | solution.py:34
  32.9 1.4 %shard_map.82 = (f32[64,1024]{1,0:T(8,128)S(1)}, f32[64,1024]{1,0:T(8,128)}) custom-call(f32[64,1024]{1,0:T(8,128)S(1)} %get-tuple-element.55.field, f32[64,1024]{1,0:T(8,128)S(1)} %copy-done.2, f32[512,1024]{1,0:T(8,128)S(1)} %copy-done.1, f32[6,96,1024]{2,1,0:T(8,128)S(1)} %copy-done, f32[6,96,1024]{2,1,0:T(8,128)S(1)} %get-tuple-element.37.row_basis), custom_call_target="tpu_custom_call" | custom-call | tf_op jit(solution)/shard_map/pallas_call | solution.py:255
  34.3 0.2 collective-permute-done.12
  34.5 1.1 %collective-permute-done.14 = f32[48,128]{1,0:T(8,128)S(1)} collective-permute-done((f32[48,128]{1,0:T(8,128)S(1)}, f32[48,128]{1,0:T(8,128)S(1)}, u32[]{:S(2)}, u32[]{:S(2)}) %collective-permute-start.14) | collective-permute-done | bytes 24608 | tf_op jit(solution)/shard_map/ppermute | solution.py:34
  35.6 0.6 %collective-permute-done.16 = f32[48,128]{1,0:T(8,128)S(1)} collective-permute-done((f32[48,128]{1,0:T(8,128)S(1)}, f32[48,128]{1,0:T(8,128)S(1)}, u32[]{:S(2)}, u32[]{:S(2)}) %collective-permute-start.16) | collective-permute-done | bytes 24608 | tf_op jit(solution)/shard_map/ppermute | solution.py:34
  36.2 0.5 %collective-permute-start.17 = (f32[3,48,128]{2,1,0:T(8,128)S(1)}, f32[3,48,128]{2,1,0:T(8,128)S(1)}, u32[]{:S(2)}, u32[]{:S(2)}) collective-permute-start(f32[3,48,128]{2,1,0:T(8,128)S(1)} %pad_maximum_fusion.2), channel_id=1, source_target_pairs={{0,4},{1,5},{2,6},{3,7},{4,0},{5,1},{6,2},{7,3},{8,12},{9,13},{10,... | collective-permute-start | bytes 221192 | tf_op jit(solution)/shard_map/ppermute | solution.py:34
  36.7 0.5 %shard_map.84.near = f32[64,1024]{1,0:T(8,128)S(1)} custom-call(f32[64,1024]{1,0:T(8,128)S(1)} %get-tuple-element.57.near, f32[2,48,128]{2,1,0:T(8,128)S(1)} %pad_maximum_fusion.7.coefs, f32[6,96,1024]{2,1,0:T(8,128)S(1)} %copy-done), custom_call_target="tpu_custom_call" | custom-call | tf_op jit(solution)/shard_map/pallas_call | solution.py:255
  37.2 0.4 %collective-permute-done.17 = f32[3,48,128]{2,1,0:T(8,128)S(1)} collective-permute-done((f32[3,48,128]{2,1,0:T(8,128)S(1)}, f32[3,48,128]{2,1,0:T(8,128)S(1)}, u32[]{:S(2)}, u32[]{:S(2)}) %collective-permute-start.17) | collective-permute-done | bytes 73760 | tf_op jit(solution)/shard_map/ppermute | solution.py:34
  37.6 1.3 %shard_map.85 = f32[64,1024]{1,0:T(8,128)} custom-call(f32[64,1024]{1,0:T(8,128)S(1)} %shard_map.84.near, f32[3,48,128]{2,1,0:T(8,128)S(1)} %pad_maximum_fusion.3.coefs, f32[6,96,1024]{2,1,0:T(8,128)S(1)} %copy-done), custom_call_target="tpu_custom_call" | custom-call | tf_op jit(solution)/shard_map/pallas_call | solution.py:316
  (49 shorter events, 0.3 us)
Async XLA Ops:
  0.6 15.7 %copy-start.1 = (f32[512,1024]{1,0:T(8,128)S(1)}, f32[512,1024]{1,0:T(8,128)}, u32[]{:S(2)}) copy-start(f32[512,1024]{1,0:T(8,128)} %leaf_blocks.3) | copy-start | bytes 6291460
  2.5 13.8 %copy-start = (f32[6,96,1024]{2,1,0:T(8,128)S(1)}, f32[6,96,1024]{2,1,0:T(8,128)}, u32[]{:S(2)}) copy-start(f32[6,96,1024]{2,1,0:T(8,128)} %col_basis.9) | copy-start | bytes 7077892
  2.5 13.8 %copy-start.2 = (f32[64,1024]{1,0:T(8,128)S(1)}, f32[64,1024]{1,0:T(8,128)}, u32[]{:S(2)}) copy-start(f32[64,1024]{1,0:T(8,128)} %incident.3) | copy-start | bytes 786436
  2.6 1.4 %collective-permute-start = (f32[2,48,128]{2,1,0:T(8,128)S(1)}, f32[2,48,128]{2,1,0:T(8,128)S(1)}, u32[]{:S(2)}, u32[]{:S(2)}) collective-permute-start(f32[2,48,128]{2,1,0:T(8,128)S(1)} %get-tuple-element.39), channel_id=1, source_target_pairs={{0,4},{1,5},{2,6},{3,7},{4,0},{5,1},{6,2},{7,3},{8,12},{9,13},{10,... | collective-permute-start | bytes 147464 | tf_op jit(solution)/shard_map/ppermute | solution.py:34
  4.0 6.8 %collective-permute-start.1 = (f32[2,48,128]{2,1,0:T(8,128)S(1)}, f32[2,48,128]{2,1,0:T(8,128)S(1)}, u32[]{:S(2)}, u32[]{:S(2)}) collective-permute-start(f32[2,48,128]{2,1,0:T(8,128)S(1)} %add.52), channel_id=1, source_target_pairs={{0,5},{1,4},{2,7},{3,6},{4,1},{5,0},{6,3},{7,2},{8,13},{9,12},{10,... | collective-permute-start | bytes 147464 | tf_op jit(solution)/shard_map/ppermute | solution.py:34
  6.7 4.1 %collective-permute-start.2 = (f32[2,48,128]{2,1,0:T(8,128)S(1)}, f32[2,48,128]{2,1,0:T(8,128)S(1)}, u32[]{:S(2)}, u32[]{:S(2)}) collective-permute-start(f32[2,48,128]{2,1,0:T(8,128)S(1)} %pad_maximum_fusion.4), channel_id=1, source_target_pairs={{0,1},{1,0},{2,3},{3,2},{4,5},{5,4},{6,7},{7,6},{8,9},{9,8},{10,11... | collective-permute-start | bytes 147464 | tf_op jit(solution)/shard_map/ppermute | solution.py:34
  7.0 9.2 %collective-permute-start.4 = (f32[2,48,128]{2,1,0:T(8,128)S(1)}, f32[2,48,128]{2,1,0:T(8,128)S(1)}, u32[]{:S(2)}, u32[]{:S(2)}) collective-permute-start(f32[2,48,128]{2,1,0:T(8,128)S(1)} %slice.80), channel_id=1, source_target_pairs={{0,3},{1,2},{2,1},{3,0},{4,7},{5,6},{6,5},{7,4},{8,11},{9,10},{10,... | collective-permute-start | bytes 147464 | tf_op jit(solution)/shard_map/ppermute | solution.py:34
  10.7 8.5 %collective-permute-start.3 = (f32[2,48,128]{2,1,0:T(8,128)S(1)}, f32[2,48,128]{2,1,0:T(8,128)S(1)}, u32[]{:S(2)}, u32[]{:S(2)}) collective-permute-start(f32[2,48,128]{2,1,0:T(8,128)S(1)} %slice.80), channel_id=1, source_target_pairs={{0,2},{1,3},{2,0},{3,1},{4,6},{5,7},{6,4},{7,5},{8,10},{9,11},{10,... | collective-permute-start | bytes 147464 | tf_op jit(solution)/shard_map/ppermute | solution.py:34
  10.8 8.5 %collective-permute-start.6 = (f32[48,128]{1,0:T(8,128)S(1)}, f32[48,128]{1,0:T(8,128)S(1)}, u32[]{:S(2)}, u32[]{:S(2)}) collective-permute-start(f32[48,128]{1,0:T(8,128)S(1)} %slice_bitcast_fusion.5), channel_id=1, source_target_pairs={{0,24},{1,31},{2,28},{3,27},{4,26},{5,29},{6,30},{7,25},{8,22},{9,... | collective-permute-start | bytes 73736 | tf_op jit(solution)/shard_map/ppermute | solution.py:34
  13.3 6.0 %collective-permute-start.5 = (f32[48,128]{1,0:T(8,128)S(1)}, f32[48,128]{1,0:T(8,128)S(1)}, u32[]{:S(2)}, u32[]{:S(2)}) collective-permute-start(f32[48,128]{1,0:T(8,128)S(1)} %bitcast_select_fusion.1), channel_id=1, source_target_pairs={{0,10},{1,19},{2,16},{3,9},{4,22},{5,15},{6,12},{7,21},{8,26},{9,3... | collective-permute-start | bytes 73736 | tf_op jit(solution)/shard_map/ppermute | solution.py:34
  16.3 3.3 %collective-permute-start.7 = (f32[48,128]{1,0:T(8,128)S(1)}, f32[48,128]{1,0:T(8,128)S(1)}, u32[]{:S(2)}, u32[]{:S(2)}) collective-permute-start(f32[48,128]{1,0:T(8,128)S(1)} %bitcast_select_fusion.1), channel_id=1, source_target_pairs={{0,12},{1,21},{2,22},{3,15},{4,16},{5,9},{6,10},{7,19},{8,28},{9,5... | collective-permute-start | bytes 73736 | tf_op jit(solution)/shard_map/ppermute | solution.py:34
  19.6 1.8 %collective-permute-start.8 = (f32[3,48,128]{2,1,0:T(8,128)S(1)}, f32[3,48,128]{2,1,0:T(8,128)S(1)}, u32[]{:S(2)}, u32[]{:S(2)}) collective-permute-start(f32[3,48,128]{2,1,0:T(8,128)S(1)} %pad_maximum_fusion), channel_id=1, source_target_pairs={{0,4},{1,5},{2,6},{3,7},{4,0},{5,1},{6,2},{7,3},{8,12},{9,13},{10,... | collective-permute-start | bytes 221192 | tf_op jit(solution)/shard_map/ppermute | solution.py:34
  22.5 1.3 %collective-permute-start.9 = (f32[2,48,128]{2,1,0:T(8,128)S(1)}, f32[2,48,128]{2,1,0:T(8,128)S(1)}, u32[]{:S(2)}, u32[]{:S(2)}) collective-permute-start(f32[2,48,128]{2,1,0:T(8,128)S(1)} %get-tuple-element.58), channel_id=1, source_target_pairs={{0,4},{1,5},{2,6},{3,7},{4,0},{5,1},{6,2},{7,3},{8,12},{9,13},{10,... | collective-permute-start | bytes 147464 | tf_op jit(solution)/shard_map/ppermute | solution.py:34
  23.8 5.0 %collective-permute-start.10 = (f32[2,48,128]{2,1,0:T(8,128)S(1)}, f32[2,48,128]{2,1,0:T(8,128)S(1)}, u32[]{:S(2)}, u32[]{:S(2)}) collective-permute-start(f32[2,48,128]{2,1,0:T(8,128)S(1)} %add.60), channel_id=1, source_target_pairs={{0,5},{1,4},{2,7},{3,6},{4,1},{5,0},{6,3},{7,2},{8,13},{9,12},{10,... | collective-permute-start | bytes 147464 | tf_op jit(solution)/shard_map/ppermute | solution.py:34
  25.3 4.1 %collective-permute-start.11 = (f32[2,48,128]{2,1,0:T(8,128)S(1)}, f32[2,48,128]{2,1,0:T(8,128)S(1)}, u32[]{:S(2)}, u32[]{:S(2)}) collective-permute-start(f32[2,48,128]{2,1,0:T(8,128)S(1)} %pad_maximum_fusion.6), channel_id=1, source_target_pairs={{0,1},{1,0},{2,3},{3,2},{4,5},{5,4},{6,7},{7,6},{8,9},{9,8},{10,11... | collective-permute-start | bytes 147464 | tf_op jit(solution)/shard_map/ppermute | solution.py:34
  25.8 7.1 %collective-permute-start.13 = (f32[2,48,128]{2,1,0:T(8,128)S(1)}, f32[2,48,128]{2,1,0:T(8,128)S(1)}, u32[]{:S(2)}, u32[]{:S(2)}) collective-permute-start(f32[2,48,128]{2,1,0:T(8,128)S(1)} %slice.85), channel_id=1, source_target_pairs={{0,3},{1,2},{2,1},{3,0},{4,7},{5,6},{6,5},{7,4},{8,11},{9,10},{10,... | collective-permute-start | bytes 147464 | tf_op jit(solution)/shard_map/ppermute | solution.py:34
  28.4 6.1 %collective-permute-start.12 = (f32[2,48,128]{2,1,0:T(8,128)S(1)}, f32[2,48,128]{2,1,0:T(8,128)S(1)}, u32[]{:S(2)}, u32[]{:S(2)}) collective-permute-start(f32[2,48,128]{2,1,0:T(8,128)S(1)} %slice.85), channel_id=1, source_target_pairs={{0,2},{1,3},{2,0},{3,1},{4,6},{5,7},{6,4},{7,5},{8,10},{9,11},{10,... | collective-permute-start | bytes 147464 | tf_op jit(solution)/shard_map/ppermute | solution.py:34
  29.4 5.1 %collective-permute-start.15 = (f32[48,128]{1,0:T(8,128)S(1)}, f32[48,128]{1,0:T(8,128)S(1)}, u32[]{:S(2)}, u32[]{:S(2)}) collective-permute-start(f32[48,128]{1,0:T(8,128)S(1)} %slice_bitcast_fusion.4), channel_id=1, source_target_pairs={{0,24},{1,31},{2,28},{3,27},{4,26},{5,29},{6,30},{7,25},{8,22},{9,... | collective-permute-start | bytes 73736 | tf_op jit(solution)/shard_map/ppermute | solution.py:34
  29.9 5.6 %collective-permute-start.14 = (f32[48,128]{1,0:T(8,128)S(1)}, f32[48,128]{1,0:T(8,128)S(1)}, u32[]{:S(2)}, u32[]{:S(2)}) collective-permute-start(f32[48,128]{1,0:T(8,128)S(1)} %bitcast_select_fusion), channel_id=1, source_target_pairs={{0,10},{1,19},{2,16},{3,9},{4,22},{5,15},{6,12},{7,21},{8,26},{9,3... | collective-permute-start | bytes 73736 | tf_op jit(solution)/shard_map/ppermute | solution.py:34
  32.9 3.3 %collective-permute-start.16 = (f32[48,128]{1,0:T(8,128)S(1)}, f32[48,128]{1,0:T(8,128)S(1)}, u32[]{:S(2)}, u32[]{:S(2)}) collective-permute-start(f32[48,128]{1,0:T(8,128)S(1)} %bitcast_select_fusion), channel_id=1, source_target_pairs={{0,12},{1,21},{2,22},{3,15},{4,16},{5,9},{6,10},{7,19},{8,28},{9,5... | collective-permute-start | bytes 73736 | tf_op jit(solution)/shard_map/ppermute | solution.py:34
  36.2 1.4 %collective-permute-start.17 = (f32[3,48,128]{2,1,0:T(8,128)S(1)}, f32[3,48,128]{2,1,0:T(8,128)S(1)}, u32[]{:S(2)}, u32[]{:S(2)}) collective-permute-start(f32[3,48,128]{2,1,0:T(8,128)S(1)} %pad_maximum_fusion.2), channel_id=1, source_target_pairs={{0,4},{1,5},{2,6},{3,7},{4,0},{5,1},{6,2},{7,3},{8,12},{9,13},{10,... | collective-permute-start | bytes 221192 | tf_op jit(solution)/shard_map/ppermute | solution.py:34

commit v6 on v5

--- a/solution.py
+++ b/solution.py
@@ -74,15 +74,16 @@
     far = swap(own, ((2, 2), (4, 2)))
     own, last_low = lax.optimization_barrier((own, last_low))
     beside = swap(own, ((3, 0), (5, 0)))
-    far_low, last_low, far, corner, beside = lax.optimization_barrier((far_low, last_low, far, corner, beside))
+    far_low, last_low = lax.optimization_barrier((far_low, last_low))
     both_low = far_low + last_low
-    near = apply(1, near, jnp.stack([next_low[0], both_low[0]]), *others)
-    third = low[2] + next_low[1] + both_low[1]
+    third = swap(low[2] + next_low[1] + both_low[1], core)
+    far, corner, beside, third = lax.optimization_barrier((far, corner, beside, third))
     mine = beside + far
-    third, other, corner_other = swap(jnp.stack([third, mine, corner]), core)
+    other, corner_other = swap(jnp.stack([mine, corner]), core)
+    near = apply(1, near, jnp.stack([next_low[0], both_low[0], third]), *others)
     fourth = jnp.where(first, mine, other)
     fifth = jnp.where(first, other, mine) + (corner + corner_other)
-    return near, 3, jnp.stack([third, fourth, fifth]), others
+    return near, 4, jnp.stack([fourth, fifth]), others
 
 
 def goes_in_lanes():
@@ -282,7 +283,7 @@
     )(*[pltpu.with_memory_space_constraint(a, pltpu.HBM) for a in (solution, row_basis)])
     (low,) = run(low_kernel, [low_out], field, row_basis)
 
-    late = 3 if goes_in_lanes() else levels - TOP
+    late = levels - TOP
     mixed_out = (((levels - late) * rank, rows), True, jnp.bfloat16)
     split_out = ((TOP * rank, rows), True, jnp.bfloat16)
 

time: 39.1 us -> 39 us (level)
  Pallas kernels: 11.2 us -> 10.8 us
    ppermute x18 -> x20, waiting for transfers between devices: 3.59 us -> 3.79 us  [swap(): return lax.ppermute(block, AXES, route)]
    ppermute x18 -> x20, starting transfers between devices: 23.1 us -> 23.2 us  [swap(): return lax.ppermute(block, AXES, route)]
  transfers between devices with their start and end apart: 18 -> 20, of which waited for: 8 -> 7; matrix products, arithmetic and copies ran while one was open for 0% -> 0% of each run, Pallas kernels for 18% -> 18%
where the time goes in v6:
time: 39 us; the launch traced here: 38.8 us
  starting transfers between devices  23.2 us (59%)
  Pallas kernels  10.8 us (28%)
  waiting for transfers between devices  3.79 us (10%)
  between operations  0.86 us (2%)
    ppermute x20, starting transfers between devices, swap(): return lax.ppermute(block, AXES, route)  23.2 us
    pallas_call x6, Pallas kernels, run(): pl.pallas_call(kernel, out_shape=[VMEM(shape, kind) if inside else jax.Sh...  5.18 us
    ppermute x20, waiting for transfers between devices, swap(): return lax.ppermute(block, AXES, route)  3.79 us
    pallas_call x1, Pallas kernels, near_and_tables(): pl.pallas_call(functools.partial(near_and_tables_kernel, late), out_shape...  2.6 us
    pallas_call x1, Pallas kernels, per_device(): pl.pallas_call(first_top_kernel, out_shape=[VMEM(top_out[0], F32), VMEM(s...  1.88 us
    pallas_call x1, Pallas kernels, per_device(): pl.pallas_call(functools.partial(last_kernel, start), out_shape=jax.Shape...  1.14 us
  transfers between devices with their start and end apart: 20, of which 7 were waited for; matrix products, arithmetic and copies ran while one was open for 0% of the time, Pallas kernels for 18%

profile of v6, /device:TPU:0, one launch (start us, length us, event | category | flops | bytes accessed | tf_op | source)
XLA Modules:
  0.0 38.8 jit_solution(14270231362783432704)
XLA Ops:
  0.7 1.9 %shard_map.77 = (f32[2,48,128]{2,1,0:T(8,128)S(1)}, f32[64,1024]{1,0:T(8,128)S(1)}, f32[6,96,1024]{2,1,0:T(8,128)S(1)}) custom-call(f32[64,1024]{1,0:T(8,128)} %field_hbm, f32[6,96,1024]{2,1,0:T(8,128)} %row_hbm.1), custom_call_target="tpu_custom_call" | custom-call | tf_op jit(solution)/shard_map/pallas_call | solution.py:276
  2.6 0.5 %collective-permute-start = (f32[2,48,128]{2,1,0:T(8,128)S(1)}, f32[2,48,128]{2,1,0:T(8,128)S(1)}, u32[]{:S(2)}, u32[]{:S(2)}) collective-permute-start(f32[2,48,128]{2,1,0:T(8,128)S(1)} %get-tuple-element.41), channel_id=1, source_target_pairs={{0,4},{1,5},{2,6},{3,7},{4,0},{5,1},{6,2},{7,3},{8,12},{9,13},{10,... | collective-permute-start | bytes 147464 | tf_op jit(solution)/shard_map/ppermute | solution.py:34
  3.1 0.7 %shard_map.79 = f32[3,48,128]{2,1,0:T(8,128)S(1)} custom-call(f32[64,1024]{1,0:T(8,128)S(1)} %get-tuple-element.38.field, f32[6,96,1024]{2,1,0:T(8,128)S(1)} %get-tuple-element.39.row_basis), custom_call_target="tpu_custom_call" | custom-call | tf_op jit(solution)/shard_map/pallas_call | solution.py:256
  3.8 0.2 collective-permute-done
  4.0 2.7 %collective-permute-start.1 = (f32[2,48,128]{2,1,0:T(8,128)S(1)}, f32[2,48,128]{2,1,0:T(8,128)S(1)}, u32[]{:S(2)}, u32[]{:S(2)}) collective-permute-start(f32[2,48,128]{2,1,0:T(8,128)S(1)} %add.56), channel_id=1, source_target_pairs={{0,5},{1,4},{2,7},{3,6},{4,1},{5,0},{6,3},{7,2},{8,13},{9,12},{10,... | collective-permute-start | bytes 147464 | tf_op jit(solution)/shard_map/ppermute | solution.py:34
  6.7 0.4 collective-permute-start.2
  7.0 3.7 %collective-permute-start.4 = (f32[2,48,128]{2,1,0:T(8,128)S(1)}, f32[2,48,128]{2,1,0:T(8,128)S(1)}, u32[]{:S(2)}, u32[]{:S(2)}) collective-permute-start(f32[2,48,128]{2,1,0:T(8,128)S(1)} %slice.80), channel_id=1, source_target_pairs={{0,3},{1,2},{2,1},{3,0},{4,7},{5,6},{6,5},{7,4},{8,11},{9,10},{10,... | collective-permute-start | bytes 147464 | tf_op jit(solution)/shard_map/ppermute | solution.py:34
  10.8 2.5 %collective-permute-start.6 = (f32[48,128]{1,0:T(8,128)S(1)}, f32[48,128]{1,0:T(8,128)S(1)}, u32[]{:S(2)}, u32[]{:S(2)}) collective-permute-start(f32[48,128]{1,0:T(8,128)S(1)} %slice_bitcast_fusion.5), channel_id=1, source_target_pairs={{0,24},{1,31},{2,28},{3,27},{4,26},{5,29},{6,30},{7,25},{8,22},{9,... | collective-permute-start | bytes 73736 | tf_op jit(solution)/shard_map/ppermute | solution.py:34
  13.3 3.0 %collective-permute-start.5 = (f32[48,128]{1,0:T(8,128)S(1)}, f32[48,128]{1,0:T(8,128)S(1)}, u32[]{:S(2)}, u32[]{:S(2)}) collective-permute-start(f32[48,128]{1,0:T(8,128)S(1)} %bitcast_select_fusion.1), channel_id=1, source_target_pairs={{0,10},{1,19},{2,16},{3,9},{4,22},{5,15},{6,12},{7,21},{8,26},{9,3... | collective-permute-start | bytes 73736 | tf_op jit(solution)/shard_map/ppermute | solution.py:34
  16.3 0.5 %collective-permute-start.8 = (f32[48,128]{1,0:T(8,128)S(1)}, f32[48,128]{1,0:T(8,128)S(1)}, u32[]{:S(2)}, u32[]{:S(2)}) collective-permute-start(f32[48,128]{1,0:T(8,128)S(1)} %get-tuple-element.84), channel_id=1, source_target_pairs={{0,4},{1,5},{2,6},{3,7},{4,0},{5,1},{6,2},{7,3},{8,12},{9,13},{10,... | collective-permute-start | bytes 73736 | tf_op jit(solution)/shard_map/ppermute | solution.py:34
  16.8 2.6 %shard_map.78 = (f32[64,1024]{1,0:T(8,128)S(1)}, f32[512,1024]{1,0:T(8,128)S(1)}, bf16[192,1024]{1,0:T(8,128)(2,1)S(1)}, bf16[192,1024]{1,0:T(8,128)(2,1)S(1)}, ...) custom-call(f32[64,1024]{1,0:T(8,128)S(1)} %get-tuple-element.38.field, f32[64,1024]{1,0:T(8,128)S(1)} %copy-done.2, ...), custom_call_target="tpu_custom_call" | custom-call | tf_op jit(solution)/shard_map/pallas_call | solution.py:293
  19.6 0.9 %collective-permute-start.9 = (f32[2,48,128]{2,1,0:T(8,128)S(1)}, f32[2,48,128]{2,1,0:T(8,128)S(1)}, u32[]{:S(2)}, u32[]{:S(2)}) collective-permute-start(f32[2,48,128]{2,1,0:T(8,128)S(1)} %pad_maximum_fusion.3), channel_id=1, source_target_pairs={{0,4},{1,5},{2,6},{3,7},{4,0},{5,1},{6,2},{7,3},{8,12},{9,13},{10,... | collective-permute-start | bytes 147464 | tf_op jit(solution)/shard_map/ppermute | solution.py:34
  20.4 1.0 %shard_map.80.base = f32[64,1024]{1,0:T(8,128)S(1)} custom-call(f32[64,1024]{1,0:T(8,128)S(1)} %get-tuple-element.40.near, f32[3,48,128]{2,1,0:T(8,128)S(1)} %pad_maximum_fusion.coefs, f32[6,96,1024]{2,1,0:T(8,128)S(1)} %copy-done, f32[64,1024]{1,0:T(8,128)S(1)} %get-tuple-element.38.field, f32[512,1024]{1,0:T(8,128)S(1)} %get-tuple-element.50.leaf_inverse), custom_call_target="tpu_custom_call" | custom-call | tf_op jit(solution)/shard_map/pallas_call | solution.py:256
  21.5 0.8 %shard_map.81 = (f32[64,1024]{1,0:T(8,128)S(1)}, f32[2,48,128]{2,1,0:T(8,128)S(1)}) custom-call(f32[64,1024]{1,0:T(8,128)S(1)} %shard_map.80.base, f32[2,48,128]{2,1,0:T(8,128)S(1)} %pad_maximum_fusion.4.coefs, bf16[192,1024]{1,0:T(8,128)(2,1)S(1)} %get-tuple-element.54.mixed_high, bf16[192,1024]{1,0:T(8,128)(2,1)S(1)} %get-tuple-element.55.mixed_low, ...), custom_call_target="tpu_custom_call" | custom-call | tf_op jit(solution)/shard_map/pallas_call | solution.py:256
  22.3 0.2 collective-permute-start.10
  22.6 0.7 %shard_map.83 = f32[3,48,128]{2,1,0:T(8,128)S(1)} custom-call(f32[64,1024]{1,0:T(8,128)S(1)} %get-tuple-element.58.field, f32[6,96,1024]{2,1,0:T(8,128)S(1)} %get-tuple-element.39.row_basis), custom_call_target="tpu_custom_call" | custom-call | tf_op jit(solution)/shard_map/pallas_call | solution.py:256
  23.3 0.4 collective-permute-done.10
  23.7 1.5 %collective-permute-start.11 = (f32[2,48,128]{2,1,0:T(8,128)S(1)}, f32[2,48,128]{2,1,0:T(8,128)S(1)}, u32[]{:S(2)}, u32[]{:S(2)}) collective-permute-start(f32[2,48,128]{2,1,0:T(8,128)S(1)} %add.65), channel_id=1, source_target_pairs={{0,5},{1,4},{2,7},{3,6},{4,1},{5,0},{6,3},{7,2},{8,13},{9,12},{10,... | collective-permute-start | bytes 147464 | tf_op jit(solution)/shard_map/ppermute | solution.py:34
  25.2 0.4 collective-permute-start.12
  25.5 2.7 %collective-permute-start.14 = (f32[2,48,128]{2,1,0:T(8,128)S(1)}, f32[2,48,128]{2,1,0:T(8,128)S(1)}, u32[]{:S(2)}, u32[]{:S(2)}) collective-permute-start(f32[2,48,128]{2,1,0:T(8,128)S(1)} %slice.85), channel_id=1, source_target_pairs={{0,3},{1,2},{2,1},{3,0},{4,7},{5,6},{6,5},{7,4},{8,11},{9,10},{10,... | collective-permute-start | bytes 147464 | tf_op jit(solution)/shard_map/ppermute | solution.py:34
  28.2 0.4 %collective-permute-start.13 = (f32[2,48,128]{2,1,0:T(8,128)S(1)}, f32[2,48,128]{2,1,0:T(8,128)S(1)}, u32[]{:S(2)}, u32[]{:S(2)}) collective-permute-start(f32[2,48,128]{2,1,0:T(8,128)S(1)} %slice.85), channel_id=1, source_target_pairs={{0,2},{1,3},{2,0},{3,1},{4,6},{5,7},{6,4},{7,5},{8,10},{9,11},{10,... | collective-permute-start | bytes 147464 | tf_op jit(solution)/shard_map/ppermute | solution.py:34
  28.7 0.6 %collective-permute-done.12 = f32[2,48,128]{2,1,0:T(8,128)S(1)} collective-permute-done((f32[2,48,128]{2,1,0:T(8,128)S(1)}, f32[2,48,128]{2,1,0:T(8,128)S(1)}, u32[]{:S(2)}, u32[]{:S(2)}) %collective-permute-start.12) | collective-permute-done | bytes 49184 | tf_op jit(solution)/shard_map/ppermute | solution.py:34
  29.3 1.4 %collective-permute-start.16 = (f32[48,128]{1,0:T(8,128)S(1)}, f32[48,128]{1,0:T(8,128)S(1)}, u32[]{:S(2)}, u32[]{:S(2)}) collective-permute-start(f32[48,128]{1,0:T(8,128)S(1)} %slice_bitcast_fusion.4), channel_id=1, source_target_pairs={{0,24},{1,31},{2,28},{3,27},{4,26},{5,29},{6,30},{7,25},{8,22},{9,... | collective-permute-start | bytes 73736 | tf_op jit(solution)/shard_map/ppermute | solution.py:34
  30.7 2.1 %collective-permute-start.15 = (f32[48,128]{1,0:T(8,128)S(1)}, f32[48,128]{1,0:T(8,128)S(1)}, u32[]{:S(2)}, u32[]{:S(2)}) collective-permute-start(f32[48,128]{1,0:T(8,128)S(1)} %bitcast_select_fusion), channel_id=1, source_target_pairs={{0,10},{1,19},{2,16},{3,9},{4,22},{5,15},{6,12},{7,21},{8,26},{9,3... | collective-permute-start | bytes 73736 | tf_op jit(solution)/shard_map/ppermute | solution.py:34
  32.8 1.2 %collective-permute-done.13 = f32[2,48,128]{2,1,0:T(8,128)S(1)} collective-permute-done((f32[2,48,128]{2,1,0:T(8,128)S(1)}, f32[2,48,128]{2,1,0:T(8,128)S(1)}, u32[]{:S(2)}, u32[]{:S(2)}) %collective-permute-start.13) | collective-permute-done | bytes 49184 | tf_op jit(solution)/shard_map/ppermute | solution.py:34
  33.9 0.2 collective-permute-start.18
  34.1 1.4 %shard_map.82 = (f32[64,1024]{1,0:T(8,128)S(1)}, f32[64,1024]{1,0:T(8,128)}) custom-call(f32[64,1024]{1,0:T(8,128)S(1)} %get-tuple-element.58.field, f32[64,1024]{1,0:T(8,128)S(1)} %copy-done.2, f32[512,1024]{1,0:T(8,128)S(1)} %copy-done.1, f32[6,96,1024]{2,1,0:T(8,128)S(1)} %copy-done, f32[6,96,1024]{2,1,0:T(8,128)S(1)} %get-tuple-element.39.row_basis), custom_call_target="tpu_custom_call" | custom-call | tf_op jit(solution)/shard_map/pallas_call | solution.py:256
  35.5 0.8 %collective-permute-done.15 = f32[48,128]{1,0:T(8,128)S(1)} collective-permute-done((f32[48,128]{1,0:T(8,128)S(1)}, f32[48,128]{1,0:T(8,128)S(1)}, u32[]{:S(2)}, u32[]{:S(2)}) %collective-permute-start.15) | collective-permute-done | bytes 24608 | tf_op jit(solution)/shard_map/ppermute | solution.py:34
  36.3 0.2 collective-permute-start.19
  36.5 0.6 %shard_map.84.near = f32[64,1024]{1,0:T(8,128)S(1)} custom-call(f32[64,1024]{1,0:T(8,128)S(1)} %get-tuple-element.60.near, f32[3,48,128]{2,1,0:T(8,128)S(1)} %pad_maximum_fusion.1.coefs, f32[6,96,1024]{2,1,0:T(8,128)S(1)} %copy-done), custom_call_target="tpu_custom_call" | custom-call | tf_op jit(solution)/shard_map/pallas_call | solution.py:256
  37.1 0.5 %collective-permute-done.19 = f32[2,48,128]{2,1,0:T(8,128)S(1)} collective-permute-done((f32[2,48,128]{2,1,0:T(8,128)S(1)}, f32[2,48,128]{2,1,0:T(8,128)S(1)}, u32[]{:S(2)}, u32[]{:S(2)}) %collective-permute-start.19) | collective-permute-done | bytes 49184 | tf_op jit(solution)/shard_map/ppermute | solution.py:34
  37.7 1.1 %shard_map.85 = f32[64,1024]{1,0:T(8,128)} custom-call(f32[64,1024]{1,0:T(8,128)S(1)} %shard_map.84.near, f32[2,48,128]{2,1,0:T(8,128)S(1)} %pad_maximum_fusion.7.coefs, f32[6,96,1024]{2,1,0:T(8,128)S(1)} %copy-done), custom_call_target="tpu_custom_call" | custom-call | tf_op jit(solution)/shard_map/pallas_call | solution.py:317
  (51 shorter events, 0.4 us)
Async XLA Ops:
  0.6 16.2 %copy-start.1 = (f32[512,1024]{1,0:T(8,128)S(1)}, f32[512,1024]{1,0:T(8,128)}, u32[]{:S(2)}) copy-start(f32[512,1024]{1,0:T(8,128)} %leaf_blocks.3) | copy-start | bytes 6291460
  2.5 14.3 %copy-start = (f32[6,96,1024]{2,1,0:T(8,128)S(1)}, f32[6,96,1024]{2,1,0:T(8,128)}, u32[]{:S(2)}) copy-start(f32[6,96,1024]{2,1,0:T(8,128)} %col_basis.9) | copy-start | bytes 7077892
  2.5 14.3 %copy-start.2 = (f32[64,1024]{1,0:T(8,128)S(1)}, f32[64,1024]{1,0:T(8,128)}, u32[]{:S(2)}) copy-start(f32[64,1024]{1,0:T(8,128)} %incident.3) | copy-start | bytes 786436
  2.6 1.4 %collective-permute-start = (f32[2,48,128]{2,1,0:T(8,128)S(1)}, f32[2,48,128]{2,1,0:T(8,128)S(1)}, u32[]{:S(2)}, u32[]{:S(2)}) collective-permute-start(f32[2,48,128]{2,1,0:T(8,128)S(1)} %get-tuple-element.41), channel_id=1, source_target_pairs={{0,4},{1,5},{2,6},{3,7},{4,0},{5,1},{6,2},{7,3},{8,12},{9,13},{10,... | collective-permute-start | bytes 147464 | tf_op jit(solution)/shard_map/ppermute | solution.py:34
  4.0 6.8 %collective-permute-start.1 = (f32[2,48,128]{2,1,0:T(8,128)S(1)}, f32[2,48,128]{2,1,0:T(8,128)S(1)}, u32[]{:S(2)}, u32[]{:S(2)}) collective-permute-start(f32[2,48,128]{2,1,0:T(8,128)S(1)} %add.56), channel_id=1, source_target_pairs={{0,5},{1,4},{2,7},{3,6},{4,1},{5,0},{6,3},{7,2},{8,13},{9,12},{10,... | collective-permute-start | bytes 147464 | tf_op jit(solution)/shard_map/ppermute | solution.py:34
  6.7 4.1 %collective-permute-start.2 = (f32[2,48,128]{2,1,0:T(8,128)S(1)}, f32[2,48,128]{2,1,0:T(8,128)S(1)}, u32[]{:S(2)}, u32[]{:S(2)}) collective-permute-start(f32[2,48,128]{2,1,0:T(8,128)S(1)} %pad_maximum_fusion.2), channel_id=1, source_target_pairs={{0,1},{1,0},{2,3},{3,2},{4,5},{5,4},{6,7},{7,6},{8,9},{9,8},{10,11... | collective-permute-start | bytes 147464 | tf_op jit(solution)/shard_map/ppermute | solution.py:34
  7.0 9.2 %collective-permute-start.4 = (f32[2,48,128]{2,1,0:T(8,128)S(1)}, f32[2,48,128]{2,1,0:T(8,128)S(1)}, u32[]{:S(2)}, u32[]{:S(2)}) collective-permute-start(f32[2,48,128]{2,1,0:T(8,128)S(1)} %slice.80), channel_id=1, source_target_pairs={{0,3},{1,2},{2,1},{3,0},{4,7},{5,6},{6,5},{7,4},{8,11},{9,10},{10,... | collective-permute-start | bytes 147464 | tf_op jit(solution)/shard_map/ppermute | solution.py:34
  10.7 5.6 %collective-permute-start.3 = (f32[2,48,128]{2,1,0:T(8,128)S(1)}, f32[2,48,128]{2,1,0:T(8,128)S(1)}, u32[]{:S(2)}, u32[]{:S(2)}) collective-permute-start(f32[2,48,128]{2,1,0:T(8,128)S(1)} %slice.80), channel_id=1, source_target_pairs={{0,2},{1,3},{2,0},{3,1},{4,6},{5,7},{6,4},{7,5},{8,10},{9,11},{10,... | collective-permute-start | bytes 147464 | tf_op jit(solution)/shard_map/ppermute | solution.py:34
  10.8 8.6 %collective-permute-start.6 = (f32[48,128]{1,0:T(8,128)S(1)}, f32[48,128]{1,0:T(8,128)S(1)}, u32[]{:S(2)}, u32[]{:S(2)}) collective-permute-start(f32[48,128]{1,0:T(8,128)S(1)} %slice_bitcast_fusion.5), channel_id=1, source_target_pairs={{0,24},{1,31},{2,28},{3,27},{4,26},{5,29},{6,30},{7,25},{8,22},{9,... | collective-permute-start | bytes 73736 | tf_op jit(solution)/shard_map/ppermute | solution.py:34
  13.3 6.1 %collective-permute-start.5 = (f32[48,128]{1,0:T(8,128)S(1)}, f32[48,128]{1,0:T(8,128)S(1)}, u32[]{:S(2)}, u32[]{:S(2)}) collective-permute-start(f32[48,128]{1,0:T(8,128)S(1)} %bitcast_select_fusion.1), channel_id=1, source_target_pairs={{0,10},{1,19},{2,16},{3,9},{4,22},{5,15},{6,12},{7,21},{8,26},{9,3... | collective-permute-start | bytes 73736 | tf_op jit(solution)/shard_map/ppermute | solution.py:34
  16.3 3.3 %collective-permute-start.7 = (f32[48,128]{1,0:T(8,128)S(1)}, f32[48,128]{1,0:T(8,128)S(1)}, u32[]{:S(2)}, u32[]{:S(2)}) collective-permute-start(f32[48,128]{1,0:T(8,128)S(1)} %bitcast_select_fusion.1), channel_id=1, source_target_pairs={{0,12},{1,21},{2,22},{3,15},{4,16},{5,9},{6,10},{7,19},{8,28},{9,5... | collective-permute-start | bytes 73736 | tf_op jit(solution)/shard_map/ppermute | solution.py:34
  16.3 3.2 %collective-permute-start.8 = (f32[48,128]{1,0:T(8,128)S(1)}, f32[48,128]{1,0:T(8,128)S(1)}, u32[]{:S(2)}, u32[]{:S(2)}) collective-permute-start(f32[48,128]{1,0:T(8,128)S(1)} %get-tuple-element.84), channel_id=1, source_target_pairs={{0,4},{1,5},{2,6},{3,7},{4,0},{5,1},{6,2},{7,3},{8,12},{9,13},{10,... | collective-permute-start | bytes 73736 | tf_op jit(solution)/shard_map/ppermute | solution.py:34
  19.6 1.9 %collective-permute-start.9 = (f32[2,48,128]{2,1,0:T(8,128)S(1)}, f32[2,48,128]{2,1,0:T(8,128)S(1)}, u32[]{:S(2)}, u32[]{:S(2)}) collective-permute-start(f32[2,48,128]{2,1,0:T(8,128)S(1)} %pad_maximum_fusion.3), channel_id=1, source_target_pairs={{0,4},{1,5},{2,6},{3,7},{4,0},{5,1},{6,2},{7,3},{8,12},{9,13},{10,... | collective-permute-start | bytes 147464 | tf_op jit(solution)/shard_map/ppermute | solution.py:34
  22.3 1.3 %collective-permute-start.10 = (f32[2,48,128]{2,1,0:T(8,128)S(1)}, f32[2,48,128]{2,1,0:T(8,128)S(1)}, u32[]{:S(2)}, u32[]{:S(2)}) collective-permute-start(f32[2,48,128]{2,1,0:T(8,128)S(1)} %get-tuple-element.61), channel_id=1, source_target_pairs={{0,4},{1,5},{2,6},{3,7},{4,0},{5,1},{6,2},{7,3},{8,12},{9,13},{10,... | collective-permute-start | bytes 147464 | tf_op jit(solution)/shard_map/ppermute | solution.py:34
  23.7 5.0 %collective-permute-start.11 = (f32[2,48,128]{2,1,0:T(8,128)S(1)}, f32[2,48,128]{2,1,0:T(8,128)S(1)}, u32[]{:S(2)}, u32[]{:S(2)}) collective-permute-start(f32[2,48,128]{2,1,0:T(8,128)S(1)} %add.65), channel_id=1, source_target_pairs={{0,5},{1,4},{2,7},{3,6},{4,1},{5,0},{6,3},{7,2},{8,13},{9,12},{10,... | collective-permute-start | bytes 147464 | tf_op jit(solution)/shard_map/ppermute | solution.py:34
  25.2 4.1 %collective-permute-start.12 = (f32[2,48,128]{2,1,0:T(8,128)S(1)}, f32[2,48,128]{2,1,0:T(8,128)S(1)}, u32[]{:S(2)}, u32[]{:S(2)}) collective-permute-start(f32[2,48,128]{2,1,0:T(8,128)S(1)} %pad_maximum_fusion.5), channel_id=1, source_target_pairs={{0,1},{1,0},{2,3},{3,2},{4,5},{5,4},{6,7},{7,6},{8,9},{9,8},{10,11... | collective-permute-start | bytes 147464 | tf_op jit(solution)/shard_map/ppermute | solution.py:34
  25.5 7.2 %collective-permute-start.14 = (f32[2,48,128]{2,1,0:T(8,128)S(1)}, f32[2,48,128]{2,1,0:T(8,128)S(1)}, u32[]{:S(2)}, u32[]{:S(2)}) collective-permute-start(f32[2,48,128]{2,1,0:T(8,128)S(1)} %slice.85), channel_id=1, source_target_pairs={{0,3},{1,2},{2,1},{3,0},{4,7},{5,6},{6,5},{7,4},{8,11},{9,10},{10,... | collective-permute-start | bytes 147464 | tf_op jit(solution)/shard_map/ppermute | solution.py:34
  28.2 5.7 %collective-permute-start.13 = (f32[2,48,128]{2,1,0:T(8,128)S(1)}, f32[2,48,128]{2,1,0:T(8,128)S(1)}, u32[]{:S(2)}, u32[]{:S(2)}) collective-permute-start(f32[2,48,128]{2,1,0:T(8,128)S(1)} %slice.85), channel_id=1, source_target_pairs={{0,2},{1,3},{2,0},{3,1},{4,6},{5,7},{6,4},{7,5},{8,10},{9,11},{10,... | collective-permute-start | bytes 147464 | tf_op jit(solution)/shard_map/ppermute | solution.py:34
  29.3 6.2 %collective-permute-start.16 = (f32[48,128]{1,0:T(8,128)S(1)}, f32[48,128]{1,0:T(8,128)S(1)}, u32[]{:S(2)}, u32[]{:S(2)}) collective-permute-start(f32[48,128]{1,0:T(8,128)S(1)} %slice_bitcast_fusion.4), channel_id=1, source_target_pairs={{0,24},{1,31},{2,28},{3,27},{4,26},{5,29},{6,30},{7,25},{8,22},{9,... | collective-permute-start | bytes 73736 | tf_op jit(solution)/shard_map/ppermute | solution.py:34
  30.7 5.6 %collective-permute-start.15 = (f32[48,128]{1,0:T(8,128)S(1)}, f32[48,128]{1,0:T(8,128)S(1)}, u32[]{:S(2)}, u32[]{:S(2)}) collective-permute-start(f32[48,128]{1,0:T(8,128)S(1)} %bitcast_select_fusion), channel_id=1, source_target_pairs={{0,10},{1,19},{2,16},{3,9},{4,22},{5,15},{6,12},{7,21},{8,26},{9,3... | collective-permute-start | bytes 73736 | tf_op jit(solution)/shard_map/ppermute | solution.py:34
  32.7 3.6 %collective-permute-start.17 = (f32[48,128]{1,0:T(8,128)S(1)}, f32[48,128]{1,0:T(8,128)S(1)}, u32[]{:S(2)}, u32[]{:S(2)}) collective-permute-start(f32[48,128]{1,0:T(8,128)S(1)} %bitcast_select_fusion), channel_id=1, source_target_pairs={{0,12},{1,21},{2,22},{3,15},{4,16},{5,9},{6,10},{7,19},{8,28},{9,5... | collective-permute-start | bytes 73736 | tf_op jit(solution)/shard_map/ppermute | solution.py:34
  33.9 2.4 %collective-permute-start.18 = (f32[48,128]{1,0:T(8,128)S(1)}, f32[48,128]{1,0:T(8,128)S(1)}, u32[]{:S(2)}, u32[]{:S(2)}) collective-permute-start(f32[48,128]{1,0:T(8,128)S(1)} %get-tuple-element.81), channel_id=1, source_target_pairs={{0,4},{1,5},{2,6},{3,7},{4,0},{5,1},{6,2},{7,3},{8,12},{9,13},{10,... | collective-permute-start | bytes 73736 | tf_op jit(solution)/shard_map/ppermute | solution.py:34
  36.3 1.3 %collective-permute-start.19 = (f32[2,48,128]{2,1,0:T(8,128)S(1)}, f32[2,48,128]{2,1,0:T(8,128)S(1)}, u32[]{:S(2)}, u32[]{:S(2)}) collective-permute-start(f32[2,48,128]{2,1,0:T(8,128)S(1)} %pad_maximum_fusion.6), channel_id=1, source_target_pairs={{0,4},{1,5},{2,6},{3,7},{4,0},{5,1},{6,2},{7,3},{8,12},{9,13},{10,... | collective-permute-start | bytes 147464 | tf_op jit(solution)/shard_map/ppermute | solution.py:34

commit v7 on v6

--- a/solution.py
+++ b/solution.py
@@ -70,7 +70,7 @@
     own = jnp.where(first, top[0], top[1])
     far_low = swap(low[1:], both(0, 2))
     last_low = swap(low[1:], both(0, 3))
-    corner = swap(top[1], ((6, 0), (7, 2)))
+    corner = swap(top[1], ((7, 2), (6, 0)))
     far = swap(own, ((2, 2), (4, 2)))
     own, last_low = lax.optimization_barrier((own, last_low))
     beside = swap(own, ((3, 0), (5, 0)))

time: 39 us -> 38.8 us (level)
  waiting for transfers between devices: 3.79 us -> 2.69 us
  starting transfers between devices: 23.2 us -> 24.1 us
    ppermute x20, waiting for transfers between devices: 3.79 us -> 2.69 us  [swap(): return lax.ppermute(block, AXES, route)]
    ppermute x20, starting transfers between devices: 23.2 us -> 24.1 us  [swap(): return lax.ppermute(block, AXES, route)]
  transfers between devices with their start and end apart: 20 -> 20, of which waited for: 7 -> 8; matrix products, arithmetic and copies ran while one was open for 0% -> 0% of each run, Pallas kernels for 18% -> 18%
where the time goes in v7:
time: 38.8 us; the launch traced here: 38.6 us
  starting transfers between devices  24.1 us (62%)
  Pallas kernels  10.8 us (28%)
  waiting for transfers between devices  2.69 us (7%)
  between operations  0.88 us (2%)
    ppermute x20, starting transfers between devices, swap(): return lax.ppermute(block, AXES, route)  24.1 us
    pallas_call x6, Pallas kernels, run(): pl.pallas_call(kernel, out_shape=[VMEM(shape, kind) if inside else jax.Sh...  5.19 us
    ppermute x20, waiting for transfers between devices, swap(): return lax.ppermute(block, AXES, route)  2.69 us
    pallas_call x1, Pallas kernels, near_and_tables(): pl.pallas_call(functools.partial(near_and_tables_kernel, late), out_shape...  2.6 us
    pallas_call x1, Pallas kernels, per_device(): pl.pallas_call(first_top_kernel, out_shape=[VMEM(top_out[0], F32), VMEM(s...  1.88 us
    pallas_call x1, Pallas kernels, per_device(): pl.pallas_call(functools.partial(last_kernel, start), out_shape=jax.Shape...  1.14 us
  transfers between devices with their start and end apart: 20, of which 8 were waited for; matrix products, arithmetic and copies ran while one was open for 0% of the time, Pallas kernels for 18%

profile of v7, /device:TPU:0, one launch (start us, length us, event | category | flops | bytes accessed | tf_op | source)
XLA Modules:
  0.0 38.6 jit_solution(3295036485912097666)
XLA Ops:
  0.7 1.9 %shard_map.77 = (f32[2,48,128]{2,1,0:T(8,128)S(1)}, f32[64,1024]{1,0:T(8,128)S(1)}, f32[6,96,1024]{2,1,0:T(8,128)S(1)}) custom-call(f32[64,1024]{1,0:T(8,128)} %field_hbm, f32[6,96,1024]{2,1,0:T(8,128)} %row_hbm.1), custom_call_target="tpu_custom_call" | custom-call | tf_op jit(solution)/shard_map/pallas_call | solution.py:276
  2.6 0.5 %collective-permute-start = (f32[2,48,128]{2,1,0:T(8,128)S(1)}, f32[2,48,128]{2,1,0:T(8,128)S(1)}, u32[]{:S(2)}, u32[]{:S(2)}) collective-permute-start(f32[2,48,128]{2,1,0:T(8,128)S(1)} %get-tuple-element.41), channel_id=1, source_target_pairs={{0,4},{1,5},{2,6},{3,7},{4,0},{5,1},{6,2},{7,3},{8,12},{9,13},{10,... | collective-permute-start | bytes 147464 | tf_op jit(solution)/shard_map/ppermute | solution.py:34
  3.1 0.7 %shard_map.79 = f32[3,48,128]{2,1,0:T(8,128)S(1)} custom-call(f32[64,1024]{1,0:T(8,128)S(1)} %get-tuple-element.38.field, f32[6,96,1024]{2,1,0:T(8,128)S(1)} %get-tuple-element.39.row_basis), custom_call_target="tpu_custom_call" | custom-call | tf_op jit(solution)/shard_map/pallas_call | solution.py:256
  3.8 0.2 collective-permute-done
  4.0 2.7 %collective-permute-start.1 = (f32[2,48,128]{2,1,0:T(8,128)S(1)}, f32[2,48,128]{2,1,0:T(8,128)S(1)}, u32[]{:S(2)}, u32[]{:S(2)}) collective-permute-start(f32[2,48,128]{2,1,0:T(8,128)S(1)} %add.56), channel_id=1, source_target_pairs={{0,5},{1,4},{2,7},{3,6},{4,1},{5,0},{6,3},{7,2},{8,13},{9,12},{10,... | collective-permute-start | bytes 147464 | tf_op jit(solution)/shard_map/ppermute | solution.py:34
  6.7 0.4 collective-permute-start.2
  7.0 3.7 %collective-permute-start.4 = (f32[2,48,128]{2,1,0:T(8,128)S(1)}, f32[2,48,128]{2,1,0:T(8,128)S(1)}, u32[]{:S(2)}, u32[]{:S(2)}) collective-permute-start(f32[2,48,128]{2,1,0:T(8,128)S(1)} %slice.80), channel_id=1, source_target_pairs={{0,3},{1,2},{2,1},{3,0},{4,7},{5,6},{6,5},{7,4},{8,11},{9,10},{10,... | collective-permute-start | bytes 147464 | tf_op jit(solution)/shard_map/ppermute | solution.py:34
  10.8 4.1 %collective-permute-start.6 = (f32[48,128]{1,0:T(8,128)S(1)}, f32[48,128]{1,0:T(8,128)S(1)}, u32[]{:S(2)}, u32[]{:S(2)}) collective-permute-start(f32[48,128]{1,0:T(8,128)S(1)} %slice_bitcast_fusion.5), channel_id=1, source_target_pairs={{0,30},{1,25},{2,26},{3,29},{4,28},{5,27},{6,24},{7,31},{8,16},{9,... | collective-permute-start | bytes 73736 | tf_op jit(solution)/shard_map/ppermute | solution.py:34
  14.8 0.3 collective-permute-start.5
  15.1 1.5 %collective-permute-start.7 = (f32[48,128]{1,0:T(8,128)S(1)}, f32[48,128]{1,0:T(8,128)S(1)}, u32[]{:S(2)}, u32[]{:S(2)}) collective-permute-start(f32[48,128]{1,0:T(8,128)S(1)} %bitcast_select_fusion.1), channel_id=1, source_target_pairs={{0,12},{1,21},{2,22},{3,15},{4,16},{5,9},{6,10},{7,19},{8,28},{9,5... | collective-permute-start | bytes 73736 | tf_op jit(solution)/shard_map/ppermute | solution.py:34
  16.6 1.4 %collective-permute-start.8 = (f32[48,128]{1,0:T(8,128)S(1)}, f32[48,128]{1,0:T(8,128)S(1)}, u32[]{:S(2)}, u32[]{:S(2)}) collective-permute-start(f32[48,128]{1,0:T(8,128)S(1)} %get-tuple-element.84), channel_id=1, source_target_pairs={{0,4},{1,5},{2,6},{3,7},{4,0},{5,1},{6,2},{7,3},{8,12},{9,13},{10,... | collective-permute-start | bytes 73736 | tf_op jit(solution)/shard_map/ppermute | solution.py:34
  18.0 2.6 %shard_map.78 = (f32[64,1024]{1,0:T(8,128)S(1)}, f32[512,1024]{1,0:T(8,128)S(1)}, bf16[192,1024]{1,0:T(8,128)(2,1)S(1)}, bf16[192,1024]{1,0:T(8,128)(2,1)S(1)}, ...) custom-call(f32[64,1024]{1,0:T(8,128)S(1)} %get-tuple-element.38.field, f32[64,1024]{1,0:T(8,128)S(1)} %copy-done.2, ...), custom_call_target="tpu_custom_call" | custom-call | tf_op jit(solution)/shard_map/pallas_call | solution.py:293
  20.8 1.0 %shard_map.80.base = f32[64,1024]{1,0:T(8,128)S(1)} custom-call(f32[64,1024]{1,0:T(8,128)S(1)} %get-tuple-element.40.near, f32[3,48,128]{2,1,0:T(8,128)S(1)} %pad_maximum_fusion.coefs, f32[6,96,1024]{2,1,0:T(8,128)S(1)} %copy-done, f32[64,1024]{1,0:T(8,128)S(1)} %get-tuple-element.38.field, f32[512,1024]{1,0:T(8,128)S(1)} %get-tuple-element.50.leaf_inverse), custom_call_target="tpu_custom_call" | custom-call | tf_op jit(solution)/shard_map/pallas_call | solution.py:256
  21.8 0.1 collective-permute-done.9
  22.0 0.8 %shard_map.81 = (f32[64,1024]{1,0:T(8,128)S(1)}, f32[2,48,128]{2,1,0:T(8,128)S(1)}) custom-call(f32[64,1024]{1,0:T(8,128)S(1)} %shard_map.80.base, f32[2,48,128]{2,1,0:T(8,128)S(1)} %pad_maximum_fusion.4.coefs, bf16[192,1024]{1,0:T(8,128)(2,1)S(1)} %get-tuple-element.54.mixed_high, bf16[192,1024]{1,0:T(8,128)(2,1)S(1)} %get-tuple-element.55.mixed_low, ...), custom_call_target="tpu_custom_call" | custom-call | tf_op jit(solution)/shard_map/pallas_call | solution.py:256
  22.8 0.4 %collective-permute-start.10 = (f32[2,48,128]{2,1,0:T(8,128)S(1)}, f32[2,48,128]{2,1,0:T(8,128)S(1)}, u32[]{:S(2)}, u32[]{:S(2)}) collective-permute-start(f32[2,48,128]{2,1,0:T(8,128)S(1)} %get-tuple-element.61), channel_id=1, source_target_pairs={{0,4},{1,5},{2,6},{3,7},{4,0},{5,1},{6,2},{7,3},{8,12},{9,13},{10,... | collective-permute-start | bytes 147464 | tf_op jit(solution)/shard_map/ppermute | solution.py:34
  23.2 0.7 %shard_map.83 = f32[3,48,128]{2,1,0:T(8,128)S(1)} custom-call(f32[64,1024]{1,0:T(8,128)S(1)} %get-tuple-element.58.field, f32[6,96,1024]{2,1,0:T(8,128)S(1)} %get-tuple-element.39.row_basis), custom_call_target="tpu_custom_call" | custom-call | tf_op jit(solution)/shard_map/pallas_call | solution.py:256
  23.9 0.2 collective-permute-done.10
  24.1 0.2 collective-permute-start.11
  24.3 1.8 %collective-permute-start.12 = (f32[2,48,128]{2,1,0:T(8,128)S(1)}, f32[2,48,128]{2,1,0:T(8,128)S(1)}, u32[]{:S(2)}, u32[]{:S(2)}) collective-permute-start(f32[2,48,128]{2,1,0:T(8,128)S(1)} %pad_maximum_fusion.5), channel_id=1, source_target_pairs={{0,1},{1,0},{2,3},{3,2},{4,5},{5,4},{6,7},{7,6},{8,9},{9,8},{10,11... | collective-permute-start | bytes 147464 | tf_op jit(solution)/shard_map/ppermute | solution.py:34
  26.2 2.1 %collective-permute-start.14 = (f32[2,48,128]{2,1,0:T(8,128)S(1)}, f32[2,48,128]{2,1,0:T(8,128)S(1)}, u32[]{:S(2)}, u32[]{:S(2)}) collective-permute-start(f32[2,48,128]{2,1,0:T(8,128)S(1)} %slice.85), channel_id=1, source_target_pairs={{0,3},{1,2},{2,1},{3,0},{4,7},{5,6},{6,5},{7,4},{8,11},{9,10},{10,... | collective-permute-start | bytes 147464 | tf_op jit(solution)/shard_map/ppermute | solution.py:34
  28.3 1.0 %collective-permute-done.12 = f32[2,48,128]{2,1,0:T(8,128)S(1)} collective-permute-done((f32[2,48,128]{2,1,0:T(8,128)S(1)}, f32[2,48,128]{2,1,0:T(8,128)S(1)}, u32[]{:S(2)}, u32[]{:S(2)}) %collective-permute-start.12) | collective-permute-done | bytes 49184 | tf_op jit(solution)/shard_map/ppermute | solution.py:34
  29.3 1.2 %collective-permute-start.16 = (f32[48,128]{1,0:T(8,128)S(1)}, f32[48,128]{1,0:T(8,128)S(1)}, u32[]{:S(2)}, u32[]{:S(2)}) collective-permute-start(f32[48,128]{1,0:T(8,128)S(1)} %slice_bitcast_fusion.4), channel_id=1, source_target_pairs={{0,30},{1,25},{2,26},{3,29},{4,28},{5,27},{6,24},{7,31},{8,16},{9,... | collective-permute-start | bytes 73736 | tf_op jit(solution)/shard_map/ppermute | solution.py:34
  30.5 1.4 %collective-permute-start.15 = (f32[48,128]{1,0:T(8,128)S(1)}, f32[48,128]{1,0:T(8,128)S(1)}, u32[]{:S(2)}, u32[]{:S(2)}) collective-permute-start(f32[48,128]{1,0:T(8,128)S(1)} %bitcast_select_fusion), channel_id=1, source_target_pairs={{0,10},{1,19},{2,16},{3,9},{4,22},{5,15},{6,12},{7,21},{8,26},{9,3... | collective-permute-start | bytes 73736 | tf_op jit(solution)/shard_map/ppermute | solution.py:34
  31.9 0.2 collective-permute-done.14
  32.1 2.1 %collective-permute-start.17 = (f32[48,128]{1,0:T(8,128)S(1)}, f32[48,128]{1,0:T(8,128)S(1)}, u32[]{:S(2)}, u32[]{:S(2)}) collective-permute-start(f32[48,128]{1,0:T(8,128)S(1)} %bitcast_select_fusion), channel_id=1, source_target_pairs={{0,12},{1,21},{2,22},{3,15},{4,16},{5,9},{6,10},{7,19},{8,28},{9,5... | collective-permute-start | bytes 73736 | tf_op jit(solution)/shard_map/ppermute | solution.py:34
  34.3 1.4 %shard_map.82 = (f32[64,1024]{1,0:T(8,128)S(1)}, f32[64,1024]{1,0:T(8,128)}) custom-call(f32[64,1024]{1,0:T(8,128)S(1)} %get-tuple-element.58.field, f32[64,1024]{1,0:T(8,128)S(1)} %copy-done.2, f32[512,1024]{1,0:T(8,128)S(1)} %copy-done.1, f32[6,96,1024]{2,1,0:T(8,128)S(1)} %copy-done, f32[6,96,1024]{2,1,0:T(8,128)S(1)} %get-tuple-element.39.row_basis), custom_call_target="tpu_custom_call" | custom-call | tf_op jit(solution)/shard_map/pallas_call | solution.py:256
  35.8 0.4 collective-permute-done.15
  36.2 0.2 collective-permute-start.19
  36.4 0.6 %shard_map.84.near = f32[64,1024]{1,0:T(8,128)S(1)} custom-call(f32[64,1024]{1,0:T(8,128)S(1)} %get-tuple-element.60.near, f32[3,48,128]{2,1,0:T(8,128)S(1)} %pad_maximum_fusion.1.coefs, f32[6,96,1024]{2,1,0:T(8,128)S(1)} %copy-done), custom_call_target="tpu_custom_call" | custom-call | tf_op jit(solution)/shard_map/pallas_call | solution.py:256
  37.0 0.5 %collective-permute-done.19 = f32[2,48,128]{2,1,0:T(8,128)S(1)} collective-permute-done((f32[2,48,128]{2,1,0:T(8,128)S(1)}, f32[2,48,128]{2,1,0:T(8,128)S(1)}, u32[]{:S(2)}, u32[]{:S(2)}) %collective-permute-start.19) | collective-permute-done | bytes 49184 | tf_op jit(solution)/shard_map/ppermute | solution.py:34
  37.5 1.1 %shard_map.85 = f32[64,1024]{1,0:T(8,128)} custom-call(f32[64,1024]{1,0:T(8,128)S(1)} %shard_map.84.near, f32[2,48,128]{2,1,0:T(8,128)S(1)} %pad_maximum_fusion.7.coefs, f32[6,96,1024]{2,1,0:T(8,128)S(1)} %copy-done), custom_call_target="tpu_custom_call" | custom-call | tf_op jit(solution)/shard_map/pallas_call | solution.py:317
  (51 shorter events, 0.5 us)
Async XLA Ops:
  0.6 17.4 %copy-start.1 = (f32[512,1024]{1,0:T(8,128)S(1)}, f32[512,1024]{1,0:T(8,128)}, u32[]{:S(2)}) copy-start(f32[512,1024]{1,0:T(8,128)} %leaf_blocks.3) | copy-start | bytes 6291460
  2.5 15.5 %copy-start = (f32[6,96,1024]{2,1,0:T(8,128)S(1)}, f32[6,96,1024]{2,1,0:T(8,128)}, u32[]{:S(2)}) copy-start(f32[6,96,1024]{2,1,0:T(8,128)} %col_basis.9) | copy-start | bytes 7077892
  2.5 15.5 %copy-start.2 = (f32[64,1024]{1,0:T(8,128)S(1)}, f32[64,1024]{1,0:T(8,128)}, u32[]{:S(2)}) copy-start(f32[64,1024]{1,0:T(8,128)} %incident.3) | copy-start | bytes 786436
  2.6 1.4 %collective-permute-start = (f32[2,48,128]{2,1,0:T(8,128)S(1)}, f32[2,48,128]{2,1,0:T(8,128)S(1)}, u32[]{:S(2)}, u32[]{:S(2)}) collective-permute-start(f32[2,48,128]{2,1,0:T(8,128)S(1)} %get-tuple-element.41), channel_id=1, source_target_pairs={{0,4},{1,5},{2,6},{3,7},{4,0},{5,1},{6,2},{7,3},{8,12},{9,13},{10,... | collective-permute-start | bytes 147464 | tf_op jit(solution)/shard_map/ppermute | solution.py:34
  4.0 6.8 %collective-permute-start.1 = (f32[2,48,128]{2,1,0:T(8,128)S(1)}, f32[2,48,128]{2,1,0:T(8,128)S(1)}, u32[]{:S(2)}, u32[]{:S(2)}) collective-permute-start(f32[2,48,128]{2,1,0:T(8,128)S(1)} %add.56), channel_id=1, source_target_pairs={{0,5},{1,4},{2,7},{3,6},{4,1},{5,0},{6,3},{7,2},{8,13},{9,12},{10,... | collective-permute-start | bytes 147464 | tf_op jit(solution)/shard_map/ppermute | solution.py:34
  6.7 4.1 %collective-permute-start.2 = (f32[2,48,128]{2,1,0:T(8,128)S(1)}, f32[2,48,128]{2,1,0:T(8,128)S(1)}, u32[]{:S(2)}, u32[]{:S(2)}) collective-permute-start(f32[2,48,128]{2,1,0:T(8,128)S(1)} %pad_maximum_fusion.2), channel_id=1, source_target_pairs={{0,1},{1,0},{2,3},{3,2},{4,5},{5,4},{6,7},{7,6},{8,9},{9,8},{10,11... | collective-permute-start | bytes 147464 | tf_op jit(solution)/shard_map/ppermute | solution.py:34
  7.0 8.0 %collective-permute-start.4 = (f32[2,48,128]{2,1,0:T(8,128)S(1)}, f32[2,48,128]{2,1,0:T(8,128)S(1)}, u32[]{:S(2)}, u32[]{:S(2)}) collective-permute-start(f32[2,48,128]{2,1,0:T(8,128)S(1)} %slice.80), channel_id=1, source_target_pairs={{0,3},{1,2},{2,1},{3,0},{4,7},{5,6},{6,5},{7,4},{8,11},{9,10},{10,... | collective-permute-start | bytes 147464 | tf_op jit(solution)/shard_map/ppermute | solution.py:34
  10.7 5.8 %collective-permute-start.3 = (f32[2,48,128]{2,1,0:T(8,128)S(1)}, f32[2,48,128]{2,1,0:T(8,128)S(1)}, u32[]{:S(2)}, u32[]{:S(2)}) collective-permute-start(f32[2,48,128]{2,1,0:T(8,128)S(1)} %slice.80), channel_id=1, source_target_pairs={{0,2},{1,3},{2,0},{3,1},{4,6},{5,7},{6,4},{7,5},{8,10},{9,11},{10,... | collective-permute-start | bytes 147464 | tf_op jit(solution)/shard_map/ppermute | solution.py:34
  10.8 9.8 %collective-permute-start.6 = (f32[48,128]{1,0:T(8,128)S(1)}, f32[48,128]{1,0:T(8,128)S(1)}, u32[]{:S(2)}, u32[]{:S(2)}) collective-permute-start(f32[48,128]{1,0:T(8,128)S(1)} %slice_bitcast_fusion.5), channel_id=1, source_target_pairs={{0,30},{1,25},{2,26},{3,29},{4,28},{5,27},{6,24},{7,31},{8,16},{9,... | collective-permute-start | bytes 73736 | tf_op jit(solution)/shard_map/ppermute | solution.py:34
  14.8 5.8 %collective-permute-start.5 = (f32[48,128]{1,0:T(8,128)S(1)}, f32[48,128]{1,0:T(8,128)S(1)}, u32[]{:S(2)}, u32[]{:S(2)}) collective-permute-start(f32[48,128]{1,0:T(8,128)S(1)} %bitcast_select_fusion.1), channel_id=1, source_target_pairs={{0,10},{1,19},{2,16},{3,9},{4,22},{5,15},{6,12},{7,21},{8,26},{9,3... | collective-permute-start | bytes 73736 | tf_op jit(solution)/shard_map/ppermute | solution.py:34
  15.1 5.5 %collective-permute-start.7 = (f32[48,128]{1,0:T(8,128)S(1)}, f32[48,128]{1,0:T(8,128)S(1)}, u32[]{:S(2)}, u32[]{:S(2)}) collective-permute-start(f32[48,128]{1,0:T(8,128)S(1)} %bitcast_select_fusion.1), channel_id=1, source_target_pairs={{0,12},{1,21},{2,22},{3,15},{4,16},{5,9},{6,10},{7,19},{8,28},{9,5... | collective-permute-start | bytes 73736 | tf_op jit(solution)/shard_map/ppermute | solution.py:34
  16.6 4.1 %collective-permute-start.8 = (f32[48,128]{1,0:T(8,128)S(1)}, f32[48,128]{1,0:T(8,128)S(1)}, u32[]{:S(2)}, u32[]{:S(2)}) collective-permute-start(f32[48,128]{1,0:T(8,128)S(1)} %get-tuple-element.84), channel_id=1, source_target_pairs={{0,4},{1,5},{2,6},{3,7},{4,0},{5,1},{6,2},{7,3},{8,12},{9,13},{10,... | collective-permute-start | bytes 73736 | tf_op jit(solution)/shard_map/ppermute | solution.py:34
  20.7 1.3 %collective-permute-start.9 = (f32[2,48,128]{2,1,0:T(8,128)S(1)}, f32[2,48,128]{2,1,0:T(8,128)S(1)}, u32[]{:S(2)}, u32[]{:S(2)}) collective-permute-start(f32[2,48,128]{2,1,0:T(8,128)S(1)} %pad_maximum_fusion.3), channel_id=1, source_target_pairs={{0,4},{1,5},{2,6},{3,7},{4,0},{5,1},{6,2},{7,3},{8,12},{9,13},{10,... | collective-permute-start | bytes 147464 | tf_op jit(solution)/shard_map/ppermute | solution.py:34
  22.8 1.3 %collective-permute-start.10 = (f32[2,48,128]{2,1,0:T(8,128)S(1)}, f32[2,48,128]{2,1,0:T(8,128)S(1)}, u32[]{:S(2)}, u32[]{:S(2)}) collective-permute-start(f32[2,48,128]{2,1,0:T(8,128)S(1)} %get-tuple-element.61), channel_id=1, source_target_pairs={{0,4},{1,5},{2,6},{3,7},{4,0},{5,1},{6,2},{7,3},{8,12},{9,13},{10,... | collective-permute-start | bytes 147464 | tf_op jit(solution)/shard_map/ppermute | solution.py:34
  24.1 4.2 %collective-permute-start.11 = (f32[2,48,128]{2,1,0:T(8,128)S(1)}, f32[2,48,128]{2,1,0:T(8,128)S(1)}, u32[]{:S(2)}, u32[]{:S(2)}) collective-permute-start(f32[2,48,128]{2,1,0:T(8,128)S(1)} %add.65), channel_id=1, source_target_pairs={{0,5},{1,4},{2,7},{3,6},{4,1},{5,0},{6,3},{7,2},{8,13},{9,12},{10,... | collective-permute-start | bytes 147464 | tf_op jit(solution)/shard_map/ppermute | solution.py:34
  24.3 5.0 %collective-permute-start.12 = (f32[2,48,128]{2,1,0:T(8,128)S(1)}, f32[2,48,128]{2,1,0:T(8,128)S(1)}, u32[]{:S(2)}, u32[]{:S(2)}) collective-permute-start(f32[2,48,128]{2,1,0:T(8,128)S(1)} %pad_maximum_fusion.5), channel_id=1, source_target_pairs={{0,1},{1,0},{2,3},{3,2},{4,5},{5,4},{6,7},{7,6},{8,9},{9,8},{10,11... | collective-permute-start | bytes 147464 | tf_op jit(solution)/shard_map/ppermute | solution.py:34
  26.2 5.9 %collective-permute-start.14 = (f32[2,48,128]{2,1,0:T(8,128)S(1)}, f32[2,48,128]{2,1,0:T(8,128)S(1)}, u32[]{:S(2)}, u32[]{:S(2)}) collective-permute-start(f32[2,48,128]{2,1,0:T(8,128)S(1)} %slice.85), channel_id=1, source_target_pairs={{0,3},{1,2},{2,1},{3,0},{4,7},{5,6},{6,5},{7,4},{8,11},{9,10},{10,... | collective-permute-start | bytes 147464 | tf_op jit(solution)/shard_map/ppermute | solution.py:34
  28.3 5.9 %collective-permute-start.13 = (f32[2,48,128]{2,1,0:T(8,128)S(1)}, f32[2,48,128]{2,1,0:T(8,128)S(1)}, u32[]{:S(2)}, u32[]{:S(2)}) collective-permute-start(f32[2,48,128]{2,1,0:T(8,128)S(1)} %slice.85), channel_id=1, source_target_pairs={{0,2},{1,3},{2,0},{3,1},{4,6},{5,7},{6,4},{7,5},{8,10},{9,11},{10,... | collective-permute-start | bytes 147464 | tf_op jit(solution)/shard_map/ppermute | solution.py:34
  29.3 6.5 %collective-permute-start.16 = (f32[48,128]{1,0:T(8,128)S(1)}, f32[48,128]{1,0:T(8,128)S(1)}, u32[]{:S(2)}, u32[]{:S(2)}) collective-permute-start(f32[48,128]{1,0:T(8,128)S(1)} %slice_bitcast_fusion.4), channel_id=1, source_target_pairs={{0,30},{1,25},{2,26},{3,29},{4,28},{5,27},{6,24},{7,31},{8,16},{9,... | collective-permute-start | bytes 73736 | tf_op jit(solution)/shard_map/ppermute | solution.py:34
  30.5 5.6 %collective-permute-start.15 = (f32[48,128]{1,0:T(8,128)S(1)}, f32[48,128]{1,0:T(8,128)S(1)}, u32[]{:S(2)}, u32[]{:S(2)}) collective-permute-start(f32[48,128]{1,0:T(8,128)S(1)} %bitcast_select_fusion), channel_id=1, source_target_pairs={{0,10},{1,19},{2,16},{3,9},{4,22},{5,15},{6,12},{7,21},{8,26},{9,3... | collective-permute-start | bytes 73736 | tf_op jit(solution)/shard_map/ppermute | solution.py:34
  32.1 4.0 %collective-permute-start.17 = (f32[48,128]{1,0:T(8,128)S(1)}, f32[48,128]{1,0:T(8,128)S(1)}, u32[]{:S(2)}, u32[]{:S(2)}) collective-permute-start(f32[48,128]{1,0:T(8,128)S(1)} %bitcast_select_fusion), channel_id=1, source_target_pairs={{0,12},{1,21},{2,22},{3,15},{4,16},{5,9},{6,10},{7,19},{8,28},{9,5... | collective-permute-start | bytes 73736 | tf_op jit(solution)/shard_map/ppermute | solution.py:34
  34.2 1.9 %collective-permute-start.18 = (f32[48,128]{1,0:T(8,128)S(1)}, f32[48,128]{1,0:T(8,128)S(1)}, u32[]{:S(2)}, u32[]{:S(2)}) collective-permute-start(f32[48,128]{1,0:T(8,128)S(1)} %get-tuple-element.81), channel_id=1, source_target_pairs={{0,4},{1,5},{2,6},{3,7},{4,0},{5,1},{6,2},{7,3},{8,12},{9,13},{10,... | collective-permute-start | bytes 73736 | tf_op jit(solution)/shard_map/ppermute | solution.py:34
  36.2 1.3 %collective-permute-start.19 = (f32[2,48,128]{2,1,0:T(8,128)S(1)}, f32[2,48,128]{2,1,0:T(8,128)S(1)}, u32[]{:S(2)}, u32[]{:S(2)}) collective-permute-start(f32[2,48,128]{2,1,0:T(8,128)S(1)} %pad_maximum_fusion.6), channel_id=1, source_target_pairs={{0,4},{1,5},{2,6},{3,7},{4,0},{5,1},{6,2},{7,3},{8,12},{9,13},{10,... | collective-permute-start | bytes 147464 | tf_op jit(solution)/shard_map/ppermute | solution.py:34

commit v8 on v7

--- a/solution.py
+++ b/solution.py
@@ -63,7 +63,7 @@
     core = both(1, 0)
     top = top + swap(top, core)
     next_low = swap(jnp.stack([low[0], low[2]]), both(0, 1))
-    top_got = swap(top, both(1, 1))
+    top_got = swap(top, both(0, 1))
     top = top + top_got
     near, *others = near_of()
     top, next_low = lax.optimization_barrier((top, next_low))

time: 38.8 us -> 38.5 us (level)
  transfers between devices with their start and end apart: 20 -> 20, of which waited for: 8 -> 9; matrix products, arithmetic and copies ran while one was open for 0% -> 0% of each run, Pallas kernels for 18% -> 18%
where the time goes in v8:
time: 38.5 us; the launch traced here: 38.3 us
  starting transfers between devices  23.8 us (62%)
  Pallas kernels  10.8 us (28%)
  waiting for transfers between devices  2.64 us (7%)
  between operations  0.89 us (2%)
    ppermute x20, starting transfers between devices, swap(): return lax.ppermute(block, AXES, route)  23.8 us
    pallas_call x6, Pallas kernels, run(): pl.pallas_call(kernel, out_shape=[VMEM(shape, kind) if inside else jax.Sh...  5.19 us
    ppermute x20, waiting for transfers between devices, swap(): return lax.ppermute(block, AXES, route)  2.64 us
    pallas_call x1, Pallas kernels, near_and_tables(): pl.pallas_call(functools.partial(near_and_tables_kernel, late), out_shape...  2.6 us
    pallas_call x1, Pallas kernels, per_device(): pl.pallas_call(first_top_kernel, out_shape=[VMEM(top_out[0], F32), VMEM(s...  1.88 us
    pallas_call x1, Pallas kernels, per_device(): pl.pallas_call(functools.partial(last_kernel, start), out_shape=jax.Shape...  1.14 us
  transfers between devices with their start and end apart: 20, of which 9 were waited for; matrix products, arithmetic and copies ran while one was open for 0% of the time, Pallas kernels for 18%

profile of v8, /device:TPU:0, one launch (start us, length us, event | category | flops | bytes accessed | tf_op | source)
XLA Modules:
  0.0 38.3 jit_solution(18432587720567551918)
XLA Ops:
  0.7 1.9 %shard_map.77 = (f32[2,48,128]{2,1,0:T(8,128)S(1)}, f32[64,1024]{1,0:T(8,128)S(1)}, f32[6,96,1024]{2,1,0:T(8,128)S(1)}) custom-call(f32[64,1024]{1,0:T(8,128)} %field_hbm, f32[6,96,1024]{2,1,0:T(8,128)} %row_hbm.1), custom_call_target="tpu_custom_call" | custom-call | tf_op jit(solution)/shard_map/pallas_call | solution.py:276
  2.6 0.5 %collective-permute-start = (f32[2,48,128]{2,1,0:T(8,128)S(1)}, f32[2,48,128]{2,1,0:T(8,128)S(1)}, u32[]{:S(2)}, u32[]{:S(2)}) collective-permute-start(f32[2,48,128]{2,1,0:T(8,128)S(1)} %get-tuple-element.41), channel_id=1, source_target_pairs={{0,4},{1,5},{2,6},{3,7},{4,0},{5,1},{6,2},{7,3},{8,12},{9,13},{10,... | collective-permute-start | bytes 147464 | tf_op jit(solution)/shard_map/ppermute | solution.py:34
  3.1 0.7 %shard_map.79 = f32[3,48,128]{2,1,0:T(8,128)S(1)} custom-call(f32[64,1024]{1,0:T(8,128)S(1)} %get-tuple-element.38.field, f32[6,96,1024]{2,1,0:T(8,128)S(1)} %get-tuple-element.39.row_basis), custom_call_target="tpu_custom_call" | custom-call | tf_op jit(solution)/shard_map/pallas_call | solution.py:256
  3.8 0.2 collective-permute-done
  4.0 3.0 %collective-permute-start.1 = (f32[2,48,128]{2,1,0:T(8,128)S(1)}, f32[2,48,128]{2,1,0:T(8,128)S(1)}, u32[]{:S(2)}, u32[]{:S(2)}) collective-permute-start(f32[2,48,128]{2,1,0:T(8,128)S(1)} %add.56), channel_id=1, source_target_pairs={{0,1},{1,0},{2,3},{3,2},{4,5},{5,4},{6,7},{7,6},{8,9},{9,8},{10,11... | collective-permute-start | bytes 147464 | tf_op jit(solution)/shard_map/ppermute | solution.py:34
  7.0 4.0 %collective-permute-start.4 = (f32[2,48,128]{2,1,0:T(8,128)S(1)}, f32[2,48,128]{2,1,0:T(8,128)S(1)}, u32[]{:S(2)}, u32[]{:S(2)}) collective-permute-start(f32[2,48,128]{2,1,0:T(8,128)S(1)} %slice.80), channel_id=1, source_target_pairs={{0,3},{1,2},{2,1},{3,0},{4,7},{5,6},{6,5},{7,4},{8,11},{9,10},{10,... | collective-permute-start | bytes 147464 | tf_op jit(solution)/shard_map/ppermute | solution.py:34
  11.1 3.5 %collective-permute-start.6 = (f32[48,128]{1,0:T(8,128)S(1)}, f32[48,128]{1,0:T(8,128)S(1)}, u32[]{:S(2)}, u32[]{:S(2)}) collective-permute-start(f32[48,128]{1,0:T(8,128)S(1)} %slice_bitcast_fusion.5), channel_id=1, source_target_pairs={{0,30},{1,25},{2,26},{3,29},{4,28},{5,27},{6,24},{7,31},{8,16},{9,... | collective-permute-start | bytes 73736 | tf_op jit(solution)/shard_map/ppermute | solution.py:34
  14.5 0.5 %collective-permute-start.5 = (f32[48,128]{1,0:T(8,128)S(1)}, f32[48,128]{1,0:T(8,128)S(1)}, u32[]{:S(2)}, u32[]{:S(2)}) collective-permute-start(f32[48,128]{1,0:T(8,128)S(1)} %bitcast_select_fusion.1), channel_id=1, source_target_pairs={{0,10},{1,19},{2,16},{3,9},{4,22},{5,15},{6,12},{7,21},{8,26},{9,3... | collective-permute-start | bytes 73736 | tf_op jit(solution)/shard_map/ppermute | solution.py:34
  15.1 1.8 %collective-permute-start.7 = (f32[48,128]{1,0:T(8,128)S(1)}, f32[48,128]{1,0:T(8,128)S(1)}, u32[]{:S(2)}, u32[]{:S(2)}) collective-permute-start(f32[48,128]{1,0:T(8,128)S(1)} %bitcast_select_fusion.1), channel_id=1, source_target_pairs={{0,12},{1,21},{2,22},{3,15},{4,16},{5,9},{6,10},{7,19},{8,28},{9,5... | collective-permute-start | bytes 73736 | tf_op jit(solution)/shard_map/ppermute | solution.py:34
  16.9 1.3 %collective-permute-start.8 = (f32[48,128]{1,0:T(8,128)S(1)}, f32[48,128]{1,0:T(8,128)S(1)}, u32[]{:S(2)}, u32[]{:S(2)}) collective-permute-start(f32[48,128]{1,0:T(8,128)S(1)} %get-tuple-element.84), channel_id=1, source_target_pairs={{0,4},{1,5},{2,6},{3,7},{4,0},{5,1},{6,2},{7,3},{8,12},{9,13},{10,... | collective-permute-start | bytes 73736 | tf_op jit(solution)/shard_map/ppermute | solution.py:34
  18.2 2.6 %shard_map.78 = (f32[64,1024]{1,0:T(8,128)S(1)}, f32[512,1024]{1,0:T(8,128)S(1)}, bf16[192,1024]{1,0:T(8,128)(2,1)S(1)}, bf16[192,1024]{1,0:T(8,128)(2,1)S(1)}, ...) custom-call(f32[64,1024]{1,0:T(8,128)S(1)} %get-tuple-element.38.field, f32[64,1024]{1,0:T(8,128)S(1)} %copy-done.2, ...), custom_call_target="tpu_custom_call" | custom-call | tf_op jit(solution)/shard_map/pallas_call | solution.py:293
  20.9 0.1 collective-permute-start.9
  21.0 1.0 %shard_map.80.base = f32[64,1024]{1,0:T(8,128)S(1)} custom-call(f32[64,1024]{1,0:T(8,128)S(1)} %get-tuple-element.40.near, f32[3,48,128]{2,1,0:T(8,128)S(1)} %pad_maximum_fusion.coefs, f32[6,96,1024]{2,1,0:T(8,128)S(1)} %copy-done, f32[64,1024]{1,0:T(8,128)S(1)} %get-tuple-element.38.field, f32[512,1024]{1,0:T(8,128)S(1)} %get-tuple-element.50.leaf_inverse), custom_call_target="tpu_custom_call" | custom-call | tf_op jit(solution)/shard_map/pallas_call | solution.py:256
  22.0 0.1 collective-permute-done.9
  22.2 0.8 %shard_map.81 = (f32[64,1024]{1,0:T(8,128)S(1)}, f32[2,48,128]{2,1,0:T(8,128)S(1)}) custom-call(f32[64,1024]{1,0:T(8,128)S(1)} %shard_map.80.base, f32[2,48,128]{2,1,0:T(8,128)S(1)} %pad_maximum_fusion.4.coefs, bf16[192,1024]{1,0:T(8,128)(2,1)S(1)} %get-tuple-element.54.mixed_high, bf16[192,1024]{1,0:T(8,128)(2,1)S(1)} %get-tuple-element.55.mixed_low, ...), custom_call_target="tpu_custom_call" | custom-call | tf_op jit(solution)/shard_map/pallas_call | solution.py:256
  23.0 0.4 %collective-permute-start.10 = (f32[2,48,128]{2,1,0:T(8,128)S(1)}, f32[2,48,128]{2,1,0:T(8,128)S(1)}, u32[]{:S(2)}, u32[]{:S(2)}) collective-permute-start(f32[2,48,128]{2,1,0:T(8,128)S(1)} %get-tuple-element.61), channel_id=1, source_target_pairs={{0,4},{1,5},{2,6},{3,7},{4,0},{5,1},{6,2},{7,3},{8,12},{9,13},{10,... | collective-permute-start | bytes 147464 | tf_op jit(solution)/shard_map/ppermute | solution.py:34
  23.4 0.7 %shard_map.83 = f32[3,48,128]{2,1,0:T(8,128)S(1)} custom-call(f32[64,1024]{1,0:T(8,128)S(1)} %get-tuple-element.58.field, f32[6,96,1024]{2,1,0:T(8,128)S(1)} %get-tuple-element.39.row_basis), custom_call_target="tpu_custom_call" | custom-call | tf_op jit(solution)/shard_map/pallas_call | solution.py:256
  24.1 0.2 collective-permute-done.10
  24.4 2.0 %collective-permute-start.12 = (f32[2,48,128]{2,1,0:T(8,128)S(1)}, f32[2,48,128]{2,1,0:T(8,128)S(1)}, u32[]{:S(2)}, u32[]{:S(2)}) collective-permute-start(f32[2,48,128]{2,1,0:T(8,128)S(1)} %pad_maximum_fusion.5), channel_id=1, source_target_pairs={{0,1},{1,0},{2,3},{3,2},{4,5},{5,4},{6,7},{7,6},{8,9},{9,8},{10,11... | collective-permute-start | bytes 147464 | tf_op jit(solution)/shard_map/ppermute | solution.py:34
  26.4 1.8 %collective-permute-start.14 = (f32[2,48,128]{2,1,0:T(8,128)S(1)}, f32[2,48,128]{2,1,0:T(8,128)S(1)}, u32[]{:S(2)}, u32[]{:S(2)}) collective-permute-start(f32[2,48,128]{2,1,0:T(8,128)S(1)} %slice.85), channel_id=1, source_target_pairs={{0,3},{1,2},{2,1},{3,0},{4,7},{5,6},{6,5},{7,4},{8,11},{9,10},{10,... | collective-permute-start | bytes 147464 | tf_op jit(solution)/shard_map/ppermute | solution.py:34
  28.2 0.6 %collective-permute-done.11 = f32[2,48,128]{2,1,0:T(8,128)S(1)} collective-permute-done((f32[2,48,128]{2,1,0:T(8,128)S(1)}, f32[2,48,128]{2,1,0:T(8,128)S(1)}, u32[]{:S(2)}, u32[]{:S(2)}) %collective-permute-start.11) | collective-permute-done | bytes 49184 | tf_op jit(solution)/shard_map/ppermute | solution.py:34
  28.9 0.5 %collective-permute-done.12 = f32[2,48,128]{2,1,0:T(8,128)S(1)} collective-permute-done((f32[2,48,128]{2,1,0:T(8,128)S(1)}, f32[2,48,128]{2,1,0:T(8,128)S(1)}, u32[]{:S(2)}, u32[]{:S(2)}) %collective-permute-start.12) | collective-permute-done | bytes 49184 | tf_op jit(solution)/shard_map/ppermute | solution.py:34
  29.4 0.7 %collective-permute-start.16 = (f32[48,128]{1,0:T(8,128)S(1)}, f32[48,128]{1,0:T(8,128)S(1)}, u32[]{:S(2)}, u32[]{:S(2)}) collective-permute-start(f32[48,128]{1,0:T(8,128)S(1)} %slice_bitcast_fusion.4), channel_id=1, source_target_pairs={{0,30},{1,25},{2,26},{3,29},{4,28},{5,27},{6,24},{7,31},{8,16},{9,... | collective-permute-start | bytes 73736 | tf_op jit(solution)/shard_map/ppermute | solution.py:34
  30.1 2.2 %collective-permute-start.15 = (f32[48,128]{1,0:T(8,128)S(1)}, f32[48,128]{1,0:T(8,128)S(1)}, u32[]{:S(2)}, u32[]{:S(2)}) collective-permute-start(f32[48,128]{1,0:T(8,128)S(1)} %bitcast_select_fusion), channel_id=1, source_target_pairs={{0,10},{1,19},{2,16},{3,9},{4,22},{5,15},{6,12},{7,21},{8,26},{9,3... | collective-permute-start | bytes 73736 | tf_op jit(solution)/shard_map/ppermute | solution.py:34
  32.3 1.5 %collective-permute-start.17 = (f32[48,128]{1,0:T(8,128)S(1)}, f32[48,128]{1,0:T(8,128)S(1)}, u32[]{:S(2)}, u32[]{:S(2)}) collective-permute-start(f32[48,128]{1,0:T(8,128)S(1)} %bitcast_select_fusion), channel_id=1, source_target_pairs={{0,12},{1,21},{2,22},{3,15},{4,16},{5,9},{6,10},{7,19},{8,28},{9,5... | collective-permute-start | bytes 73736 | tf_op jit(solution)/shard_map/ppermute | solution.py:34
  33.8 0.3 collective-permute-done.13
  34.2 1.4 %shard_map.82 = (f32[64,1024]{1,0:T(8,128)S(1)}, f32[64,1024]{1,0:T(8,128)}) custom-call(f32[64,1024]{1,0:T(8,128)S(1)} %get-tuple-element.58.field, f32[64,1024]{1,0:T(8,128)S(1)} %copy-done.2, f32[512,1024]{1,0:T(8,128)S(1)} %copy-done.1, f32[6,96,1024]{2,1,0:T(8,128)S(1)} %copy-done, f32[6,96,1024]{2,1,0:T(8,128)S(1)} %get-tuple-element.39.row_basis), custom_call_target="tpu_custom_call" | custom-call | tf_op jit(solution)/shard_map/pallas_call | solution.py:256
  35.6 0.2 collective-permute-done.16
  35.8 0.3 collective-permute-start.19
  36.2 0.6 %shard_map.84.near = f32[64,1024]{1,0:T(8,128)S(1)} custom-call(f32[64,1024]{1,0:T(8,128)S(1)} %get-tuple-element.60.near, f32[3,48,128]{2,1,0:T(8,128)S(1)} %pad_maximum_fusion.1.coefs, f32[6,96,1024]{2,1,0:T(8,128)S(1)} %copy-done), custom_call_target="tpu_custom_call" | custom-call | tf_op jit(solution)/shard_map/pallas_call | solution.py:256
  36.8 0.4 collective-permute-done.19
  37.2 1.1 %shard_map.85 = f32[64,1024]{1,0:T(8,128)} custom-call(f32[64,1024]{1,0:T(8,128)S(1)} %shard_map.84.near, f32[2,48,128]{2,1,0:T(8,128)S(1)} %pad_maximum_fusion.7.coefs, f32[6,96,1024]{2,1,0:T(8,128)S(1)} %copy-done), custom_call_target="tpu_custom_call" | custom-call | tf_op jit(solution)/shard_map/pallas_call | solution.py:317
  (51 shorter events, 0.5 us)
Async XLA Ops:
  0.6 17.5 %copy-start.1 = (f32[512,1024]{1,0:T(8,128)S(1)}, f32[512,1024]{1,0:T(8,128)}, u32[]{:S(2)}) copy-start(f32[512,1024]{1,0:T(8,128)} %leaf_blocks.3) | copy-start | bytes 6291460
  2.5 15.6 %copy-start = (f32[6,96,1024]{2,1,0:T(8,128)S(1)}, f32[6,96,1024]{2,1,0:T(8,128)}, u32[]{:S(2)}) copy-start(f32[6,96,1024]{2,1,0:T(8,128)} %col_basis.9) | copy-start | bytes 7077892
  2.5 15.6 %copy-start.2 = (f32[64,1024]{1,0:T(8,128)S(1)}, f32[64,1024]{1,0:T(8,128)}, u32[]{:S(2)}) copy-start(f32[64,1024]{1,0:T(8,128)} %incident.3) | copy-start | bytes 786436
  2.6 1.4 %collective-permute-start = (f32[2,48,128]{2,1,0:T(8,128)S(1)}, f32[2,48,128]{2,1,0:T(8,128)S(1)}, u32[]{:S(2)}, u32[]{:S(2)}) collective-permute-start(f32[2,48,128]{2,1,0:T(8,128)S(1)} %get-tuple-element.41), channel_id=1, source_target_pairs={{0,4},{1,5},{2,6},{3,7},{4,0},{5,1},{6,2},{7,3},{8,12},{9,13},{10,... | collective-permute-start | bytes 147464 | tf_op jit(solution)/shard_map/ppermute | solution.py:34
  4.0 7.0 %collective-permute-start.1 = (f32[2,48,128]{2,1,0:T(8,128)S(1)}, f32[2,48,128]{2,1,0:T(8,128)S(1)}, u32[]{:S(2)}, u32[]{:S(2)}) collective-permute-start(f32[2,48,128]{2,1,0:T(8,128)S(1)} %add.56), channel_id=1, source_target_pairs={{0,1},{1,0},{2,3},{3,2},{4,5},{5,4},{6,7},{7,6},{8,9},{9,8},{10,11... | collective-permute-start | bytes 147464 | tf_op jit(solution)/shard_map/ppermute | solution.py:34
  7.0 4.1 %collective-permute-start.2 = (f32[2,48,128]{2,1,0:T(8,128)S(1)}, f32[2,48,128]{2,1,0:T(8,128)S(1)}, u32[]{:S(2)}, u32[]{:S(2)}) collective-permute-start(f32[2,48,128]{2,1,0:T(8,128)S(1)} %pad_maximum_fusion.2), channel_id=1, source_target_pairs={{0,1},{1,0},{2,3},{3,2},{4,5},{5,4},{6,7},{7,6},{8,9},{9,8},{10,11... | collective-permute-start | bytes 147464 | tf_op jit(solution)/shard_map/ppermute | solution.py:34
  7.0 8.0 %collective-permute-start.4 = (f32[2,48,128]{2,1,0:T(8,128)S(1)}, f32[2,48,128]{2,1,0:T(8,128)S(1)}, u32[]{:S(2)}, u32[]{:S(2)}) collective-permute-start(f32[2,48,128]{2,1,0:T(8,128)S(1)} %slice.80), channel_id=1, source_target_pairs={{0,3},{1,2},{2,1},{3,0},{4,7},{5,6},{6,5},{7,4},{8,11},{9,10},{10,... | collective-permute-start | bytes 147464 | tf_op jit(solution)/shard_map/ppermute | solution.py:34
  11.0 5.8 %collective-permute-start.3 = (f32[2,48,128]{2,1,0:T(8,128)S(1)}, f32[2,48,128]{2,1,0:T(8,128)S(1)}, u32[]{:S(2)}, u32[]{:S(2)}) collective-permute-start(f32[2,48,128]{2,1,0:T(8,128)S(1)} %slice.80), channel_id=1, source_target_pairs={{0,2},{1,3},{2,0},{3,1},{4,6},{5,7},{6,4},{7,5},{8,10},{9,11},{10,... | collective-permute-start | bytes 147464 | tf_op jit(solution)/shard_map/ppermute | solution.py:34
  11.1 9.7 %collective-permute-start.6 = (f32[48,128]{1,0:T(8,128)S(1)}, f32[48,128]{1,0:T(8,128)S(1)}, u32[]{:S(2)}, u32[]{:S(2)}) collective-permute-start(f32[48,128]{1,0:T(8,128)S(1)} %slice_bitcast_fusion.5), channel_id=1, source_target_pairs={{0,30},{1,25},{2,26},{3,29},{4,28},{5,27},{6,24},{7,31},{8,16},{9,... | collective-permute-start | bytes 73736 | tf_op jit(solution)/shard_map/ppermute | solution.py:34
  14.5 6.3 %collective-permute-start.5 = (f32[48,128]{1,0:T(8,128)S(1)}, f32[48,128]{1,0:T(8,128)S(1)}, u32[]{:S(2)}, u32[]{:S(2)}) collective-permute-start(f32[48,128]{1,0:T(8,128)S(1)} %bitcast_select_fusion.1), channel_id=1, source_target_pairs={{0,10},{1,19},{2,16},{3,9},{4,22},{5,15},{6,12},{7,21},{8,26},{9,3... | collective-permute-start | bytes 73736 | tf_op jit(solution)/shard_map/ppermute | solution.py:34
  15.1 5.8 %collective-permute-start.7 = (f32[48,128]{1,0:T(8,128)S(1)}, f32[48,128]{1,0:T(8,128)S(1)}, u32[]{:S(2)}, u32[]{:S(2)}) collective-permute-start(f32[48,128]{1,0:T(8,128)S(1)} %bitcast_select_fusion.1), channel_id=1, source_target_pairs={{0,12},{1,21},{2,22},{3,15},{4,16},{5,9},{6,10},{7,19},{8,28},{9,5... | collective-permute-start | bytes 73736 | tf_op jit(solution)/shard_map/ppermute | solution.py:34
  16.9 4.0 %collective-permute-start.8 = (f32[48,128]{1,0:T(8,128)S(1)}, f32[48,128]{1,0:T(8,128)S(1)}, u32[]{:S(2)}, u32[]{:S(2)}) collective-permute-start(f32[48,128]{1,0:T(8,128)S(1)} %get-tuple-element.84), channel_id=1, source_target_pairs={{0,4},{1,5},{2,6},{3,7},{4,0},{5,1},{6,2},{7,3},{8,12},{9,13},{10,... | collective-permute-start | bytes 73736 | tf_op jit(solution)/shard_map/ppermute | solution.py:34
  20.9 1.3 %collective-permute-start.9 = (f32[2,48,128]{2,1,0:T(8,128)S(1)}, f32[2,48,128]{2,1,0:T(8,128)S(1)}, u32[]{:S(2)}, u32[]{:S(2)}) collective-permute-start(f32[2,48,128]{2,1,0:T(8,128)S(1)} %pad_maximum_fusion.3), channel_id=1, source_target_pairs={{0,4},{1,5},{2,6},{3,7},{4,0},{5,1},{6,2},{7,3},{8,12},{9,13},{10,... | collective-permute-start | bytes 147464 | tf_op jit(solution)/shard_map/ppermute | solution.py:34
  23.0 1.3 %collective-permute-start.10 = (f32[2,48,128]{2,1,0:T(8,128)S(1)}, f32[2,48,128]{2,1,0:T(8,128)S(1)}, u32[]{:S(2)}, u32[]{:S(2)}) collective-permute-start(f32[2,48,128]{2,1,0:T(8,128)S(1)} %get-tuple-element.61), channel_id=1, source_target_pairs={{0,4},{1,5},{2,6},{3,7},{4,0},{5,1},{6,2},{7,3},{8,12},{9,13},{10,... | collective-permute-start | bytes 147464 | tf_op jit(solution)/shard_map/ppermute | solution.py:34
  24.3 4.6 %collective-permute-start.11 = (f32[2,48,128]{2,1,0:T(8,128)S(1)}, f32[2,48,128]{2,1,0:T(8,128)S(1)}, u32[]{:S(2)}, u32[]{:S(2)}) collective-permute-start(f32[2,48,128]{2,1,0:T(8,128)S(1)} %add.65), channel_id=1, source_target_pairs={{0,1},{1,0},{2,3},{3,2},{4,5},{5,4},{6,7},{7,6},{8,9},{9,8},{10,11... | collective-permute-start | bytes 147464 | tf_op jit(solution)/shard_map/ppermute | solution.py:34
  24.4 5.0 %collective-permute-start.12 = (f32[2,48,128]{2,1,0:T(8,128)S(1)}, f32[2,48,128]{2,1,0:T(8,128)S(1)}, u32[]{:S(2)}, u32[]{:S(2)}) collective-permute-start(f32[2,48,128]{2,1,0:T(8,128)S(1)} %pad_maximum_fusion.5), channel_id=1, source_target_pairs={{0,1},{1,0},{2,3},{3,2},{4,5},{5,4},{6,7},{7,6},{8,9},{9,8},{10,11... | collective-permute-start | bytes 147464 | tf_op jit(solution)/shard_map/ppermute | solution.py:34
  26.4 5.9 %collective-permute-start.14 = (f32[2,48,128]{2,1,0:T(8,128)S(1)}, f32[2,48,128]{2,1,0:T(8,128)S(1)}, u32[]{:S(2)}, u32[]{:S(2)}) collective-permute-start(f32[2,48,128]{2,1,0:T(8,128)S(1)} %slice.85), channel_id=1, source_target_pairs={{0,3},{1,2},{2,1},{3,0},{4,7},{5,6},{6,5},{7,4},{8,11},{9,10},{10,... | collective-permute-start | bytes 147464 | tf_op jit(solution)/shard_map/ppermute | solution.py:34
  28.2 5.8 %collective-permute-start.13 = (f32[2,48,128]{2,1,0:T(8,128)S(1)}, f32[2,48,128]{2,1,0:T(8,128)S(1)}, u32[]{:S(2)}, u32[]{:S(2)}) collective-permute-start(f32[2,48,128]{2,1,0:T(8,128)S(1)} %slice.85), channel_id=1, source_target_pairs={{0,2},{1,3},{2,0},{3,1},{4,6},{5,7},{6,4},{7,5},{8,10},{9,11},{10,... | collective-permute-start | bytes 147464 | tf_op jit(solution)/shard_map/ppermute | solution.py:34
  29.4 6.3 %collective-permute-start.16 = (f32[48,128]{1,0:T(8,128)S(1)}, f32[48,128]{1,0:T(8,128)S(1)}, u32[]{:S(2)}, u32[]{:S(2)}) collective-permute-start(f32[48,128]{1,0:T(8,128)S(1)} %slice_bitcast_fusion.4), channel_id=1, source_target_pairs={{0,30},{1,25},{2,26},{3,29},{4,28},{5,27},{6,24},{7,31},{8,16},{9,... | collective-permute-start | bytes 73736 | tf_op jit(solution)/shard_map/ppermute | solution.py:34
  30.1 5.7 %collective-permute-start.15 = (f32[48,128]{1,0:T(8,128)S(1)}, f32[48,128]{1,0:T(8,128)S(1)}, u32[]{:S(2)}, u32[]{:S(2)}) collective-permute-start(f32[48,128]{1,0:T(8,128)S(1)} %bitcast_select_fusion), channel_id=1, source_target_pairs={{0,10},{1,19},{2,16},{3,9},{4,22},{5,15},{6,12},{7,21},{8,26},{9,3... | collective-permute-start | bytes 73736 | tf_op jit(solution)/shard_map/ppermute | solution.py:34
  32.3 3.5 %collective-permute-start.17 = (f32[48,128]{1,0:T(8,128)S(1)}, f32[48,128]{1,0:T(8,128)S(1)}, u32[]{:S(2)}, u32[]{:S(2)}) collective-permute-start(f32[48,128]{1,0:T(8,128)S(1)} %bitcast_select_fusion), channel_id=1, source_target_pairs={{0,12},{1,21},{2,22},{3,15},{4,16},{5,9},{6,10},{7,19},{8,28},{9,5... | collective-permute-start | bytes 73736 | tf_op jit(solution)/shard_map/ppermute | solution.py:34
  34.1 1.7 %collective-permute-start.18 = (f32[48,128]{1,0:T(8,128)S(1)}, f32[48,128]{1,0:T(8,128)S(1)}, u32[]{:S(2)}, u32[]{:S(2)}) collective-permute-start(f32[48,128]{1,0:T(8,128)S(1)} %get-tuple-element.81), channel_id=1, source_target_pairs={{0,4},{1,5},{2,6},{3,7},{4,0},{5,1},{6,2},{7,3},{8,12},{9,13},{10,... | collective-permute-start | bytes 73736 | tf_op jit(solution)/shard_map/ppermute | solution.py:34
  35.8 1.3 %collective-permute-start.19 = (f32[2,48,128]{2,1,0:T(8,128)S(1)}, f32[2,48,128]{2,1,0:T(8,128)S(1)}, u32[]{:S(2)}, u32[]{:S(2)}) collective-permute-start(f32[2,48,128]{2,1,0:T(8,128)S(1)} %pad_maximum_fusion.6), channel_id=1, source_target_pairs={{0,4},{1,5},{2,6},{3,7},{4,0},{5,1},{6,2},{7,3},{8,12},{9,13},{10,... | collective-permute-start | bytes 147464 | tf_op jit(solution)/shard_map/ppermute | solution.py:34
